TPU v7x, 32 devices: a whole 2x2x4 slice. The times are simulated.
32 devices in a mesh: dp: 16 (over z, x, core), tensor: 2 (over y).
Axes of the slice: x: 2, y: 2, z: 4, core: 2. Of those that a mesh axis runs over, the one named last changes fastest.
Arguments:
- patches: bfloat16 [5440, 768], P(('dp', 'tensor')), may hold values from -6 to 6
- out_grad: bfloat16 [5440, 768], P(('dp', 'tensor')), may hold values from -6 to 6
- score_grad: bfloat16 [320, 65536], P(None, ('dp', 'tensor')), may hold values from -6 to 6
- crop_size: int32 [320], P('dp'), may hold values from 9 to 49, as said below
- frozen: int32 [65536], P(('dp', 'tensor')), may hold values 0 or 1
- attn_gain: float32 [768], replicated, may hold values from 0.5 to 1.5
- attn_shift: float32 [768], replicated, may hold values from -3 to 3
- qkv_weight: bfloat16 [768, 24, 96], P(None, 'tensor'), may hold values from -0.21875 to 0.21875
- qkv_bias: float32 [24, 64], P('tensor'), may hold values from -3 to 3
- rel_table: float32 [24, 169], P('tensor'), may hold values from -4 to 4
- proj_weight: bfloat16 [24, 32, 768], P('tensor'), may hold values from -0.875 to 0.875
- proj_bias: float32 [768], replicated, may hold values from -3 to 3
- mlp_gain: float32 [768], replicated, may hold values from 0.5 to 1.5
- mlp_shift: float32 [768], replicated, may hold values from -3 to 3
- hidden_weight: bfloat16 [768, 3072], P(None, 'tensor'), may hold values from -0.21875 to 0.21875
- hidden_bias: float32 [3072], P('tensor'), may hold values from -3 to 3
- output_weight: bfloat16 [3072, 768], P('tensor'), may hold values from -0.21875 to 0.21875
- output_bias: float32 [768], replicated, may hold values from -3 to 3
- prototypes: bfloat16 [65536, 768], P(('dp', 'tensor')), may hold values from -6 to 6
Outputs:
- block_out: bfloat16 [5440, 768], P(('dp', 'tensor'))
- patch_grad: float32 [5440, 768], P(('dp', 'tensor'))
- attn_gain_grad: float32 [768], replicated
- attn_shift_grad: float32 [768], replicated
- qkv_weight_grad: float32 [768, 24, 96], P(None, 'tensor')
- qkv_bias_grad: float32 [24, 64], P('tensor')
- rel_table_grad: float32 [24, 169], P('tensor')
- proj_weight_grad: float32 [24, 32, 768], P('tensor')
- proj_bias_grad: float32 [768], replicated
- mlp_gain_grad: float32 [768], replicated
- mlp_shift_grad: float32 [768], replicated
- hidden_weight_grad: float32 [768, 3072], P(None, 'tensor')
- hidden_bias_grad: float32 [3072], P('tensor')
- output_weight_grad: float32 [3072, 768], P('tensor')
- output_bias_grad: float32 [768], replicated
- prototype_grad: float32 [65536, 768], P(('dp', 'tensor'))
Inputs may be any that keep to these rules, and one draw needn't show every extreme that they name: `crop_size`: each aligned block of 10 entries, the crops of one device, holds exactly 2 entries 49 and the others 9, in an order drawn from the seed, so that its crops fill exactly the 170 rows of that device.
All inputs are finite; a program needn't handle non-finite values. No bound on the sum of `frozen` on one device may be relied on, other than what follows from the above.
Results may differ from a plain program's by a relative error of at most 0.018.
Values may be sent and summed in bfloat16 or wider, within the bound.
No kernel may reach another device: no remote copies, remote signals or barrier semaphores. Data moves between devices by JAX's collectives and lax.ppermute only.
A program may use at most 448 MiB of HBM per device.

v0:
```python
from functools import partial

import jax
import jax.numpy as jnp
import numpy as np
from jax import lax
from jax.sharding import PartitionSpec as P

PATCHES_IMG = 170
BLOCK_IMG = 4


HIGH = lax.Precision.HIGHEST
EPS = 1e-05


def layer_norm(values, norm_gain, norm_shift):
    center = values - jnp.mean(values, axis=-1, keepdims=True)
    spread = jnp.mean(center * center, axis=-1, keepdims=True)
    return center * lax.rsqrt(spread + EPS) * norm_gain + norm_shift


def offset_table():
    places = np.arange(49)
    across = places // 7
    inside = places % 7
    relative = (across[:, None] - across[None, :] + 6) * 13 + (
        inside[:, None] - inside[None, :] + 6
    )
    return (relative.reshape(-1)[:, None] == np.arange(169)[None, :]).astype(np.float32)


def crop_layout(crop_sizes, row_count):
    crop_ends = jnp.cumsum(crop_sizes)
    starts = crop_ends - crop_sizes
    position = jnp.arange(row_count, dtype=jnp.int32)
    reached = starts[None, :] <= position[:, None]
    segment = jnp.sum(reached.astype(jnp.int32), axis=1) - 1
    crop_first = jnp.max(jnp.where(reached, starts[None, :], 0), axis=1)
    finish = jnp.min(
        jnp.where(crop_ends[None, :] > position[:, None], crop_ends[None, :], row_count), axis=1
    )
    crop_side = jnp.where(finish - crop_first == 49, 7, 3)
    offset = position - crop_first
    return (segment, offset // crop_side * 7 + offset % crop_side)


def block_scores(
    queries, keys_block, bias_table, query_seg, key_seg, query_place, key_place, score_scale
):
    scores = (
        jnp.einsum("qhd,khd->hqk", queries, keys_block, preferred_element_type=jnp.float32)
        * score_scale
    )
    query_hot = (query_place[:, None] == jnp.arange(49)[None, :]).astype(jnp.bfloat16)
    key_hot = (key_place[:, None] == jnp.arange(49)[None, :]).astype(jnp.bfloat16)
    rel_bias = bias_table[:, query_place[:, None], key_place[None, :]]
    same_crop = query_seg[:, None] == key_seg[None, :]
    return (jnp.where(same_crop[None], scores + rel_bias, -jnp.inf), query_hot, key_hot)


def per_device(
    patches,
    out_grad,
    score_grad,
    crop_size,
    frozen,
    attn_gain,
    attn_shift,
    qkv_weight,
    qkv_bias,
    rel_table,
    proj_weight,
    proj_bias,
    mlp_gain,
    mlp_shift,
    hidden_weight,
    hidden_bias,
    output_weight,
    output_bias,
    prototypes,
):
    row_count = patches.shape[0]
    feature_width = patches.shape[1]
    tensor_parts = lax.axis_size("tensor")
    tensor_rank = lax.axis_index("tensor")
    group_rows = row_count * tensor_parts
    head_count = qkv_weight.shape[1]
    head_size = qkv_weight.shape[2] // 3
    crops_dev = crop_size.shape[0] // tensor_parts
    score_scale = head_size ** (-0.5)
    halo_rows = 48
    segment, crop_place = crop_layout(crop_size, group_rows)
    own_sizes = lax.dynamic_slice_in_dim(crop_size, tensor_rank * crops_dev, crops_dev, 0)
    own_segment, own_place = crop_layout(own_sizes, row_count)
    pool_matrix = (own_segment[None, :] == jnp.arange(crops_dev)[:, None]).astype(jnp.float32)
    pool_matrix = pool_matrix / own_sizes[:, None].astype(jnp.float32)
    patch_full = patches.astype(jnp.float32)
    normed_one, norm_pull_one = jax.vjp(layer_norm, patch_full, attn_gain, attn_shift)
    group_normed = lax.all_gather(normed_one.astype(jnp.bfloat16), "tensor", axis=0, tiled=True)
    qkv_flat = qkv_weight.reshape(feature_width, head_count * 3 * head_size)
    mixed = jnp.dot(group_normed, qkv_flat, preferred_element_type=jnp.float32).reshape(
        group_rows, head_count, 3 * head_size
    )
    middle_zero = jnp.zeros((head_count, head_size), jnp.float32)
    full_bias = jnp.concatenate(
        [qkv_bias[:, :head_size], middle_zero, qkv_bias[:, head_size:]], axis=1
    )
    mixed_low = (mixed + full_bias).astype(jnp.bfloat16)
    table_hot = jnp.asarray(offset_table())
    bias_table = jnp.dot(rel_table, table_hot.T, precision=HIGH).reshape(head_count, 49, 49)
    padded = jnp.pad(mixed_low, ((halo_rows, halo_rows), (0, 0), (0, 0)))
    segment_pad = jnp.pad(segment, (halo_rows, halo_rows), constant_values=-1)
    place_pad = jnp.pad(crop_place, (halo_rows, halo_rows))
    block_rows = PATCHES_IMG * min(BLOCK_IMG, group_rows // PATCHES_IMG)
    blocks = group_rows // block_rows
    key_rows = block_rows + 2 * halo_rows

    def block_inputs(block_index):
        first_row = block_index * block_rows
        queries = lax.dynamic_slice_in_dim(mixed_low, first_row, block_rows, 0)[:, :, :head_size]
        window = lax.dynamic_slice_in_dim(padded, first_row, key_rows, 0)
        scores, query_hot, key_hot = block_scores(
            queries,
            window[:, :, head_size : 2 * head_size],
            bias_table,
            lax.dynamic_slice_in_dim(segment, first_row, block_rows, 0),
            lax.dynamic_slice_in_dim(segment_pad, first_row, key_rows, 0),
            lax.dynamic_slice_in_dim(crop_place, first_row, block_rows, 0),
            lax.dynamic_slice_in_dim(place_pad, first_row, key_rows, 0),
            score_scale,
        )
        return (queries, window, scores, query_hot, key_hot)

    def attend(block_index):
        queries, window, scores, query_hot, key_hot = block_inputs(block_index)
        row_max = jnp.max(scores, axis=-1, keepdims=True)
        raised = jnp.exp(scores - row_max)
        row_sum = jnp.sum(raised, axis=-1, keepdims=True)
        weights_low = (raised / row_sum).astype(jnp.bfloat16)
        output = jnp.einsum(
            "hqk,khd->qhd",
            weights_low,
            window[:, :, 2 * head_size :],
            preferred_element_type=jnp.float32,
        )
        return (output.astype(jnp.bfloat16), row_max[..., 0] + jnp.log(row_sum[..., 0]))

    attended, log_total = lax.map(attend, jnp.arange(blocks, dtype=jnp.int32))
    attn_flat = attended.reshape(group_rows, head_count * head_size)
    proj_flat = proj_weight.reshape(head_count * head_size, feature_width)
    attn_sum = lax.psum_scatter(
        jnp.dot(attn_flat, proj_flat, preferred_element_type=jnp.float32).astype(jnp.bfloat16),
        "tensor",
        scatter_dimension=0,
        tiled=True,
    ).astype(jnp.float32)
    middle = patch_full + attn_sum + proj_bias
    normed_two, norm_pull_two = jax.vjp(layer_norm, middle, mlp_gain, mlp_shift)
    group_normed_two = lax.all_gather(normed_two.astype(jnp.bfloat16), "tensor", axis=0, tiled=True)
    before = (
        jnp.dot(group_normed_two, hidden_weight, preferred_element_type=jnp.float32) + hidden_bias
    )
    active, gelu_pull = jax.vjp(partial(jax.nn.gelu, approximate=False), before)
    active_low = active.astype(jnp.bfloat16)
    mlp_sum = lax.psum_scatter(
        jnp.dot(
            lax.slice_in_dim(active_low, 0, row_count * lax.axis_size("tensor"), axis=0),
            output_weight,
            preferred_element_type=jnp.float32,
        ).astype(jnp.bfloat16),
        "tensor",
        scatter_dimension=0,
        tiled=True,
    ).astype(jnp.float32)
    result = middle + mlp_sum + output_bias
    pooled = jnp.dot(pool_matrix, result, precision=HIGH).astype(jnp.bfloat16)
    all_pooled = lax.all_gather(pooled, ("dp", "tensor"), axis=0, tiled=True)
    proto_full = prototypes.astype(jnp.float32)
    inverse = lax.rsqrt(jnp.sum(proto_full * proto_full, axis=1, keepdims=True) + 1e-06)
    unit = proto_full * inverse
    unit_low = unit.astype(jnp.bfloat16)
    crop_grads = lax.psum_scatter(
        jnp.dot(score_grad, unit_low, preferred_element_type=jnp.float32),
        ("dp", "tensor"),
        scatter_dimension=0,
        tiled=True,
    )
    unit_grad = jnp.einsum("cp,cd->pd", score_grad, all_pooled, preferred_element_type=jnp.float32)
    keep = (1 - frozen).astype(jnp.float32)[:, None]
    prototype_grad = (
        (unit_grad - unit * jnp.sum(unit * unit_grad, axis=1, keepdims=True)) * inverse * keep
    )
    result_grad = out_grad.astype(jnp.float32) + jnp.dot(pool_matrix.T, crop_grads, precision=HIGH)
    output_bias_part = jnp.sum(result_grad, axis=0)
    group_update_grad = lax.all_gather(
        result_grad.astype(jnp.bfloat16), "tensor", axis=0, tiled=True
    )
    output_weight_grad = jnp.dot(
        active_low.T, group_update_grad, preferred_element_type=jnp.float32
    )
    active_grad = jnp.dot(group_update_grad, output_weight.T, preferred_element_type=jnp.float32)
    before_grad = gelu_pull(active_grad)[0].astype(jnp.bfloat16)
    hidden_bias_grad = jnp.sum(before_grad.astype(jnp.float32), axis=0)
    hidden_weight_grad = jnp.dot(
        group_normed_two.T, before_grad, preferred_element_type=jnp.float32
    )
    normed_two_grad = lax.psum_scatter(
        jnp.dot(before_grad, hidden_weight.T, preferred_element_type=jnp.float32).astype(
            jnp.bfloat16
        ),
        "tensor",
        scatter_dimension=0,
        tiled=True,
    ).astype(jnp.float32)
    middle_part, mlp_gain_part, mlp_shift_part = norm_pull_two(normed_two_grad)
    middle_grad = result_grad + middle_part
    proj_bias_part = jnp.sum(middle_grad, axis=0)
    group_attn_grad = lax.all_gather(middle_grad.astype(jnp.bfloat16), "tensor", axis=0, tiled=True)
    proj_weight_grad = jnp.dot(attn_flat.T, group_attn_grad, preferred_element_type=jnp.float32)
    attended_grad = jnp.dot(group_attn_grad, proj_flat.T, preferred_element_type=jnp.float32)
    attended_grad = attended_grad.astype(jnp.bfloat16).reshape(group_rows, head_count, head_size)

    def attend_back(carry, block_index):
        key_grads, table_grads = carry
        queries, window, scores, query_hot, key_hot = block_inputs(block_index)
        first_row = block_index * block_rows
        softmax_full = jnp.exp(scores - log_total[block_index][..., None])
        softmax_low = softmax_full.astype(jnp.bfloat16)
        out_grads = lax.dynamic_slice_in_dim(attended_grad, first_row, block_rows, 0)
        value_grads = jnp.einsum(
            "hqk,qhd->khd", softmax_low, out_grads, preferred_element_type=jnp.float32
        )
        weight_grads = jnp.einsum(
            "qhd,khd->hqk",
            out_grads,
            window[:, :, 2 * head_size :],
            preferred_element_type=jnp.float32,
        )
        centered = jnp.sum(softmax_full * weight_grads, axis=-1, keepdims=True)
        score_grads = (softmax_full * (weight_grads - centered)).astype(jnp.bfloat16)
        query_grads = (
            jnp.einsum(
                "hqk,khd->qhd",
                score_grads,
                window[:, :, head_size : 2 * head_size],
                preferred_element_type=jnp.float32,
            )
            * score_scale
        )
        key_part = (
            jnp.einsum("hqk,qhd->khd", score_grads, queries, preferred_element_type=jnp.float32)
            * score_scale
        )
        joined = jnp.concatenate([key_part, value_grads], axis=2)
        current = lax.dynamic_slice_in_dim(key_grads, first_row, key_rows, 0)
        key_grads = lax.dynamic_update_slice_in_dim(key_grads, current + joined, first_row, 0)
        by_key_place = jnp.einsum(
            "hqk,kb->hqb", score_grads, key_hot, preferred_element_type=jnp.float32
        )
        table_grads = table_grads + jnp.einsum(
            "qa,hqb->hab", query_hot.astype(jnp.float32), by_key_place, precision=HIGH
        )
        return ((key_grads, table_grads), query_grads)

    carry_start = (
        jnp.zeros((group_rows + 2 * halo_rows, head_count, 2 * head_size), jnp.float32),
        jnp.zeros((head_count, 49, 49), jnp.float32),
    )
    (key_grads, table_grads), query_grads = lax.scan(
        attend_back, carry_start, jnp.arange(blocks, dtype=jnp.int32)
    )
    query_grads = query_grads.reshape(group_rows, head_count, head_size)
    mixed_grad = jnp.concatenate(
        [query_grads, key_grads[halo_rows : halo_rows + group_rows]], axis=2
    ).astype(jnp.bfloat16)
    column_sums = jnp.sum(mixed_grad.astype(jnp.float32), axis=0)
    qkv_bias_grad = jnp.concatenate(
        [column_sums[:, :head_size], column_sums[:, 2 * head_size :]], axis=1
    )
    mixed_flat = mixed_grad.reshape(group_rows, head_count * 3 * head_size)
    qkv_weight_grad = jnp.dot(group_normed.T, mixed_flat, preferred_element_type=jnp.float32)
    rel_table_grad = jnp.dot(table_grads.reshape(head_count, 2401), table_hot, precision=HIGH)
    normed_one_grad = lax.psum_scatter(
        jnp.dot(mixed_flat, qkv_flat.T, preferred_element_type=jnp.float32).astype(jnp.bfloat16),
        "tensor",
        scatter_dimension=0,
        tiled=True,
    ).astype(jnp.float32)
    patch_part, attn_gain_part, attn_shift_part = norm_pull_one(normed_one_grad)
    patch_grad = middle_grad + patch_part
    grad_parts = (
        qkv_weight_grad,
        qkv_bias_grad,
        rel_table_grad,
        proj_weight_grad,
        hidden_weight_grad,
        hidden_bias_grad,
        output_weight_grad,
    )
    flattened = jnp.concatenate([piece.reshape(-1) for piece in grad_parts])
    data_parts = lax.axis_size("dp")
    grad_length = flattened.shape[0]
    padded_length = -(-grad_length // data_parts) * data_parts
    flattened = jnp.pad(flattened, (0, padded_length - grad_length))
    shares = lax.psum_scatter(
        flattened.astype(jnp.bfloat16), "dp", scatter_dimension=0, tiled=True
    ).astype(jnp.float32)
    gathered = lax.all_gather(shares.astype(jnp.bfloat16), "dp", axis=0, tiled=True).astype(
        shares.dtype
    )[:grad_length]
    summed = []
    position_now = 0
    for piece in grad_parts:
        piece_length = piece.size
        summed.append(gathered[position_now : position_now + piece_length].reshape(piece.shape))
        position_now = position_now + piece_length
    smalls = lax.psum(
        (
            attn_gain_part,
            attn_shift_part,
            proj_bias_part,
            mlp_gain_part,
            mlp_shift_part,
            output_bias_part,
        ),
        ("dp", "tensor"),
    )
    return (
        result.astype(jnp.bfloat16),
        patch_grad,
        smalls[0],
        smalls[1],
        summed[0].reshape(feature_width, head_count, 3 * head_size),
        summed[1],
        summed[2],
        summed[3].reshape(head_count, head_size, feature_width),
        smalls[2],
        smalls[3],
        smalls[4],
        summed[4],
        summed[5],
        summed[6],
        smalls[5],
        prototype_grad,
    )


def solution(mesh):
    return jax.shard_map(
        per_device,
        mesh=mesh,
        in_specs=(
            P(("dp", "tensor"), None),
            P(("dp", "tensor"), None),
            P(None, ("dp", "tensor")),
            P("dp"),
            P(("dp", "tensor")),
            P(),
            P(),
            P(None, "tensor", None),
            P("tensor", None),
            P("tensor", None),
            P("tensor", None, None),
            P(),
            P(),
            P(),
            P(None, "tensor"),
            P("tensor"),
            P("tensor", None),
            P(),
            P(("dp", "tensor"), None),
        ),
        out_specs=(
            P(("dp", "tensor"), None),
            P(("dp", "tensor"), None),
            P(),
            P(),
            P(None, "tensor", None),
            P("tensor", None),
            P("tensor", None),
            P("tensor", None, None),
            P(),
            P(),
            P(),
            P(None, "tensor"),
            P("tensor"),
            P("tensor", None),
            P(),
            P(("dp", "tensor"), None),
        ),
        check_vma=False,
    )
```

profile of v0, /device:TPU:0, one launch (start us, length us, event | category | flops | bytes accessed | tf_op | source)
XLA Modules:
  0.0 3034.3 jit_solution(6259155224773630758)
XLA Ops:
  18.9 2116.9 %gather_fusion = f32[148240,12]{1,0:T(8,128)} fusion(f32[12,49,49]{0,2,1:T(8,128)} %copy.60, s32[148240]{0:T(1024)S(1)} %reshape.340), kind=kCustom, calls=%fused_computation | custom fusion | bytes 15416960 | tf_op jit(solution)/shard_map/while/body/eval_jaxpr/gather | solution.py:57
  2135.8 41.2 %copy.61 = f32[148240,12]{0,1:T(8,128)} copy(f32[148240,12]{1,0:T(8,128)} %gather_fusion) | data formatting | bytes 14231040 | tf_op jit(solution)/shard_map/while/body/eval_jaxpr/gather | solution.py:57
  2177.0 17.4 reshape.343
  2194.4 9.0 copy.62
  2204.0 8.3 all-gather
  2216.4 6.7 fusion.121
  2229.8 10.9 fusion
  2264.2 7.5 all-gather.1
  2276.8 128.4 %all-reduce.23.cloned.1.call-done = f32[320,768]{0,1:T(8,128)} async-done(((f32[320,768]{0,1:T(8,128)}), f32[320,768]{0,1:T(8,128)}) %all-reduce.23.cloned.1.call-update) | async-done | bytes 983056
  2408.0 8.0 all-gather.2
  2417.0 8.8 fusion.110
  2430.4 10.3 fusion.2
  2449.8 5.6 reshape.331
  2455.5 5.3 reshape.332
  2463.8 7.4 all-gather.3
  2477.4 9.6 multiply_reduce_fusion
  2487.0 7.1 multiply_convert_fusion
  2500.2 5.5 fusion.39
  2529.8 111.2 %concatenate.29 = bf16[3543276]{0:T(1024)(128)(2,1)} concatenate(bf16[884736]{0:T(1024)(128)(2,1)} %reshape.325, bf16[768]{0:T(1024)(128)(2,1)S(1)} %reshape.326, bf16[2028]{0:T(1024)(128)(2,1)S(1)} %reshape.328, bf16[294912]{0:T(1024)(128)(2,1)} %reshape.330, bf16[1179648]{0:T(1024)(128)(2,1)} %reshape.331, bf16[1536]{0:T(1024)(128)(2,1)S(1)} %copy-done.30, ...), dimensions={0} | concatenate | bytes 14173104 | tf_op jit(solution)/shard_map/concatenate | solution.py:301
  2640.9 7.4 pad.19
  2654.2 144.0 %all-reduce.25.cloned.1.call-done = bf16[3543280]{0:T(1024)(128)(2,1)} async-done(((bf16[3543280]{0:T(1024)(128)(2,1)}), bf16[3543280]{0:T(1024)(128)(2,1)}) %all-reduce.25.cloned.1.call-update) | async-done | bytes 7086576
  2803.7 7.7 dynamic-update-slice
  2814.9 17.8 fusion.109
  2844.1 78.1 %all-gather.4 = bf16[32,10,768]{2,1,0:T(8,128)(2,1)} all-gather(bf16[1,10,768]{2,1,0:T(8,128)(2,1)S(1)} %fusion.45), channel_id=1, replica_groups=mesh['dp'=16,'tensor'=2] {'dp','tensor'}, dimensions={0}, use_global_device_ids=true | all-gather | bytes 506880 | tf_op jit(solution)/shard_map/all_gather | solution.py:178
  2924.5 4.7 fusion.9
  2933.0 6.7 copy.67
  2946.3 37.7 %all-reduce.15 = (f32[768]{0:T(1024)}, f32[768]{0:T(1024)}, f32[768]{0:T(1024)}, f32[768]{0:T(1024)}, f32[768]{0:T(1024)}, /*index=5*/f32[768]{0:T(1024)}) all-reduce(f32[768]{0:T(1024)S(1)} %get-tuple-element.151, f32[768]{0:T(1024)S(1)} %get-tuple-element.154, ...), channel_id=1, replica_groups=mesh['dp'=16,'tensor'=2] {'dp','tensor'}, use_global_device_ids=true, to_apply=%region_24.25 | all-reduce | flops 4608 | bytes 36864 | tf_op jit(solution)/shard_map/psum | solution.py:318
  2986.4 6.5 fusion.116
  2992.8 5.8 reshape.335
  2998.6 6.0 reshape.336
  3008.1 6.7 reshape_reshape.6
  3014.8 5.9 copy.66
  (199 shorter events, 157.5 us)
Async XLA Ops:
  7.2 2409.8 %copy-start = (bf16[1536,768]{1,0:T(8,128)(2,1)S(1)}, bf16[1536,768]{1,0:T(8,128)(2,1)}, u32[]{:S(2)}) copy-start(bf16[1536,768]{1,0:T(8,128)(2,1)} %param.36) | copy-start | bytes 7077892
  7.2 2398.0 %all-reduce.23.cloned.1.call-start = ((), (), s32[]{:S(2)}) async-start(), calls=%async_computation.1 | async-start | bytes 2359296
  2194.4 9.0 copy-start.5
  2194.4 9.4 copy-start.20
  2194.4 9.4 copy-start.28
  2203.4 9.8 copy-start.21
  2203.7 8.5 copy-start.24
  2216.4 7.9 copy-start.6
  2240.8 20.8 collective-permute-start
  2254.3 8.5 copy-start.18
  2256.9 6.4 copy-start.19
  2256.9 541.3 %all-reduce.25.cloned.1.call-start = ((), (), s32[]{:S(2)}) async-start(), calls=%async_computation.2 | async-start | bytes 14176256
  2258.6 146.6 %copy-start.33 = (f32[10]{0:T(128)}, f32[10]{0:T(128)S(1)}, u32[]{:S(2)}) copy-start(f32[10]{0:T(128)S(1)} %get-tuple-element.190) | copy-start | bytes 124
  2258.7 146.5 %copy-start.31 = (s32[170]{0:T(256)}, s32[170]{0:T(256)S(1)}, u32[]{:S(2)}) copy-start(s32[170]{0:T(256)S(1)} %broadcast_add_fusion.1) | copy-start | bytes 2044
  2261.6 11.1 copy-start.36
  2272.7 132.6 %copy-start.17 = (bf16[170,768]{1,0:T(8,128)(2,1)S(1)}, bf16[170,768]{1,0:T(8,128)(2,1)}, u32[]{:S(2)}) copy-start(bf16[170,768]{1,0:T(8,128)(2,1)} %param.21) | copy-start | bytes 783364
  2417.0 8.8 copy-start.35
  2440.7 20.1 collective-permute-start.2
  2443.3 3.7 copy-start.14
  2497.0 3.2 copy-start.10
  2500.2 5.5 copy-start.8
  2500.2 5.5 copy-start.16
  2516.2 4.4 copy-start.26
  2523.6 6.2 copy-start.30
  2648.4 337.9 %all-reduce.21.cloned.1.call-start = ((), (), s32[]{:S(2)}) async-start(), calls=%async_computation | async-start | bytes 14176256
  2811.4 25.2 copy-start.27
  2811.5 31.1 %copy-start.29 = (f32[768]{0:T(1024)S(1)}, f32[768]{0:T(1024)}, u32[]{:S(2)}) copy-start(f32[768]{0:T(1024)} %param.37) | copy-start | bytes 9220
  2811.5 31.1 %copy-start.32 = (s32[170]{0:T(256)S(1)}, s32[170]{0:T(256)}, u32[]{:S(2)}) copy-start(s32[170]{0:T(256)} %copy-done.31) | copy-start | bytes 2044
  2833.5 5.8 collective-permute-start.1
  2837.4 102.3 %collective-permute-start.3 = (bf16[6,768]{1,0:T(8,128)(2,1)S(1)}, bf16[6,768]{1,0:T(8,128)(2,1)}, u32[]{:S(2)}, u32[]{:S(2)}) collective-permute-start(bf16[6,768]{1,0:T(8,128)(2,1)S(1)} %slice.95), channel_id=1, source_target_pairs={{0,1},{2,3},{4,5},{6,7},{8,9},{10,11},{12,13},{14,15},{16,17},{18,... | collective-permute-start | bytes 27656
  2924.5 4.7 copy-start.4
  2933.0 11.8 copy-start.25
  (12 other events, 20.6 us)
Sparse Core Ops, SparseCore 0:
  2257.0 148.1 all-reduce.22
  2648.5 149.6 all-reduce.24
  2811.6 153.8 all-reduce.20
where the time goes:
time: 3070 us; the launch traced here: 3030 us
  local copies, waits for them, and re-layouts  2420 us (79%)
  waiting for transfers between devices  272 us (9%)
  blocking collectives  186 us (6%)
  matrix products  90.8 us (3%)
  other arithmetic  33.8 us (1%)
    gather x4, local copies, waits for them, and re-layouts, block_scores(): rel_bias = bias_table[:, query_place[:, None], key_place[None, :]]  2180 us
    unnamed x10, waiting for transfers between devices  272 us
    concatenate x1, local copies, waits for them, and re-layouts, per_device(): flattened = jnp.concatenate([piece.reshape(-1) for piece in grad_parts])  111 us
    all_gather x1, blocking collectives, per_device(): all_pooled = lax.all_gather(pooled, ('dp', 'tensor'), axis=0, tiled=True)  78.1 us
  transfers between devices with their start and end apart: 7, of which 2 were waited for; matrix products, arithmetic and copies ran while one was open for 3% of the time, Pallas kernels for 0%

commit v1 on v0

v1 whole, which is shorter than its diff:
```python
import functools

import jax
import jax.numpy as jnp
import numpy as np
from jax import lax
from jax.experimental import pallas as pl
from jax.experimental.pallas import tpu as pltpu
from jax.sharding import PartitionSpec as P

EPS = 1e-05
BF = jnp.bfloat16
F32 = jnp.float32
HIGH = lax.Precision.HIGHEST
SIDE = 7
PLACES = SIDE * SIDE
OFFSETS = 2 * SIDE - 1
LAST = (SIDE - 1) * (OFFSETS + 1)
SLOTS = 96
LANES = 128
COST = 0.01


def nn(a, b):
    return jnp.dot(a, b, preferred_element_type=F32)


def nt(a, b):
    return lax.dot_general(a, b, (((1,), (1,)), ((), ())), preferred_element_type=F32)


def split(v):
    high = v.astype(BF)
    return high, (v - high.astype(F32)).astype(BF)


def line(ref):
    return ref[...].reshape(1, -1)


def normalize(v):
    center = v - jnp.mean(v, axis=-1, keepdims=True)
    spread = jnp.mean(center * center, axis=-1, keepdims=True)
    inverse = lax.rsqrt(spread + EPS)
    return center * inverse, inverse


def norm_back(hat, inverse, gain, grad):
    scaled = grad * gain
    first = jnp.mean(scaled, axis=-1, keepdims=True)
    second = jnp.mean(scaled * hat, axis=-1, keepdims=True)
    return (scaled - first - hat * second) * inverse


def row_layout(sizes_ref, base, crops, rows, padded, axis):
    shape = (padded, 1) if axis == 0 else (1, padded)
    position = lax.broadcasted_iota(jnp.int32, shape, axis)
    start = jnp.int32(0)
    segment = jnp.zeros(shape, jnp.int32)
    first = jnp.zeros(shape, jnp.int32)
    length = jnp.zeros(shape, jnp.int32)
    for crop in range(crops):
        size = sizes_ref[base + crop]
        reached = position >= start
        segment = jnp.where(reached, crop, segment)
        first = jnp.where(reached, start, first)
        length = jnp.where(reached, size, length)
        start = start + size
    offset = position - first
    by_seven = offset + ((offset * 37) >> 8) * (OFFSETS - SIDE)
    by_three = offset + ((offset * 11) >> 5) * (OFFSETS - 3)
    place = jnp.where(length == PLACES, by_seven, by_three)
    real = position < rows
    segment = jnp.where(real, segment, crops)
    place = jnp.where(real, place, 2 * LANES)
    return segment, place, jnp.where(real, length, 1).astype(F32)


def call(body, grid, ins, outs, scratch, prefetch, args, name, flops, vmem):
    moved = sum(int(np.prod(a.shape)) * a.dtype.itemsize for a in args)
    moved += sum(int(np.prod(s.shape)) * s.dtype.itemsize for s, _ in outs)
    return pl.pallas_call(
        body,
        grid_spec=pltpu.PrefetchScalarGridSpec(
            num_scalar_prefetch=prefetch,
            grid=grid,
            in_specs=ins,
            out_specs=[spec for _, spec in outs],
            scratch_shapes=scratch,
        ),
        out_shape=[shape for shape, _ in outs],
        compiler_params=pltpu.CompilerParams(
            dimension_semantics=("arbitrary",) * len(grid), vmem_limit_bytes=vmem * 2**20
        ),
        cost_estimate=pl.CostEstimate(
            flops=int(flops * COST), bytes_accessed=int(moved * COST), transcendentals=0
        ),
        name=name,
    )(*args)


def whole(shape):
    zeros = (0,) * len(shape)
    return pl.BlockSpec(tuple(shape), lambda *_: zeros)


def sds(shape, dtype):
    return jax.ShapeDtypeStruct(tuple(shape), dtype)


def crop_grad_kernel(groups, crops, bits, ids, score, proto, keep, send, total):
    step = pl.program_id(0)

    @pl.when(step == 0)
    def _():
        total[...] = jnp.zeros_like(total)

    p = proto[...].astype(F32)
    unit = p * lax.rsqrt(jnp.sum(p * p, axis=1, keepdims=True) + 1e-06)
    total[...] += nn(score[...], unit.astype(BF))

    @pl.when(step == pl.num_programs(0) - 1)
    def _():
        odd = (ids[1] & 1) == 1
        for pair in range(groups // 2):
            at = 0
            for bit in bits:
                at = 2 * at + (((pair ^ (ids[1] >> 1)) >> (bit.bit_length() - 2)) & 1)
            first = total[2 * pair * crops : (2 * pair + 1) * crops, :]
            second = total[(2 * pair + 1) * crops : (2 * pair + 2) * crops, :]
            keep[at, 0:crops, :] = jnp.where(odd, second, first)
            send[at, 0:crops, :] = jnp.where(odd, first, second)
            if keep.shape[1] > crops:
                tail = jnp.zeros((keep.shape[1] - crops, keep.shape[2]), F32)
                keep[at, crops:, :] = tail
                send[at, crops:, :] = tail


def table_kernel(heads, scale, ids, rel, tables):
    for h in range(heads):
        line = jnp.concatenate(
            [rel[h : h + 1, :], jnp.zeros((1, 2 * LANES - rel.shape[1]), F32)], axis=1
        )
        line = jnp.broadcast_to(line * scale, (8, 2 * LANES))
        line = pltpu.roll(line, 2 * LANES - LAST % 8, 1)
        line = jnp.broadcast_to(line[0:1, :], (SLOTS, 2 * LANES))
        slid = pltpu.roll(line, 2 * LANES - LAST // 8 * 8, 1, stride=1, stride_axis=0)
        high, low = split(slid[:, 0:LANES])
        tables[2 * h * SLOTS : (2 * h + 1) * SLOTS, :] = high
        tables[(2 * h + 1) * SLOTS : (2 * h + 2) * SLOTS, :] = low


def attend_kernel(
    dims, ids, sizes, x0, gain, shift, w, bias, tables, wp, xo, ho, qo, po, oo, ao, xs, rr, hide
):
    first, rows, padded, heads, head_size, crops, unroll = dims
    wide = 3 * head_size
    step = pl.program_id(0)
    base = ((first + step) ^ ids[0]) * crops
    tail = padded - 8
    xs[tail:padded, :] = jnp.zeros((padded - tail, xs.shape[1]), F32)
    xs[0:rows, :] = x0[0].astype(F32)
    x = xs[...]
    xo[0] = x.astype(BF)
    hat, _ = normalize(x)
    h1 = (hat * line(gain) + line(shift)).astype(BF)
    ho[0] = h1
    mixed = nt(w[...], h1)
    bias_cols = jnp.transpose(bias[...])
    for h in range(heads):
        low = h * wide
        qo[0, low : low + head_size, :] = (
            mixed[low : low + head_size] + bias_cols[0:head_size, h : h + 1]
        ).astype(BF)
        qo[0, low + head_size : low + 2 * head_size, :] = mixed[
            low + head_size : low + 2 * head_size
        ].astype(BF)
        qo[0, low + 2 * head_size : low + wide, :] = (
            mixed[low + 2 * head_size : low + wide] + bias_cols[head_size : 2 * head_size, h : h + 1]
        ).astype(BF)
    seg_row, place_row, _ = row_layout(sizes, base, crops, rows, padded, 1)
    seg_col, place_col, _ = row_layout(sizes, base, crops, rows, padded, 0)
    hide[...] = jnp.where(seg_col == seg_row, 0.0, -jnp.inf).astype(F32)
    lane = lax.broadcasted_iota(jnp.int32, (padded, LANES), 1)
    hot = (lane == place_col).astype(F32).astype(BF)
    slot = lax.broadcasted_iota(jnp.int32, (LANES, padded), 0)
    hot_t = (slot == place_row).astype(F32).astype(BF)

    rr[...] = nn(tables[...], hot_t).astype(BF)
    zeros = jnp.zeros((2 * LANES - 2 * SLOTS - head_size, padded), BF)

    def some_heads(i, carry):
        for u in range(unroll):
            h = i * unroll + u
            slab = qo[0, pl.ds(pl.multiple_of(h * wide, 32), wide), :]
            q = slab[0:head_size]
            v = slab[2 * head_size : wide]
            k = slab[head_size : 2 * head_size]
            left_t = jnp.transpose(jnp.concatenate([k, hot_t[0:SLOTS]], axis=0))
            left = jnp.concatenate([left_t, hot], axis=1)
            biases = rr[pl.ds(pl.multiple_of(h * 2 * SLOTS, 64), 2 * SLOTS), :]
            right = jnp.concatenate([q, biases, zeros], axis=0)
            s = nn(left, right) * (head_size**-0.5) + hide[...]
            e = jnp.exp(s - jnp.max(s, axis=0, keepdims=True))
            p = (e * (1.0 / jnp.sum(e, axis=0, keepdims=True))).astype(BF)
            po[0, h] = p
            oo[0, pl.ds(pl.multiple_of(h * head_size, 32), head_size), :] = nn(v, p).astype(BF)
        return carry

    lax.fori_loop(0, heads // unroll, some_heads, 0)
    ao[0] = nn(jnp.transpose(oo[0]), wp[...]).astype(BF)


def hidden_kernel(
    dims, ids, sizes, x0, x1, a0, a1, b0, b1, g0, g1, *rest,
):
    parts, rows, padded, crops, group_crops = dims
    terms, rest = rest[: 2 * parts], rest[2 * parts :]
    pb, gain, shift, w1, bias1, w2 = rest[:6]
    y1o, gyo, h2o, gzo, mo, guo, gh0, gh1, obo, hbo, gs, cs, total = rest[6:]
    step = pl.program_id(0)

    @pl.when(step == 0)
    def _():
        cs[...] = jnp.zeros_like(cs)
        cs[0 : terms[0].shape[1], :] = sum(term[0] for term in terms)
        high, low = split(cs[...])
        bias_sum = jnp.zeros((1, gs.shape[1]), F32)
        tail, half = padded - 8, parts // 2
        for r in range(parts):
            x, own, other, g = (x0, a0, b1, g0) if r < half else (x1, a1, b0, g1)
            k = r % half
            y1 = x[k].astype(F32) + (own[k].astype(F32) + other[k].astype(F32)) + line(pb)
            y1o[r] = y1
            hat, _ = normalize(y1)
            h2o[r * padded : (r + 1) * padded, :] = (hat * line(gain) + line(shift)).astype(BF)
            base = (ids[0] ^ r) * crops
            segment, _, length = row_layout(sizes, base, crops, rows, padded, 0)
            lane = lax.broadcasted_iota(jnp.int32, (padded, cs.shape[0]), 1)
            mine = (lane == segment + base) & (segment < crops)
            hot = mine.astype(F32).astype(BF)
            gs[tail:padded, :] = jnp.zeros((padded - tail, gs.shape[1]), F32)
            gs[0:rows, :] = g[k].astype(F32)
            gy = gs[...] + (nn(hot, high) + nn(hot, low)) / length
            gyo[r] = gy
            gzo[r * padded : (r + 1) * padded, :] = gy.astype(BF)
            bias_sum = bias_sum + jnp.sum(gy, axis=0, keepdims=True)
        obo[...] = bias_sum
        total[...] = jnp.zeros_like(total)

    u = nn(h2o[...], w1[...]) + bias1[...]
    spread = 0.5 * (1.0 + lax.erf(u * np.float32(np.sqrt(0.5))))
    mo[...] = (u * spread).astype(BF)
    slope = spread + u * (jnp.exp(-0.5 * u * u) * np.float32(1.0 / np.sqrt(2.0 * np.pi)))
    gu = (nt(gzo[...], w2[...]) * slope).astype(BF)
    guo[...] = gu
    hbo[...] = jnp.sum(gu.astype(F32), axis=0, keepdims=True)
    total[...] += nt(gu, w1[...])

    @pl.when(step == pl.num_programs(0) - 1)
    def _():
        half = parts // 2
        for r in range(parts):
            gho = gh0 if r < half else gh1
            gho[r % half] = total[r * padded : (r + 1) * padded, :].astype(BF)


def spot(pair, mine, core, orders):
    spots = []
    for order in orders:
        at = 0
        for bit in order:
            source = pair if bit == order[-1] else pair ^ mine
            at = 2 * at + ((source >> (bit.bit_length() - 2)) & 1)
        spots.append(at)
    return jnp.where(core == 1, spots[1], spots[0])


def put_chunk(keep, send, spots, odd, first, second, at):
    rows = pl.ds(at, first.shape[0])
    keep[spots[0], rows, :] = jnp.where(odd, second, first).astype(BF)
    send[spots[1], rows, :] = jnp.where(odd, first, second).astype(BF)


def pair_spots(pair, rank, orders):
    core, mine = rank & 1, rank >> 1
    return spot(pair, mine, core, orders), spot(pair, mine, 1 - core, orders)


def hidden_grad_kernel(dims, ids, h2, gz, m, gu, keep, send, h2t):
    chunks, chunks_step, wide, orders = dims
    step = pl.program_id(0)
    rank = ids[1] & (chunks - 1)
    odd = (rank & 1) == 1

    @pl.when(step == 0)
    def _():
        h2t[...] = jnp.transpose(h2[...])

    d1 = nn(h2t[...], gu[...])
    n1 = d1.shape[0] // chunks
    steps = d1.shape[1] // wide
    for pair in range(chunks // 2):
        spots = pair_spots(pair, rank, orders)
        for part in range(steps):
            piece = d1[2 * pair * n1 : (2 * pair + 2) * n1, part * wide : (part + 1) * wide]
            at = pl.multiple_of((step * steps + part) * n1, 16)
            put_chunk(keep, send, spots, odd, piece[:n1], piece[n1:], at)
    d2 = nn(jnp.transpose(m[...]), gz[...])
    n2 = d2.shape[0] // chunks_step
    base = keep.shape[1] - d2.shape[1] // wide * n2
    for pair in range(chunks_step // 2):
        spots = pair_spots(step * (chunks_step // 2) + pair, rank, orders)
        for part in range(d2.shape[1] // wide):
            piece = d2[2 * pair * n2 : (2 * pair + 2) * n2, part * wide : (part + 1) * wide]
            put_chunk(keep, send, spots, odd, piece[:n2], piece[n2:], base + part * n2)


def share_kernel(parts, padded, m, w2, zo, total):
    step = pl.program_id(0)

    @pl.when(step == 0)
    def _():
        total[...] = jnp.zeros_like(total)

    total[...] += nn(m[...], w2[...])

    @pl.when(step == pl.num_programs(0) - 1)
    def _():
        for r in range(parts):
            zo[r] = total[r * padded : (r + 1) * padded, :].astype(BF)


def result_kernel(dims, ids, sizes, y1, z0, z1, bias, out, pooled):
    rows, padded, crops = dims
    y = y1[0] + (z0[0].astype(F32) + z1[0].astype(F32)) + line(bias)
    out[...] = y[0:rows, :].astype(BF)
    segment, _, _ = row_layout(sizes, ids[0] * crops, crops, rows, padded, 1)
    crop = lax.broadcasted_iota(jnp.int32, (pooled.shape[1], padded), 0)
    member = ((crop == segment) & (crop < crops)).astype(F32)
    high, low = split(y)
    hot = member.astype(BF)
    count = jnp.maximum(jnp.sum(member, axis=1, keepdims=True), 1.0)
    pooled[0] = ((nn(hot, high) + nn(hot, low)) / count).astype(BF)


def attend_back_kernel(
    dims, ids, sizes, y1, gy, e0, e1, gain, x, qkv, pt, wp, w, g1o, gho, gao, gqo, sums, qb, tt, go, by
):
    first, rows, padded, heads, head_size, crops, unroll = dims
    wide = 3 * head_size
    step = pl.program_id(0)
    base = ((first + step) ^ ids[0]) * crops

    @pl.when(step == 0)
    def _():
        sums[...] = jnp.zeros_like(sums)
        qb[...] = jnp.zeros_like(qb)
        tt[...] = jnp.zeros_like(tt)

    hat2, inv2 = normalize(y1[0])
    grad2 = e0[0].astype(F32) + e1[0].astype(F32)
    gy1 = gy[0] + norm_back(hat2, inv2, line(gain), grad2)
    g1o[0] = gy1
    ga = gy1.astype(BF)
    gao[0] = ga
    sums[2:3, :] += jnp.sum(grad2 * hat2, axis=0, keepdims=True)
    sums[3:4, :] += jnp.sum(grad2, axis=0, keepdims=True)
    sums[4:5, :] += jnp.sum(gy1, axis=0, keepdims=True)
    go[...] = nt(wp[...], ga).astype(BF)
    _, place_row, _ = row_layout(sizes, base, crops, rows, padded, 1)
    _, place_col, _ = row_layout(sizes, base, crops, rows, padded, 0)
    slot = lax.broadcasted_iota(jnp.int32, (SLOTS, padded), 0)
    hot_t = (slot == LAST - place_row).astype(F32).astype(BF)
    lane = lax.broadcasted_iota(jnp.int32, (padded, LANES), 1)
    hot = (lane == place_col).astype(F32).astype(BF)
    zeros_a = jnp.zeros((LANES - wide, padded), BF)
    zeros_b = jnp.zeros((2 * head_size, padded), BF)
    scale = head_size**-0.5

    def some_heads(i, carry):
        for u in range(unroll):
            h = i * unroll + u
            at = pl.multiple_of(h * wide, 32)
            slab = qkv[0, pl.ds(at, wide), :]
            q = slab[0:head_size]
            k = slab[head_size : 2 * head_size]
            goh = go[pl.ds(pl.multiple_of(h * head_size, 32), head_size), :]
            p = pt[0, h]
            slab_t = jnp.transpose(jnp.concatenate([slab, zeros_a], axis=0))
            gp = nn(slab_t, jnp.concatenate([zeros_b, goh, zeros_a], axis=0))
            pf = p.astype(F32)
            both = pf * gp
            gs = (both - pf * jnp.sum(both, axis=0, keepdims=True)).astype(BF)
            gv = nt(goh, p)
            gk = nt(q, gs)
            gqe = nn(jnp.concatenate([k, hot_t], axis=0), gs)
            gqo[0, pl.ds(at, head_size), :] = (gqe[0:head_size] * scale).astype(BF)
            gqo[0, pl.ds(at + head_size, head_size), :] = (gk * scale).astype(BF)
            gqo[0, pl.ds(at + 2 * head_size, head_size), :] = gv.astype(BF)
            by[pl.ds(pl.multiple_of(h * SLOTS, 32), SLOTS), :] = gqe[head_size:]
        return carry

    lax.fori_loop(0, heads // unroll, some_heads, 0)
    high, low = split(by[...])
    tt[...] += nn(high, hot) + nn(low, hot)
    g = gqo[0]
    qb[...] += nt(jnp.ones((8, padded), BF), g)
    gh1 = nn(jnp.transpose(g), w[...])
    gho[0] = gh1.astype(BF)
    hat1, _ = normalize(x[0].astype(F32))
    sums[0:1, :] += jnp.sum(gh1 * hat1, axis=0, keepdims=True)
    sums[1:2, :] += jnp.sum(gh1, axis=0, keepdims=True)


def attend_grad_kernel(
    dims, ids, o0, o1, ga0, ga1, gq0, gq1, h0, h1, u0, u1, q0, q1, t0, t1, ob, hb, keep, send, small, dp, dq
):
    parts, heads, chunks, orders = dims
    half = parts // 2
    dp[...] = jnp.zeros_like(dp)
    dq[...] = jnp.zeros_like(dq)
    for r in range(parts):
        o, ga, gq, h = (o0, ga0, gq0, h0) if r < half else (o1, ga1, gq1, h1)
        dp[...] += nn(o[r % half], ga[r % half])
        dq[...] += nn(gq[r % half], h[r % half])
    n = (dp.shape[0] + dq.shape[0]) // chunks
    edge = dp.shape[0] // n
    rank = ids[1] & (chunks - 1)
    for pair in range(chunks // 2):
        source, at = (dp, 2 * pair * n) if 2 * pair < edge else (dq, (2 * pair - edge) * n)
        put_chunk(
            keep, send, pair_spots(pair, rank, orders), (rank & 1) == 1,
            source[at : at + n, :], source[at + n : at + 2 * n, :], 0,
        )
    width = small.shape[1]
    small[...] = jnp.zeros_like(small)
    small[0:5, :] = u0[0:5, :] + u1[0:5, :]
    small[5:6, :] = ob[...]
    at = 6
    for line in (q0[0:1, :] + q1[0:1, :], hb[...]):
        for low in range(0, line.shape[1], width):
            high = min(low + width, line.shape[1])
            small[at : at + 1, 0 : high - low] = line[:, low:high]
            at += 1
    held = width // (2 * LANES)
    for h in range(heads):
        block = t0[h * SLOTS : (h + 1) * SLOTS, :] + t1[h * SLOTS : (h + 1) * SLOTS, :]
        block = jnp.concatenate([block, jnp.zeros((SLOTS, LANES), F32)], axis=1)
        slid = pltpu.roll(block, 0, 1, stride=1, stride_axis=0)
        low = h % held * 2 * LANES
        small[at + h // held : at + h // held + 1, low : low + 2 * LANES] = jnp.sum(
            slid, axis=0, keepdims=True
        )


def patch_grad_kernel(rows, g1, e0, e1, x, gain, out):
    hat, inv = normalize(x[0].astype(F32))
    grad = g1[0] + norm_back(hat, inv, line(gain), e0[0].astype(F32) + e1[0].astype(F32))
    out[...] = grad[0:rows, :]


def proto_grad_kernel(dims, ids, score, pooled, proto, frozen, out, ordered):
    crops, slots, weights = dims

    @pl.when(pl.program_id(0) == 0)
    def _():
        count = pooled.shape[0]
        column = lax.broadcasted_iota(jnp.int32, (1, count), 1)
        block = column // slots
        device = jnp.zeros((1, count), jnp.int32)
        for k, weight in enumerate(weights):
            device = device + ((block >> k) & 1) * weight
        inside = column - block * slots
        target = jnp.where(inside < crops, (device ^ ids[2]) * crops + inside, -1)
        row = lax.broadcasted_iota(jnp.int32, (ordered.shape[0], count), 0)
        hot = (row == target).astype(F32).astype(BF)
        ordered[...] = nn(hot, pooled[...]).astype(BF)

    keep = (1 - frozen[...]).astype(F32).astype(BF)
    grad = nn(jnp.transpose(score[...] * keep), ordered[...])
    p = proto[...].astype(F32)
    inverse = lax.rsqrt(jnp.sum(p * p, axis=1, keepdims=True) + 1e-06)
    unit = p * inverse
    out[...] = (grad - unit * jnp.sum(unit * grad, axis=1, keepdims=True)) * inverse


def unpack_kernel(layout, group, places, own, other, *outs):
    odd = places[0] == 1
    step = pl.program_id(0)
    pairs, _, wide = own.shape
    for out, first, last, at, n, parts in layout:
        for flag, a, b, c, d in ((False, own, other, 1, 1 + pairs), (True, other, own, 1 + pairs, 1)):

            @pl.when((odd == flag) & (step >= first) & (step < last))
            def _():
                for g in range(group):
                    pair = step * group + g
                    for part in range(parts):
                        rows = slice(at + part * n, at + (part + 1) * n)
                        columns = slice(part * wide, (part + 1) * wide)
                        low = 2 * g * n
                        outs[out][low : low + n, columns] = a[places[c + pair], rows, :].astype(F32)
                        outs[out][low + n : low + 2 * n, columns] = b[
                            places[d + pair], rows, :
                        ].astype(F32)


def tie(v, *after):
    return lax.optimization_barrier((v, *after))[0]


def rounds(threads):
    done, waiting = {}, {name: next(thread) for name, thread in threads.items()}
    while waiting:
        ready = lax.optimization_barrier(waiting)
        waiting = {}
        for name, value in ready.items():
            try:
                waiting[name] = threads[name].send(value)
            except StopIteration as stop:
                done[name] = stop.value
    return done


def finish_kernel(dims, small, *outs):
    heads, head_size, hidden = dims
    width = small.shape[1]
    wide = 3 * head_size
    for i in range(6):
        outs[i][...] = small[i, :]
    at = 6
    for h in range(heads):
        row, low = at + h * wide // width, h * wide % width
        line = small[row : row + 1, low : low + wide]
        outs[6][h : h + 1, 0:head_size] = line[:, 0:head_size]
        outs[6][h : h + 1, head_size:] = line[:, 2 * head_size :]
    at += -(-heads * wide // width)
    for low in range(0, hidden, width):
        high = min(low + width, hidden)
        outs[8][low:high] = small[at, 0 : high - low]
        at += 1
    held = width // (2 * LANES)
    for h in range(heads):
        low = h % held * 2 * LANES
        row = at + h // held
        outs[7][h : h + 1, :] = small[row : row + 1, low : low + outs[7].shape[1]]


def partner(axis, bit):
    return [(i, i ^ bit) for i in range(lax.axis_size(axis))]


def swap(v, axis, bit):
    return lax.ppermute(v, axis, partner(axis, bit))


def bits_of(count):
    return [1 << i for i in range(count.bit_length() - 1)]


def add_low(a, b):
    return (a.astype(F32) + b.astype(F32)).astype(a.dtype)


def gather_halves(v, axis):
    held = v[None]
    bits = bits_of(lax.axis_size(axis))
    for bit in bits[:-1]:
        held = jnp.concatenate([held, swap(held, axis, bit)], axis=0)
    return held, swap(held, axis, bits[-1])


def sum_halves(v, axis):
    bits = bits_of(lax.axis_size(axis))
    for bit in bits[:-1]:
        other = swap(v, axis, bit)
        shape = other.shape
        other = other.reshape((shape[0] // (2 * bit), 2, bit) + shape[1:])[:, ::-1].reshape(shape)
        v = add_low(v, other)
    return v, swap(v, axis, bits[-1])


def scatter_halves(v, axis, count=None):
    bits = bits_of(count or lax.axis_size(axis))
    for bit in bits[:0:-1]:
        v = add_low(v[:bit], swap(v[bit:], axis, bit))
    return v[:1], swap(v[1:], axis, 1)


def gather_all(v, steps):
    for axis, bit in steps:
        v = jnp.concatenate([v, swap(v, axis, bit)], axis=0)
    return v


def mixed_swap(v, bits):
    size = lax.axis_size("dp")
    return lax.ppermute(v, "dp", [(i, i ^ bits[i & 1]) for i in range(size)])


def add_halves(kept, other):
    half = kept.shape[0] // 2
    return add_low(kept[:half], other[:half]), add_low(kept[half:], other[half:])


def unpack(places, own, other, layout, group, outs, name):
    return call(
        functools.partial(unpack_kernel, layout, group),
        (own.shape[0] // group,),
        [whole(own.shape), whole(own.shape)],
        outs,
        [],
        1,
        (places, own, other),
        name,
        0,
        30,
    )


def largest(count, most):
    return max(n for n in range(1, most + 1) if count % n == 0)


def per_device(
    patches,
    out_grad,
    score_grad,
    crop_size,
    frozen,
    attn_gain,
    attn_shift,
    qkv_weight,
    qkv_bias,
    rel_table,
    proj_weight,
    proj_bias,
    mlp_gain,
    mlp_shift,
    hidden_weight,
    hidden_bias,
    output_weight,
    output_bias,
    prototypes,
):
    rows, width = patches.shape
    padded = -(-rows // 16) * 16
    parts = lax.axis_size("tensor")
    groups = lax.axis_size("dp")
    heads = qkv_weight.shape[1]
    head_size = qkv_weight.shape[2] // 3
    hidden = hidden_weight.shape[1]
    inner = heads * head_size
    group_crops = crop_size.shape[0]
    crops = group_crops // parts
    slots = -(-crops // 16) * 16
    protos = prototypes.shape[0]
    all_rows = parts * padded
    half = parts // 2
    tensor_rank, dp_rank = lax.axis_index("tensor"), lax.axis_index("dp")
    ids = jnp.stack([tensor_rank, dp_rank, dp_rank * parts + tensor_rank]).astype(jnp.int32)
    chunks = groups
    while (width // chunks) % 16 or (hidden // chunks) % 16 or (4 * inner // chunks) % 16:
        chunks //= 2
    pairs = chunks // 2
    scatter = [b for b in bits_of(chunks) if b > 1]
    rest_bits = [b for b in bits_of(groups) if b >= chunks]
    orders_a = (scatter, scatter[1:2] + scatter[:1] + scatter[2:])
    orders_b = orders_a
    vector = whole((width,))

    x0, x1 = gather_halves(patches, "tensor")

    proto_step = min(512, protos)
    crop_bits = bits_of(groups)[1:]
    crop_rows = -(-group_crops // 8) * 8
    crop_shape = (groups // 2, crop_rows, width)
    def crop_step(kept, other, bit, *after):
        kept, other = (lax.optimization_barrier((v, after))[0] for v in (kept, other))
        half = kept.shape[0] // 2
        return kept[:half] + other[:half], swap(kept[half:] + other[half:], "dp", bit)

    tables = call(
        functools.partial(table_kernel, heads, head_size**0.5),
        (1,),
        [whole(rel_table.shape)],
        [(sds((heads * 2 * SLOTS, LANES), BF), whole((heads * 2 * SLOTS, LANES)))],
        [],
        1,
        (ids, rel_table),
        "tables",
        0,
        24,
    )[0]
    w_t = jnp.transpose(qkv_weight, (1, 2, 0)).reshape(3 * inner, width)
    wp = proj_weight.reshape(inner, width)
    unroll = largest(heads, 12)
    block3 = lambda a, b: pl.BlockSpec((1, a, b), lambda i, *_: (i, 0, 0))
    halves3 = lambda a, b, dtype: (sds((half, a, b), dtype), block3(a, b))

    def attend(first, x, ids):
        dims = (first, rows, padded, heads, head_size, crops, unroll)
        return call(
            functools.partial(attend_kernel, dims),
            (half,),
            [
                block3(rows, width),
                vector,
                vector,
                whole(w_t.shape),
                whole(qkv_bias.shape),
                whole(tables.shape),
                whole(wp.shape),
            ],
            [
                halves3(padded, width, BF),
                halves3(padded, width, BF),
                halves3(3 * inner, padded, BF),
                (
                    sds((half, heads, padded, padded), BF),
                    pl.BlockSpec((1, heads, padded, padded), lambda i, *_: (i, 0, 0, 0)),
                ),
                halves3(inner, padded, BF),
                halves3(padded, width, BF),
            ],
            [
                pltpu.VMEM((padded, width), F32),
                pltpu.VMEM((heads * 2 * SLOTS, padded), BF),
                pltpu.VMEM((padded, padded), F32),
            ],
            2,
            (ids, crop_size, x, attn_gain, attn_shift, w_t, qkv_bias, tables, wp),
            "attend",
            all_rows * 4 * inner * width,
            20,
        )

    crop_keep, crop_send = call(
        functools.partial(crop_grad_kernel, groups, group_crops, crop_bits),
        (protos // proto_step,),
        [
            pl.BlockSpec((score_grad.shape[0], proto_step), lambda i, s: (0, i)),
            pl.BlockSpec((proto_step, width), lambda i, s: (i, 0)),
        ],
        [(sds(crop_shape, F32), whole(crop_shape)), (sds(crop_shape, F32), whole(crop_shape))],
        [pltpu.VMEM((score_grad.shape[0], width), F32)],
        1,
        (tie(ids, tables), score_grad, prototypes),
        "crop_grads",
        2 * score_grad.shape[0] * protos * width,
        16,
    )
    crop_other = swap(tie(crop_send, x1), "dp", 1)
    g0, g1 = gather_halves(tie(out_grad, x1), "tensor")
    xf0, h1_0, qkv0, pt0, ot0, a0 = attend(0, x0, tie(ids, crop_send))
    a0, g1 = lax.optimization_barrier((a0, g1))
    b0 = swap(a0, "tensor", 1)
    crop_held = crop_step(crop_keep, crop_other, crop_bits[0], a0)
    xf1, h1_1, qkv1, pt1, ot1, a1 = attend(half, x1, tie(ids, crop_held[0]))
    b1 = swap(tie(a1, b0, g1), "tensor", 1)
    if parts > 2:
        a_all, b_all = sum_halves(jnp.concatenate([a0, a1]), "tensor")
        a0, a1, b0, b1 = a_all[:half], a_all[half:], b_all[:half], b_all[half:]
    for bit in crop_bits[1:-1]:
        crop_held = crop_step(*crop_held, bit, a1)
    kept, other = (tie(v, a1) for v in crop_held)
    kept, sent = kept[:1] + other[:1], kept[1:] + other[1:]
    far = crop_bits[-1] * parts
    crop_terms = [kept, swap(sent, ("dp", "tensor"), far)]
    for move in range(1, parts):
        crop_terms += [
            swap(kept, ("dp", "tensor"), move),
            swap(sent, ("dp", "tensor"), far + move),
        ]

    hidden_step = 768 if hidden % 768 == 0 else hidden
    hidden_steps = hidden // hidden_step
    crops_slots = -(-group_crops // 16) * 16
    full = whole((parts, padded, width))
    columns = lambda a: pl.BlockSpec((a, hidden_step), lambda i, *_: (0, i))
    y1, gy, h2, gz, m, gu, gh2_near, gh2_far, ob, hb = call(
        functools.partial(hidden_kernel, (parts, rows, padded, crops, group_crops)),
        (hidden_steps,),
        [
            *[whole((half, padded, width))] * 6,
            whole(g0.shape),
            whole(g1.shape),
            *[whole(kept.shape)] * len(crop_terms),
            vector,
            vector,
            vector,
            columns(width),
            columns(1),
            pl.BlockSpec((hidden_step, width), lambda i, *_: (i, 0)),
        ],
        [
            (sds((parts, padded, width), F32), full),
            (sds((parts, padded, width), F32), full),
            (sds((all_rows, width), BF), whole((all_rows, width))),
            (sds((all_rows, width), BF), whole((all_rows, width))),
            (sds((all_rows, hidden), BF), columns(all_rows)),
            (sds((all_rows, hidden), BF), columns(all_rows)),
            (sds((half, padded, width), BF), whole((half, padded, width))),
            (sds((half, padded, width), BF), whole((half, padded, width))),
            (sds((1, width), F32), whole((1, width))),
            (sds((1, hidden), F32), columns(1)),
        ],
        [
            pltpu.VMEM((padded, width), F32),
            pltpu.VMEM((crops_slots, width), F32),
            pltpu.VMEM((all_rows, width), F32),
        ],
        2,
        (
            ids, crop_size, xf0, xf1, a0, a1, b0, b1, g0, g1, *crop_terms, proj_bias, mlp_gain, mlp_shift,
            hidden_weight, hidden_bias.reshape(1, hidden), output_weight,
        ),
        "hidden",
        6 * all_rows * hidden * width,
        34,
    )
    near_other = swap(gh2_near, "tensor", half)

    chunks_step = chunks // hidden_steps
    wide = min(hidden, width)
    n1, n2 = width // chunks, hidden // chunks
    rows_a = (n1 * hidden + n2 * width) // wide
    chunk_a = whole((pairs, rows_a, wide))
    keep_a, send_a = call(
        functools.partial(hidden_grad_kernel, (chunks, chunks_step, wide, orders_a)),
        (hidden_steps,),
        [
            whole((all_rows, width)),
            whole((all_rows, width)),
            pl.BlockSpec((all_rows, hidden_step), lambda i, s: (0, i)),
            pl.BlockSpec((all_rows, hidden_step), lambda i, s: (0, i)),
        ],
        [
            (sds((pairs, rows_a, wide), BF), chunk_a),
            (sds((pairs, rows_a, wide), BF), chunk_a),
        ],
        [pltpu.VMEM((width, all_rows), BF)],
        1,
        (ids, h2, gz, m, gu),
        "hidden_grads",
        4 * all_rows * hidden * width,
        30,
    )
    if parts > 2:
        e_all, f_all = sum_halves(jnp.concatenate([gh2_near, gh2_far]), "tensor")
        gh2_near, gh2_far = e_all[:half], e_all[half:]
        near_other, far_other = f_all[:half], f_all[half:]
    else:
        far_other = swap(tie(gh2_far, near_other), "tensor", half)
    core_a = swap(tie(send_a, near_other), "dp", 1)

    n_b = 4 * inner // chunks
    chunk_b = whole((pairs, n_b, width))

    def attend_back(first, e0, e1, xf, qkv, pt, ids):
        dims = (first, rows, padded, heads, head_size, crops, unroll)
        at = lambda a, b: pl.BlockSpec((1, a, b), lambda i, *_: (first + i, 0, 0))
        return call(
            functools.partial(attend_back_kernel, dims),
            (half,),
            [
                at(padded, width),
                at(padded, width),
                block3(padded, width),
                block3(padded, width),
                vector,
                block3(padded, width),
                block3(3 * inner, padded),
                pl.BlockSpec((1, heads, padded, padded), lambda i, *_: (i, 0, 0, 0)),
                whole(wp.shape),
                whole(w_t.shape),
            ],
            [
                (sds((half, padded, width), F32), block3(padded, width)),
                (sds((half, padded, width), BF), block3(padded, width)),
                (sds((half, padded, width), BF), block3(padded, width)),
                (sds((half, 3 * inner, padded), BF), block3(3 * inner, padded)),
                (sds((8, width), F32), whole((8, width))),
                (sds((8, 3 * inner), F32), whole((8, 3 * inner))),
                (sds((heads * SLOTS, LANES), F32), whole((heads * SLOTS, LANES))),
            ],
            [pltpu.VMEM((inner, padded), BF), pltpu.VMEM((heads * SLOTS, padded), F32)],
            2,
            (ids, crop_size, y1, gy, e0, e1, mlp_gain, xf, qkv, pt, wp, w_t),
            "attend_back",
            2 * all_rows * 4 * inner * width,
            22,
        )

    z_part = call(
        functools.partial(share_kernel, parts, padded),
        (hidden_steps,),
        [
            pl.BlockSpec((all_rows, hidden_step), lambda i: (0, i)),
            pl.BlockSpec((hidden_step, width), lambda i: (i, 0)),
        ],
        [(sds((parts, padded, width), BF), full)],
        [pltpu.VMEM((all_rows, width), F32)],
        0,
        (tie(m, keep_a), output_weight),
        "share",
        2 * all_rows * hidden * width,
        16,
    )[0]
    kept_a, sent_a = add_halves(tie(keep_a, z_part), tie(core_a, z_part))
    other_a = mixed_swap(sent_a, list(zip(*orders_a))[0])
    _, gh1_far, ga1, gq1, sums1, qb1, tt1 = attend_back(
        half, gh2_far, near_other, xf1, qkv1, pt1, tie(ids, sent_a)
    )
    gh1_far, far_other = lax.optimization_barrier((gh1_far, far_other))
    z0, z1 = scatter_halves(tie(z_part, gh1_far), "tensor")
    g_own, gh1_near, ga0, gq0, sums0, qb0, tt0 = attend_back(
        0, gh2_near, far_other, xf0, qkv0, pt0, tie(ids, gh1_far)
    )
    small_rows = 6 + -(-3 * inner // width) + -(-hidden // width) + -(-heads // (width // (2 * LANES)))
    small_rows = -(-small_rows // 8) * 8
    args = (ot0, ot1, ga0, ga1, gq0, gq1, h1_0, h1_1, sums0, sums1, qb0, qb1, tt0, tt1, ob, hb)
    keep_b, send_b, small = call(
        functools.partial(attend_grad_kernel, (parts, heads, chunks, orders_b)),
        (1,),
        [whole(v.shape) for v in args],
        [
            (sds((pairs, n_b, width), BF), chunk_b),
            (sds((pairs, n_b, width), BF), chunk_b),
            (sds((small_rows, width), F32), whole((small_rows, width))),
        ],
        [pltpu.VMEM((inner, width), F32), pltpu.VMEM((3 * inner, width), F32)],
        1,
        (tie(ids, other_a, z1), *args),
        "attend_grads",
        2 * all_rows * 4 * inner * width,
        30,
    )

    one = whole((1, padded, width))

    def places_of(orders):
        spots = pair_spots(jnp.arange(pairs, dtype=jnp.int32), dp_rank & (chunks - 1), orders)
        return jnp.concatenate([(dp_rank & 1)[None], *spots]).astype(jnp.int32)

    def all_sum(kept, other, orders, begin, cuts):
        stages = list(zip(*orders))
        for stage in stages[begin:-1]:
            kept, sent = add_halves(kept, other)
            kept, other = yield kept, mixed_swap(sent, stage)
        held = add_low(kept, other)
        for bits in [stages[-1], *[(bit, bit) for bit in rest_bits]]:
            size = held.shape[0] // cuts
            pieces = [held[i * size : (i + 1) * size] for i in range(cuts)]
            for i in range(cuts):
                pieces[i], pieces[i + 1 :], other = yield (
                    pieces[i],
                    pieces[i + 1 :],
                    mixed_swap(pieces[i], bits),
                )
                pieces[i] = add_low(pieces[i], other)
            held = jnp.concatenate(pieces, axis=0) if cuts > 1 else pieces[0]
        for stage in stages[-2::-1]:
            held = jnp.concatenate((yield held, mixed_swap(held, stage)), axis=0)
        return held, swap(held, "dp", 1)

    def hidden_sum():
        kept, other = yield kept_a, other_a
        held, other = yield from all_sum(kept, other, orders_a, 1, 2)
        group = 2 - pairs % 2
        layout = (
            (0, 0, pairs, 0, n1, hidden // wide),
            (1, 0, pairs, rows_a - n2 * width // wide, n2, width // wide),
        )
        outs = [
            (sds((width, hidden), F32), pl.BlockSpec((2 * group * n1, hidden), lambda i, s: (i, 0))),
            (sds((hidden, width), F32), pl.BlockSpec((2 * group * n2, width), lambda i, s: (i, 0))),
        ]
        return (yield unpack(places_of(orders_a), held, other, layout, group, outs, "unpack_hidden"))

    def attend_sum():
        kept, sent = yield keep_b, send_b
        kept, other = yield kept, swap(sent, "dp", 1)
        held, other = yield from all_sum(kept, other, orders_b, 0, 1)
        edge = inner // (2 * n_b)
        group = 2 - edge % 2
        edge = edge // group
        layout = ((0, 0, edge, 0, n_b, 1), (1, edge, pairs, 0, n_b, 1))
        shape = (2 * group * n_b, width)
        early = pl.BlockSpec(shape, lambda i, s: (jnp.minimum(i, edge - 1), 0))
        late = pl.BlockSpec(shape, lambda i, s: (jnp.maximum(i - edge, 0), 0))
        outs = [(sds((inner, width), F32), early), (sds((3 * inner, width), F32), late)]
        return unpack(places_of(orders_b), held, other, layout, group, outs, "unpack_attend")

    def patch():
        yield ()
        near, far = gh1_near, gh1_far
        if half > 1:
            near, far = yield near, swap(far, "tensor", half)
            near, far = scatter_halves(add_low(near, far), "tensor", half)
        else:
            far = swap(far, "tensor", 1)
        near, far = yield near, far
        return (yield call(
            functools.partial(patch_grad_kernel, rows),
            (1,),
            [one, one, one, one, vector],
            [(sds((rows, width), F32), whole((rows, width)))],
            [],
            0,
            (g_own, near, far, xf0, attn_gain),
            "patch_grads",
            0,
            24,
        )[0])

    def head():
        own, other, held = yield z0, z1, small
        block_out, pooled = call(
            functools.partial(result_kernel, (rows, padded, crops)),
            (1,),
            [one, one, one, vector],
            [
                (sds((rows, width), BF), whole((rows, width))),
                (sds((1, slots, width), BF), whole((1, slots, width))),
            ],
            [],
            2,
            (ids, crop_size, y1, own, other, output_bias),
            "result",
            0,
            24,
        )
        steps = [[b * parts] for b in bits_of(groups)[:0:-1]]
        steps += [[1, parts]] if parts == 2 else [[b] for b in [*bits_of(parts), parts]]
        weights = [weight for step in steps for weight in step]
        pooled = pooled[0]
        first = lax.broadcasted_iota(jnp.int32, (small_rows, 1), 0) < 2
        for step in steps:
            count = pooled.shape[0]
            high = lax.reduce_precision(held, 8, 7)
            payload = jnp.concatenate([pooled, high.astype(BF), (held - high).astype(BF)], axis=0)
            moves = [sum(w for k, w in enumerate(step) if i >> k & 1) for i in range(1, 2 ** len(step))]
            pooled, held, *others = yield (
                pooled,
                held,
                *[swap(payload, ("dp", "tensor"), move) for move in moves],
            )
            for move, other in zip(moves, others):
                high = other[count : count + small_rows].astype(F32)
                part = high + other[count + small_rows :].astype(F32)
                held = held + (jnp.where(first, part, 0.0) if move % parts else part)
            pooled = jnp.concatenate([pooled, *[other[:count] for other in others]], axis=0)
        step_spec = pl.BlockSpec((proto_step, width), lambda i, s: (i, 0))
        prototype_grad = call(
            functools.partial(proto_grad_kernel, (crops, slots, weights)),
            (protos // proto_step,),
            [
                pl.BlockSpec((score_grad.shape[0], proto_step), lambda i, s: (0, i)),
                whole(pooled.shape),
                step_spec,
                pl.BlockSpec((1, proto_step), lambda i, s: (0, i)),
            ],
            [(sds((protos, width), F32), step_spec)],
            [pltpu.VMEM((score_grad.shape[0], width), BF)],
            1,
            (ids, score_grad, pooled, prototypes, frozen.reshape(1, protos)),
            "proto_grads",
            2 * score_grad.shape[0] * protos * width,
            40,
        )[0]
        finished = call(
            functools.partial(finish_kernel, (heads, head_size, hidden)),
            (1,),
            [whole(held.shape)],
            [
                *[(sds((width,), F32), whole((width,)))] * 6,
                (sds((heads, 2 * head_size), F32), whole((heads, 2 * head_size))),
                (sds(rel_table.shape, F32), whole(rel_table.shape)),
                (sds((hidden,), F32), whole((hidden,))),
            ],
            [],
            0,
            (held,),
            "finish",
            0,
            8,
        )
        prototype_grad, finished = yield prototype_grad, finished
        return block_out, prototype_grad, finished

    threads = {"A": hidden_sum(), "B": attend_sum(), "H": head(), "P": patch()}
    done = rounds(threads)
    out_w1, out_w2 = done["A"]
    proj_weight_grad, qkv_weight_grad = done["B"]
    block_out, prototype_grad, (*small, qb, rel, hb) = done["H"]
    return (
        block_out,
        done["P"],
        small[0],
        small[1],
        jnp.transpose(qkv_weight_grad.reshape(heads, 3 * head_size, width), (2, 0, 1)),
        qb,
        rel,
        proj_weight_grad.reshape(heads, head_size, width),
        small[4],
        small[2],
        small[3],
        out_w1,
        hb,
        out_w2,
        small[5],
        prototype_grad,
    )


def solution(mesh):
    both = ("dp", "tensor")
    return jax.shard_map(
        per_device,
        mesh=mesh,
        in_specs=(
            P(both, None),
            P(both, None),
            P(None, both),
            P("dp"),
            P(both),
            P(),
            P(),
            P(None, "tensor", None),
            P("tensor", None),
            P("tensor", None),
            P("tensor", None, None),
            P(),
            P(),
            P(),
            P(None, "tensor"),
            P("tensor"),
            P("tensor", None),
            P(),
            P(both, None),
        ),
        out_specs=(
            P(both, None),
            P(both, None),
            P(),
            P(),
            P(None, "tensor", None),
            P("tensor", None),
            P("tensor", None),
            P("tensor", None, None),
            P(),
            P(),
            P(),
            P(None, "tensor"),
            P("tensor"),
            P("tensor", None),
            P(),
            P(both, None),
        ),
        check_vma=False,
    )
```

time: 3070 us -> 179 us (0.06); the launches traced: 3030 us -> 179 us
  local copies, waits for them, and re-layouts: 2420 us -> 5.48 us
  waiting for transfers between devices: 272 us -> 71.8 us
  blocking collectives: 186 us -> 0 us
  matrix products: 90.8 us -> 0 us
  Pallas kernels: 0 us -> 58.2 us
  other arithmetic: 33.8 us -> 2.73 us
    gather x4 -> x0, local copies, waits for them, and re-layouts: 2180 us -> none  [block_scores(): rel_bias = bias_table[:, query_place[:, None], key_place[None, :]]]
    unnamed x10 -> x0, waiting for transfers between devices: 272 us -> none
    concatenate x3 -> x4, local copies, waits for them, and re-layouts: 113 us -> 0.18 us  [all_sum(): held = jnp.concatenate((yield (held, mixed_swap(held, stage))), axis=0)]
    all_gather x5 -> x0, blocking collectives: 109 us -> none  [the longest x1 78.1 us: per_device(): all_pooled = lax.all_gather(pooled, ('dp', 'tensor'), axis=0, tiled=True)]
    dot_general x26 -> x0, matrix products: 90.8 us -> none  [the longest x1 9.63 us: attend_back(): jnp.einsum('qhd,khd->hqk', out_grads, window[:, :, 2 * head_size:], prefe...]
    ppermute x0 -> x35, waiting for transfers between devices: none -> 71.8 us  [the longest x24 42.4 us: swap(): return lax.ppermute(v, axis, partner(axis, bit))]
    pallas_call x0 -> x16, Pallas kernels: none -> 58.2 us  [call(): pl.pallas_call(body, grid_spec=pltpu.PrefetchScalarGridSpec(num_scalar_pr...]
    unnamed x96 -> x46, local copies, waits for them, and re-layouts: 56.1 us -> 5.16 us
  transfers between devices with their start and end apart: 7 -> 35, of which waited for: 2 -> 25; matrix products, arithmetic and copies ran while one was open for 3% -> 1% of each run, Pallas kernels for 0% -> 27%
where the time goes in v1:
time: 179 us
  waiting for transfers between devices  71.8 us (40%)
  Pallas kernels  58.2 us (33%)
  starting transfers between devices  39.6 us (22%)
  local copies, waits for them, and re-layouts  5.48 us (3%)
  other arithmetic  2.73 us (2%)
    pallas_call x16, Pallas kernels, call(): pl.pallas_call(body, grid_spec=pltpu.PrefetchScalarGridSpec(num_scalar_pr...  58.2 us
    ppermute x24, waiting for transfers between devices, swap(): return lax.ppermute(v, axis, partner(axis, bit))  42.4 us
    ppermute x11, waiting for transfers between devices, mixed_swap(): return lax.ppermute(v, 'dp', [(i, i ^ bits[i & 1]) for i in range(size)])  29.4 us
    ppermute x24, starting transfers between devices, swap(): return lax.ppermute(v, axis, partner(axis, bit))  25.8 us
    ppermute x11, starting transfers between devices, mixed_swap(): return lax.ppermute(v, 'dp', [(i, i ^ bits[i & 1]) for i in range(size)])  13.8 us
    unnamed x46, local copies, waits for them, and re-layouts  5.16 us
  transfers between devices with their start and end apart: 35, of which 25 were waited for; matrix products, arithmetic and copies ran while one was open for 1% of the time, Pallas kernels for 27%

profile of v1, /device:TPU:0, one launch (start us, length us, event | category | flops | bytes accessed | tf_op | source)
XLA Modules:
  0.0 179.1 jit_solution(8880556027979893201)
XLA Ops:
  0.6 3.0 %collective-permute-start = (bf16[1,170,768]{2,1,0:T(8,128)(2,1)}, bf16[1,170,768]{2,1,0:T(8,128)(2,1)S(1)}, u32[]{:S(2)}, u32[]{:S(2)}) collective-permute-start(bf16[1,170,768]{2,1,0:T(8,128)(2,1)} %bitcast.24), channel_id=1, source_target_pairs={{0,1},{1,0},{2,3},{3,2},{4,5},{5,4},{6,7},{7,6},{8,9},{9,8},{10,11... | collective-permute-start | bytes 783368 | tf_op jit(solution)/shard_map/ppermute | solution.py:555
  9.3 3.4 %crop_grads.1 = (f32[8,24,768]{2,1,0:T(8,128)S(1)}, f32[8,24,768]{2,1,0:T(8,128)S(1)}) custom-call(s32[3]{0:T(128)S(1)} %pad_add_fusion.ids, bf16[320,2048]{1,0:T(8,128)(2,1)S(1)} %copy-done.5, bf16[2048,768]{1,0:T(8,128)(2,1)S(1)} %copy-done.1), custom_call_target="tpu_custom_call" | custom-call | flops 10066329 | bytes 56361 | tf_op jit(solution)/shard_map/crop_grads/pallas_call | solution.py:82
  12.9 5.3 %attend.2 = (bf16[1,176,768]{2,1,0:T(8,128)(2,1)S(1)}, bf16[1,176,768]{2,1,0:T(8,128)(2,1)S(1)}, bf16[1,1152,176]{2,1,0:T(8,128)(2,1)S(1)}, bf16[1,12,176,176]{3...) custom-call(s32[3]{0:T(128)S(1)} %pad_add_fusion.ids, s32[20]{0:T(128)S(1)} %copy-done.13, ...), custom_call_target="tpu_custom_call" | custom-call | flops 4152360 | bytes 53146 | tf_op jit(solution)/shard_map/attend/pallas_call | solution.py:82
  18.2 3.4 %collective-permute-done.1.g1 = bf16[1,170,768]{2,1,0:T(8,128)(2,1)S(1)} collective-permute-done((bf16[1,170,768]{2,1,0:T(8,128)(2,1)S(1)}, bf16[1,170,768]{2,1,0:T(8,128)(2,1)S(1)}, u32[]{:S(2)}, u32[]{:S(2)}) %collective-permute-start.1) | collective-permute-done | bytes 261152 | tf_op jit(solution)/shard_map/ppermute | solution.py:555
  23.8 5.3 %attend.3 = (bf16[1,176,768]{2,1,0:T(8,128)(2,1)S(1)}, bf16[1,176,768]{2,1,0:T(8,128)(2,1)S(1)}, bf16[1,1152,176]{2,1,0:T(8,128)(2,1)S(1)}, bf16[1,12,176,176]{3...) custom-call(s32[3]{0:T(128)S(1)} %pad_add_fusion.ids, s32[20]{0:T(128)S(1)} %copy-done.13, ...), custom_call_target="tpu_custom_call" | custom-call | flops 4152360 | bytes 53146 | tf_op jit(solution)/shard_map/attend/pallas_call | solution.py:82
  32.6 3.1 %collective-permute-done.6 = f32[2,24,768]{2,1,0:T(8,128)S(1)} collective-permute-done((f32[2,24,768]{2,1,0:T(8,128)S(1)}, f32[2,24,768]{2,1,0:T(8,128)S(1)}, u32[]{:S(2)}, u32[]{:S(2)}) %collective-permute-start.6) | collective-permute-done | bytes 147488 | tf_op jit(solution)/shard_map/ppermute | solution.py:555
  35.7 2.6 %collective-permute-start.9 = (f32[1,24,768]{2,1,0:T(8,128)S(1)}, f32[1,24,768]{2,1,0:T(8,128)S(1)}, u32[]{:S(2)}, u32[]{:S(2)}) collective-permute-start(f32[1,24,768]{2,1,0:T(8,128)S(1)} %get-tuple-element.320), channel_id=1, source_target_pairs={{0,17},{1,16},{2,19},{3,18},{4,21},{5,20},{6,23},{7,22},{8,25},{9,... | collective-permute-start | bytes 221192 | tf_op jit(solution)/shard_map/ppermute | solution.py:555
  40.5 2.9 %collective-permute-done.9.rest_3_ = f32[1,24,768]{2,1,0:T(8,128)S(1)} collective-permute-done((f32[1,24,768]{2,1,0:T(8,128)S(1)}, f32[1,24,768]{2,1,0:T(8,128)S(1)}, u32[]{:S(2)}, u32[]{:S(2)}) %collective-permute-start.9) | collective-permute-done | bytes 73760 | tf_op jit(solution)/shard_map/ppermute | solution.py:555
  43.5 5.3 %hidden.1 = (f32[2,176,768]{2,1,0:T(8,128)S(1)}, f32[2,176,768]{2,1,0:T(8,128)S(1)}, bf16[352,768]{1,0:T(8,128)(2,1)S(1)}, bf16[352,768]{1,0:T(8,128)(2,1)S(1)},...) custom-call(s32[3]{0:T(128)S(1)} %pad_add_fusion.ids, ...), custom_call_target="tpu_custom_call" | custom-call | flops 24914164 | bytes 131298 | tf_op jit(solution)/shard_map/hidden/pallas_call | solution.py:82
  50.4 3.8 %hidden_grads.1 = (bf16[8,192,768]{2,1,0:T(8,128)(2,1)S(1)}, bf16[8,192,768]{2,1,0:T(8,128)(2,1)S(1)}) custom-call(s32[3]{0:T(128)S(1)} %pad_add_fusion.ids, bf16[352,768]{1,0:T(8,128)(2,1)S(1)} %get-tuple-element.178.h2, bf16[352,768]{1,0:T(8,128)(2,1)S(1)} %get-tuple-element.179.gz, bf16[352,1536]{1,0:T(8,128)(2,1)S(1)} %get-tuple-element.183.m, ...), custom_call_target="tpu_custom_call" | custom-call | flops 16609443 | bytes 79626 | tf_op jit(solution)/shard_map/hidden_grads/pallas_call | solution.py:82
  57.0 2.9 %collective-permute-done.11 = bf16[8,192,768]{2,1,0:T(8,128)(2,1)S(1)} collective-permute-done((bf16[8,192,768]{2,1,0:T(8,128)(2,1)S(1)}, bf16[8,192,768]{2,1,0:T(8,128)(2,1)S(1)}, u32[]{:S(2)}, u32[]{:S(2)}) %collective-permute-start.11) | collective-permute-done | bytes 2359328 | tf_op jit(solution)/shard_map/ppermute | solution.py:555
  63.6 5.8 %attend_back.2 = (f32[1,176,768]{2,1,0:T(8,128)}, bf16[1,176,768]{2,1,0:T(8,128)(2,1)S(1)}, bf16[1,176,768]{2,1,0:T(8,128)(2,1)S(1)}, bf16[1,1152,176]{2,1,0:T(8...) custom-call(s32[3]{0:T(128)S(1)} %pad_add_fusion.ids, s32[20]{0:T(128)S(1)} %copy-done.13, ...), custom_call_target="tpu_custom_call" | custom-call | flops 8304721 | bytes 86231 | tf_op jit(solution)/shard_map/attend_back/pallas_call | solution.py:82
  72.1 5.4 %attend_back.3 = (f32[1,176,768]{2,1,0:T(8,128)S(1)}, bf16[1,176,768]{2,1,0:T(8,128)(2,1)S(1)}, bf16[1,176,768]{2,1,0:T(8,128)(2,1)S(1)}, bf16[1,1152,176]{2,1,0...) custom-call(s32[3]{0:T(128)S(1)} %pad_add_fusion.ids, s32[20]{0:T(128)S(1)} %copy-done.13, ...), custom_call_target="tpu_custom_call" | custom-call | flops 8304721 | bytes 86231 | tf_op jit(solution)/shard_map/attend_back/pallas_call | solution.py:82
  78.0 2.1 %attend_grads.1 = (bf16[8,96,768]{2,1,0:T(8,128)(2,1)S(1)}, bf16[8,96,768]{2,1,0:T(8,128)(2,1)S(1)}, f32[16,768]{1,0:T(8,128)S(1)}) custom-call(s32[3]{0:T(128)S(1)} %pad_add_fusion.ids, bf16[1,384,176]{2,1,0:T(8,128)(2,1)S(1)} %get-tuple-element.199.o0, bf16[1,384,176]{2,1,0:T(8,128)(2,1)S(1)} %get-tuple-element.200.o1, ...), custom_call_target="tpu_custom_call" | custom-call | flops 8304721 | bytes 58828 | tf_op jit(solution)/shard_map/attend_grads/pallas_call | solution.py:82
  83.9 2.3 %collective-permute-start.17 = (bf16[48,768]{1,0:T(8,128)(2,1)S(1)}, bf16[48,768]{1,0:T(8,128)(2,1)S(1)}, u32[]{:S(2)}, u32[]{:S(2)}) collective-permute-start(bf16[48,768]{1,0:T(8,128)(2,1)S(1)} %pad_maximum_fusion.7), channel_id=1, source_target_pairs={{0,16},{1,17},{2,18},{3,19},{4,20},{5,21},{6,22},{7,23},{8,24},{9,... | collective-permute-start | bytes 221192 | tf_op jit(solution)/shard_map/ppermute | solution.py:555
  86.2 2.8 %collective-permute-done.18.e1 = bf16[1,176,768]{2,1,0:T(8,128)(2,1)S(1)} collective-permute-done((bf16[1,176,768]{2,1,0:T(8,128)(2,1)S(1)}, bf16[1,176,768]{2,1,0:T(8,128)(2,1)S(1)}, u32[]{:S(2)}, u32[]{:S(2)}) %collective-permute-start.18) | collective-permute-done | bytes 270368 | tf_op jit(solution)/shard_map/ppermute | solution.py:555
  92.2 2.9 %collective-permute-start.19 = (bf16[1,192,768]{2,1,0:T(8,128)(2,1)S(1)}, bf16[1,192,768]{2,1,0:T(8,128)(2,1)S(1)}, u32[]{:S(2)}, u32[]{:S(2)}) collective-permute-start(bf16[1,192,768]{2,1,0:T(8,128)(2,1)S(1)} %get-tuple-element.243), channel_id=1, source_target_pairs={{0,16},{2,18},{4,20},{6,22},{8,24},{10,26},{12,28},{14,30},{16,0},... | collective-permute-start | bytes 884744 | tf_op jit(solution)/shard_map/ppermute | solution.py:599
  99.5 5.8 %collective-permute-done.21 = bf16[64,768]{1,0:T(8,128)(2,1)S(1)} collective-permute-done((bf16[64,768]{1,0:T(8,128)(2,1)S(1)}, bf16[64,768]{1,0:T(8,128)(2,1)S(1)}, u32[]{:S(2)}, u32[]{:S(2)}) %collective-permute-start.21) | collective-permute-done | bytes 98336 | tf_op jit(solution)/shard_map/ppermute | solution.py:555
  105.3 2.3 %collective-permute-done.19 = bf16[1,192,768]{2,1,0:T(8,128)(2,1)S(1)} collective-permute-done((bf16[1,192,768]{2,1,0:T(8,128)(2,1)S(1)}, bf16[1,192,768]{2,1,0:T(8,128)(2,1)S(1)}, u32[]{:S(2)}, u32[]{:S(2)}) %collective-permute-start.19) | collective-permute-done | bytes 294944 | tf_op jit(solution)/shard_map/ppermute | solution.py:599
  108.9 1.9 %collective-permute-start.22 = (bf16[1,192,768]{2,1,0:T(8,128)(2,1)S(1)}, bf16[1,192,768]{2,1,0:T(8,128)(2,1)S(1)}, u32[]{:S(2)}, u32[]{:S(2)}) collective-permute-start(bf16[1,192,768]{2,1,0:T(8,128)(2,1)S(1)} %get-tuple-element.251), channel_id=1, source_target_pairs={{0,16},{2,18},{4,20},{6,22},{8,24},{10,26},{12,28},{14,30},{16,0},... | collective-permute-start | bytes 884744 | tf_op jit(solution)/shard_map/ppermute | solution.py:599
  112.9 12.8 %collective-permute-done.22 = bf16[1,192,768]{2,1,0:T(8,128)(2,1)S(1)} collective-permute-done((bf16[1,192,768]{2,1,0:T(8,128)(2,1)S(1)}, bf16[1,192,768]{2,1,0:T(8,128)(2,1)S(1)}, u32[]{:S(2)}, u32[]{:S(2)}) %collective-permute-start.22) | collective-permute-done | bytes 294944 | tf_op jit(solution)/shard_map/ppermute | solution.py:599
  126.2 3.4 %collective-permute-start.25 = (bf16[2,192,768]{2,1,0:T(8,128)(2,1)S(1)}, bf16[2,192,768]{2,1,0:T(8,128)(2,1)S(1)}, u32[]{:S(2)}, u32[]{:S(2)}) collective-permute-start(bf16[2,192,768]{2,1,0:T(8,128)(2,1)S(1)} %pad_maximum_fusion.1), channel_id=1, source_target_pairs={{0,8},{2,6},{4,12},{6,2},{8,0},{10,14},{12,4},{14,10},{16,24},{18,... | collective-permute-start | bytes 1769480 | tf_op jit(solution)/shard_map/ppermute | solution.py:599
  129.8 2.0 %collective-permute-start.27 = (bf16[160,768]{1,0:T(8,128)(2,1)S(1)}, bf16[160,768]{1,0:T(8,128)(2,1)S(1)}, u32[]{:S(2)}, u32[]{:S(2)}) collective-permute-start(bf16[160,768]{1,0:T(8,128)(2,1)S(1)} %pad_maximum_fusion.2), channel_id=1, source_target_pairs={{0,1},{1,0},{2,3},{3,2},{4,5},{5,4},{6,7},{7,6},{8,9},{9,8},{10,11... | collective-permute-start | bytes 737288 | tf_op jit(solution)/shard_map/ppermute | solution.py:555
  131.9 6.2 %collective-permute-done.29 = bf16[160,768]{1,0:T(8,128)(2,1)S(1)} collective-permute-done((bf16[160,768]{1,0:T(8,128)(2,1)S(1)}, bf16[160,768]{1,0:T(8,128)(2,1)S(1)}, u32[]{:S(2)}, u32[]{:S(2)}) %collective-permute-start.29) | collective-permute-done | bytes 245792 | tf_op jit(solution)/shard_map/ppermute | solution.py:555
  138.0 2.5 %collective-permute-done.27 = bf16[160,768]{1,0:T(8,128)(2,1)S(1)} collective-permute-done((bf16[160,768]{1,0:T(8,128)(2,1)S(1)}, bf16[160,768]{1,0:T(8,128)(2,1)S(1)}, u32[]{:S(2)}, u32[]{:S(2)}) %collective-permute-start.27) | collective-permute-done | bytes 245792 | tf_op jit(solution)/shard_map/ppermute | solution.py:555
  146.5 5.9 %proto_grads.1 = f32[2048,768]{1,0:T(8,128)} custom-call(s32[3]{0:T(128)S(1)} %pad_add_fusion.ids, bf16[320,2048]{1,0:T(8,128)(2,1)S(1)} %copy-done.6, bf16[512,768]{1,0:T(8,128)(2,1)S(1)} %pad_maximum_fusion.pooled, bf16[2048,768]{1,0:T(8,128)(2,1)S(1)} %copy-done.2, s32[1,2048]{1,0:T(1,128)S(1)} %bitcast.31), custom_call_target="tpu_custom_call" | custom-call | flops 10066329 | bytes 115425 | tf_op jit(solution)/shard_map/proto_grads/pallas_call | solution.py:82
  152.4 2.2 %collective-permute-done.31 = bf16[2,96,768]{2,1,0:T(8,128)(2,1)S(1)} collective-permute-done((bf16[2,96,768]{2,1,0:T(8,128)(2,1)S(1)}, bf16[2,96,768]{2,1,0:T(8,128)(2,1)S(1)}, u32[]{:S(2)}, u32[]{:S(2)}) %collective-permute-start.31) | collective-permute-done | bytes 294944 | tf_op jit(solution)/shard_map/ppermute | solution.py:599
  154.6 7.1 %collective-permute-done.30 = bf16[4,192,768]{2,1,0:T(8,128)(2,1)S(1)} collective-permute-done((bf16[4,192,768]{2,1,0:T(8,128)(2,1)S(1)}, bf16[4,192,768]{2,1,0:T(8,128)(2,1)S(1)}, u32[]{:S(2)}, u32[]{:S(2)}) %collective-permute-start.30) | collective-permute-done | bytes 1179680 | tf_op jit(solution)/shard_map/ppermute | solution.py:599
  162.6 4.1 %collective-permute-done.32.other = bf16[8,192,768]{2,1,0:T(8,128)(2,1)} collective-permute-done((bf16[8,192,768]{2,1,0:T(8,128)(2,1)S(1)}, bf16[8,192,768]{2,1,0:T(8,128)(2,1)}, u32[]{:S(2)}, u32[]{:S(2)}) %collective-permute-start.32) | collective-permute-done | bytes 2359328 | tf_op jit(solution)/shard_map/ppermute | solution.py:555
  166.6 6.1 %unpack_hidden.1 = (f32[768,1536]{1,0:T(8,128)}, f32[1536,768]{1,0:T(8,128)}) custom-call(s32[17]{0:T(128)S(1)} %pad_add_fusion.1.places, bf16[8,192,768]{2,1,0:T(8,128)(2,1)S(1)} %constant_dynamic-update-slice_fusion.2.own, bf16[8,192,768]{2,1,0:T(8,128)(2,1)} %collective-permute-done.32.other), custom_call_target="tpu_custom_call" | custom-call | bytes 141558 | tf_op jit(solution)/shard_map/unpack_hidden/pallas_call | solution.py:82
  173.0 2.7 %collective-permute-done.34.other = bf16[8,96,768]{2,1,0:T(8,128)(2,1)S(1)} collective-permute-done((bf16[8,96,768]{2,1,0:T(8,128)(2,1)S(1)}, bf16[8,96,768]{2,1,0:T(8,128)(2,1)S(1)}, u32[]{:S(2)}, u32[]{:S(2)}) %collective-permute-start.34) | collective-permute-done | bytes 1179680 | tf_op jit(solution)/shard_map/ppermute | solution.py:555
  175.8 3.3 %unpack_attend.1 = (f32[384,768]{1,0:T(8,128)}, f32[1152,768]{1,0:T(8,128)}) custom-call(s32[17]{0:T(128)S(1)} %pad_add_fusion.1.places, bf16[8,96,768]{2,1,0:T(8,128)(2,1)S(1)} %constant_dynamic-update-slice_fusion.6.own, bf16[8,96,768]{2,1,0:T(8,128)(2,1)S(1)} %collective-permute-done.34.other), custom_call_target="tpu_custom_call" | custom-call | bytes 70779 | tf_op jit(solution)/shard_map/unpack_attend/pallas_call | solution.py:82
  (146 shorter events, 47.3 us)
Async XLA Ops:
  0.6 12.0 %collective-permute-start = (bf16[1,170,768]{2,1,0:T(8,128)(2,1)}, bf16[1,170,768]{2,1,0:T(8,128)(2,1)S(1)}, u32[]{:S(2)}, u32[]{:S(2)}) collective-permute-start(bf16[1,170,768]{2,1,0:T(8,128)(2,1)} %bitcast.24), channel_id=1, source_target_pairs={{0,1},{1,0},{2,3},{3,2},{4,5},{5,4},{6,7},{7,6},{8,9},{9,8},{10,11... | collective-permute-start | bytes 783368 | tf_op jit(solution)/shard_map/ppermute | solution.py:555
  12.7 9.0 %collective-permute-start.2 = (f32[8,24,768]{2,1,0:T(8,128)S(1)}, f32[8,24,768]{2,1,0:T(8,128)S(1)}, u32[]{:S(2)}, u32[]{:S(2)}) collective-permute-start(f32[8,24,768]{2,1,0:T(8,128)S(1)} %get-tuple-element.166), channel_id=1, source_target_pairs={{0,2},{2,0},{4,6},{6,4},{8,10},{10,8},{12,14},{14,12},{16,18},{18,... | collective-permute-start | bytes 1769480 | tf_op jit(solution)/shard_map/ppermute | solution.py:555
  12.8 8.9 %collective-permute-start.1 = (bf16[1,170,768]{2,1,0:T(8,128)(2,1)S(1)}, bf16[1,170,768]{2,1,0:T(8,128)(2,1)S(1)}, u32[]{:S(2)}, u32[]{:S(2)}) collective-permute-start(bf16[1,170,768]{2,1,0:T(8,128)(2,1)S(1)} %bitcast.26), channel_id=1, source_target_pairs={{0,1},{1,0},{2,3},{3,2},{4,5},{5,4},{6,7},{7,6},{8,9},{9,8},{10,11... | collective-permute-start | bytes 783368 | tf_op jit(solution)/shard_map/ppermute | solution.py:555
  21.7 8.6 %collective-permute-start.5 = (f32[4,24,768]{2,1,0:T(8,128)S(1)}, f32[4,24,768]{2,1,0:T(8,128)S(1)}, u32[]{:S(2)}, u32[]{:S(2)}) collective-permute-start(f32[4,24,768]{2,1,0:T(8,128)S(1)} %get-tuple-element.312), channel_id=1, source_target_pairs={{0,4},{2,6},{4,0},{6,2},{8,12},{10,14},{12,8},{14,10},{16,20},{18,... | collective-permute-start | bytes 884744 | tf_op jit(solution)/shard_map/ppermute | solution.py:555
  23.3 8.8 %collective-permute-start.3 = (bf16[1,176,768]{2,1,0:T(8,128)(2,1)S(1)}, bf16[1,176,768]{2,1,0:T(8,128)(2,1)S(1)}, u32[]{:S(2)}, u32[]{:S(2)}) collective-permute-start(bf16[1,176,768]{2,1,0:T(8,128)(2,1)S(1)} %get-tuple-element.164.a0), channel_id=1, source_target_pairs={{0,1},{1,0},{2,3},{3,2},{4,5},{5,4},{6,7},{7,6},{8,9},{9,8},{10,11... | collective-permute-start | bytes 811016 | tf_op jit(solution)/shard_map/ppermute | solution.py:555
  30.4 5.2 %collective-permute-start.6 = (f32[2,24,768]{2,1,0:T(8,128)S(1)}, f32[2,24,768]{2,1,0:T(8,128)S(1)}, u32[]{:S(2)}, u32[]{:S(2)}) collective-permute-start(f32[2,24,768]{2,1,0:T(8,128)S(1)} %get-tuple-element.317), channel_id=1, source_target_pairs={{0,8},{2,10},{4,12},{6,14},{8,0},{10,2},{12,4},{14,6},{16,24},{18,... | collective-permute-start | bytes 442376 | tf_op jit(solution)/shard_map/ppermute | solution.py:555
  32.1 8.4 %collective-permute-start.4 = (bf16[1,176,768]{2,1,0:T(8,128)(2,1)S(1)}, bf16[1,176,768]{2,1,0:T(8,128)(2,1)S(1)}, u32[]{:S(2)}, u32[]{:S(2)}) collective-permute-start(bf16[1,176,768]{2,1,0:T(8,128)(2,1)S(1)} %get-tuple-element.172.a1), channel_id=1, source_target_pairs={{0,1},{1,0},{2,3},{3,2},{4,5},{5,4},{6,7},{7,6},{8,9},{9,8},{10,11... | collective-permute-start | bytes 811016 | tf_op jit(solution)/shard_map/ppermute | solution.py:555
  35.7 7.7 %collective-permute-start.9 = (f32[1,24,768]{2,1,0:T(8,128)S(1)}, f32[1,24,768]{2,1,0:T(8,128)S(1)}, u32[]{:S(2)}, u32[]{:S(2)}) collective-permute-start(f32[1,24,768]{2,1,0:T(8,128)S(1)} %get-tuple-element.320), channel_id=1, source_target_pairs={{0,17},{1,16},{2,19},{3,18},{4,21},{5,20},{6,23},{7,22},{8,25},{9,... | collective-permute-start | bytes 221192 | tf_op jit(solution)/shard_map/ppermute | solution.py:555
  38.2 5.3 %collective-permute-start.7 = (f32[1,24,768]{2,1,0:T(8,128)S(1)}, f32[1,24,768]{2,1,0:T(8,128)S(1)}, u32[]{:S(2)}, u32[]{:S(2)}) collective-permute-start(f32[1,24,768]{2,1,0:T(8,128)S(1)} %get-tuple-element.320), channel_id=1, source_target_pairs={{0,16},{1,17},{2,18},{3,19},{4,20},{5,21},{6,22},{7,23},{8,24},{9,... | collective-permute-start | bytes 221192 | tf_op jit(solution)/shard_map/ppermute | solution.py:555
  38.5 5.0 %collective-permute-start.8 = (f32[1,24,768]{2,1,0:T(8,128)S(1)}, f32[1,24,768]{2,1,0:T(8,128)S(1)}, u32[]{:S(2)}, u32[]{:S(2)}) collective-permute-start(f32[1,24,768]{2,1,0:T(8,128)S(1)} %get-tuple-element.321.rest_0_), channel_id=1, source_target_pairs={{0,1},{1,0},{2,3},{3,2},{4,5},{5,4},{6,7},{7,6},{8,9},{9,8},{10,11... | collective-permute-start | bytes 221192 | tf_op jit(solution)/shard_map/ppermute | solution.py:555
  48.8 6.5 %collective-permute-start.10 = (bf16[1,176,768]{2,1,0:T(8,128)(2,1)S(1)}, bf16[1,176,768]{2,1,0:T(8,128)(2,1)S(1)}, u32[]{:S(2)}, u32[]{:S(2)}) collective-permute-start(bf16[1,176,768]{2,1,0:T(8,128)(2,1)S(1)} %get-tuple-element.186.e0), channel_id=1, source_target_pairs={{0,1},{1,0},{2,3},{3,2},{4,5},{5,4},{6,7},{7,6},{8,9},{9,8},{10,11... | collective-permute-start | bytes 811016 | tf_op jit(solution)/shard_map/ppermute | solution.py:555
  60.6 17.5 %collective-permute-start.12 = (bf16[4,192,768]{2,1,0:T(8,128)(2,1)S(1)}, bf16[4,192,768]{2,1,0:T(8,128)(2,1)S(1)}, u32[]{:S(2)}, u32[]{:S(2)}) collective-permute-start(bf16[4,192,768]{2,1,0:T(8,128)(2,1)S(1)} %get-tuple-element.304), channel_id=1, source_target_pairs={{0,4},{2,10},{4,0},{6,14},{8,12},{10,2},{12,8},{14,6},{16,20},{18,... | collective-permute-start | bytes 3538952 | tf_op jit(solution)/shard_map/ppermute | solution.py:599
  62.1 8.3 %collective-permute-start.13 = (bf16[1,176,768]{2,1,0:T(8,128)(2,1)S(1)}, bf16[1,176,768]{2,1,0:T(8,128)(2,1)S(1)}, u32[]{:S(2)}, u32[]{:S(2)}) collective-permute-start(bf16[1,176,768]{2,1,0:T(8,128)(2,1)S(1)} %get-tuple-element.195.e0), channel_id=1, source_target_pairs={{0,1},{1,0},{2,3},{3,2},{4,5},{5,4},{6,7},{7,6},{8,9},{9,8},{10,11... | collective-permute-start | bytes 811016 | tf_op jit(solution)/shard_map/ppermute | solution.py:555
  70.5 7.5 %collective-permute-start.14 = (bf16[1,176,768]{2,1,0:T(8,128)(2,1)S(1)}, bf16[1,176,768]{2,1,0:T(8,128)(2,1)S(1)}, u32[]{:S(2)}, u32[]{:S(2)}) collective-permute-start(bf16[1,176,768]{2,1,0:T(8,128)(2,1)S(1)} %get-tuple-element.319), channel_id=1, source_target_pairs={{0,1},{1,0},{2,3},{3,2},{4,5},{5,4},{6,7},{7,6},{8,9},{9,8},{10,11... | collective-permute-start | bytes 811016 | tf_op jit(solution)/shard_map/ppermute | solution.py:555
  80.1 11.9 %collective-permute-start.16 = (bf16[8,96,768]{2,1,0:T(8,128)(2,1)S(1)}, bf16[8,96,768]{2,1,0:T(8,128)(2,1)S(1)}, u32[]{:S(2)}, u32[]{:S(2)}) collective-permute-start(bf16[8,96,768]{2,1,0:T(8,128)(2,1)S(1)} %get-tuple-element.228), channel_id=1, source_target_pairs={{0,2},{2,0},{4,6},{6,4},{8,10},{10,8},{12,14},{14,12},{16,18},{18,... | collective-permute-start | bytes 3538952 | tf_op jit(solution)/shard_map/ppermute | solution.py:555
  80.5 11.5 %collective-permute-start.15 = (bf16[2,192,768]{2,1,0:T(8,128)(2,1)S(1)}, bf16[2,192,768]{2,1,0:T(8,128)(2,1)S(1)}, u32[]{:S(2)}, u32[]{:S(2)}) collective-permute-start(bf16[2,192,768]{2,1,0:T(8,128)(2,1)S(1)} %get-tuple-element.308), channel_id=1, source_target_pairs={{0,8},{2,6},{4,12},{6,2},{8,0},{10,14},{12,4},{14,10},{16,24},{18,... | collective-permute-start | bytes 1769480 | tf_op jit(solution)/shard_map/ppermute | solution.py:599
  80.9 8.0 %collective-permute-start.18 = (bf16[1,176,768]{2,1,0:T(8,128)(2,1)S(1)}, bf16[1,176,768]{2,1,0:T(8,128)(2,1)S(1)}, u32[]{:S(2)}, u32[]{:S(2)}) collective-permute-start(bf16[1,176,768]{2,1,0:T(8,128)(2,1)S(1)} %get-tuple-element.196), channel_id=1, source_target_pairs={{0,1},{1,0},{2,3},{3,2},{4,5},{5,4},{6,7},{7,6},{8,9},{9,8},{10,11... | collective-permute-start | bytes 811016 | tf_op jit(solution)/shard_map/ppermute | solution.py:555
  83.9 6.4 %collective-permute-start.17 = (bf16[48,768]{1,0:T(8,128)(2,1)S(1)}, bf16[48,768]{1,0:T(8,128)(2,1)S(1)}, u32[]{:S(2)}, u32[]{:S(2)}) collective-permute-start(bf16[48,768]{1,0:T(8,128)(2,1)S(1)} %pad_maximum_fusion.7), channel_id=1, source_target_pairs={{0,16},{1,17},{2,18},{3,19},{4,20},{5,21},{6,22},{7,23},{8,24},{9,... | collective-permute-start | bytes 221192 | tf_op jit(solution)/shard_map/ppermute | solution.py:555
  92.2 15.4 %collective-permute-start.19 = (bf16[1,192,768]{2,1,0:T(8,128)(2,1)S(1)}, bf16[1,192,768]{2,1,0:T(8,128)(2,1)S(1)}, u32[]{:S(2)}, u32[]{:S(2)}) collective-permute-start(bf16[1,192,768]{2,1,0:T(8,128)(2,1)S(1)} %get-tuple-element.243), channel_id=1, source_target_pairs={{0,16},{2,18},{4,20},{6,22},{8,24},{10,26},{12,28},{14,30},{16,0},... | collective-permute-start | bytes 884744 | tf_op jit(solution)/shard_map/ppermute | solution.py:599
  95.5 12.1 %collective-permute-start.20 = (bf16[4,96,768]{2,1,0:T(8,128)(2,1)S(1)}, bf16[4,96,768]{2,1,0:T(8,128)(2,1)S(1)}, u32[]{:S(2)}, u32[]{:S(2)}) collective-permute-start(bf16[4,96,768]{2,1,0:T(8,128)(2,1)S(1)} %get-tuple-element.306), channel_id=1, source_target_pairs={{0,4},{2,10},{4,0},{6,14},{8,12},{10,2},{12,8},{14,6},{16,20},{18,... | collective-permute-start | bytes 1769480 | tf_op jit(solution)/shard_map/ppermute | solution.py:599
  96.6 8.7 %collective-permute-start.21 = (bf16[64,768]{1,0:T(8,128)(2,1)S(1)}, bf16[64,768]{1,0:T(8,128)(2,1)S(1)}, u32[]{:S(2)}, u32[]{:S(2)}) collective-permute-start(bf16[64,768]{1,0:T(8,128)(2,1)S(1)} %pad_maximum_fusion.5), channel_id=1, source_target_pairs={{0,8},{1,9},{2,10},{3,11},{4,12},{5,13},{6,14},{7,15},{8,0},{9,1},... | collective-permute-start | bytes 294920 | tf_op jit(solution)/shard_map/ppermute | solution.py:555
  107.7 5.2 %collective-permute-start.24 = (bf16[96,768]{1,0:T(8,128)(2,1)S(1)}, bf16[96,768]{1,0:T(8,128)(2,1)S(1)}, u32[]{:S(2)}, u32[]{:S(2)}) collective-permute-start(bf16[96,768]{1,0:T(8,128)(2,1)S(1)} %pad_maximum_fusion.4), channel_id=1, source_target_pairs={{0,4},{1,5},{2,6},{3,7},{4,0},{5,1},{6,2},{7,3},{8,12},{9,13},{10,... | collective-permute-start | bytes 442376 | tf_op jit(solution)/shard_map/ppermute | solution.py:555
  108.9 16.7 %collective-permute-start.22 = (bf16[1,192,768]{2,1,0:T(8,128)(2,1)S(1)}, bf16[1,192,768]{2,1,0:T(8,128)(2,1)S(1)}, u32[]{:S(2)}, u32[]{:S(2)}) collective-permute-start(bf16[1,192,768]{2,1,0:T(8,128)(2,1)S(1)} %get-tuple-element.251), channel_id=1, source_target_pairs={{0,16},{2,18},{4,20},{6,22},{8,24},{10,26},{12,28},{14,30},{16,0},... | collective-permute-start | bytes 884744 | tf_op jit(solution)/shard_map/ppermute | solution.py:599
  111.0 14.6 %collective-permute-start.23 = (bf16[2,96,768]{2,1,0:T(8,128)(2,1)S(1)}, bf16[2,96,768]{2,1,0:T(8,128)(2,1)S(1)}, u32[]{:S(2)}, u32[]{:S(2)}) collective-permute-start(bf16[2,96,768]{2,1,0:T(8,128)(2,1)S(1)} %get-tuple-element.310), channel_id=1, source_target_pairs={{0,8},{2,6},{4,12},{6,2},{8,0},{10,14},{12,4},{14,10},{16,24},{18,... | collective-permute-start | bytes 884744 | tf_op jit(solution)/shard_map/ppermute | solution.py:599
  126.0 16.4 %collective-permute-start.26 = (bf16[2,96,768]{2,1,0:T(8,128)(2,1)S(1)}, bf16[2,96,768]{2,1,0:T(8,128)(2,1)S(1)}, u32[]{:S(2)}, u32[]{:S(2)}) collective-permute-start(bf16[2,96,768]{2,1,0:T(8,128)(2,1)S(1)} %add_convert_fusion.8), channel_id=1, source_target_pairs={{0,16},{2,18},{4,20},{6,22},{8,24},{10,26},{12,28},{14,30},{16,0},... | collective-permute-start | bytes 884744 | tf_op jit(solution)/shard_map/ppermute | solution.py:599
  126.2 17.5 %collective-permute-start.25 = (bf16[2,192,768]{2,1,0:T(8,128)(2,1)S(1)}, bf16[2,192,768]{2,1,0:T(8,128)(2,1)S(1)}, u32[]{:S(2)}, u32[]{:S(2)}) collective-permute-start(bf16[2,192,768]{2,1,0:T(8,128)(2,1)S(1)} %pad_maximum_fusion.1), channel_id=1, source_target_pairs={{0,8},{2,6},{4,12},{6,2},{8,0},{10,14},{12,4},{14,10},{16,24},{18,... | collective-permute-start | bytes 1769480 | tf_op jit(solution)/shard_map/ppermute | solution.py:599
  129.6 8.4 %collective-permute-start.29 = (bf16[160,768]{1,0:T(8,128)(2,1)S(1)}, bf16[160,768]{1,0:T(8,128)(2,1)S(1)}, u32[]{:S(2)}, u32[]{:S(2)}) collective-permute-start(bf16[160,768]{1,0:T(8,128)(2,1)S(1)} %pad_maximum_fusion.2), channel_id=1, source_target_pairs={{0,3},{1,2},{2,1},{3,0},{4,7},{5,6},{6,5},{7,4},{8,11},{9,10},{10,... | collective-permute-start | bytes 737288 | tf_op jit(solution)/shard_map/ppermute | solution.py:555
  129.7 8.3 %collective-permute-start.28 = (bf16[160,768]{1,0:T(8,128)(2,1)S(1)}, bf16[160,768]{1,0:T(8,128)(2,1)S(1)}, u32[]{:S(2)}, u32[]{:S(2)}) collective-permute-start(bf16[160,768]{1,0:T(8,128)(2,1)S(1)} %pad_maximum_fusion.2), channel_id=1, source_target_pairs={{0,2},{1,3},{2,0},{3,1},{4,6},{5,7},{6,4},{7,5},{8,10},{9,11},{10,... | collective-permute-start | bytes 737288 | tf_op jit(solution)/shard_map/ppermute | solution.py:555
  129.8 10.7 %collective-permute-start.27 = (bf16[160,768]{1,0:T(8,128)(2,1)S(1)}, bf16[160,768]{1,0:T(8,128)(2,1)S(1)}, u32[]{:S(2)}, u32[]{:S(2)}) collective-permute-start(bf16[160,768]{1,0:T(8,128)(2,1)S(1)} %pad_maximum_fusion.2), channel_id=1, source_target_pairs={{0,1},{1,0},{2,3},{3,2},{4,5},{5,4},{6,7},{7,6},{8,9},{9,8},{10,11... | collective-permute-start | bytes 737288 | tf_op jit(solution)/shard_map/ppermute | solution.py:555
  143.8 17.9 %collective-permute-start.30 = (bf16[4,192,768]{2,1,0:T(8,128)(2,1)S(1)}, bf16[4,192,768]{2,1,0:T(8,128)(2,1)S(1)}, u32[]{:S(2)}, u32[]{:S(2)}) collective-permute-start(bf16[4,192,768]{2,1,0:T(8,128)(2,1)S(1)} %constant_dynamic-update-slice_fusion), channel_id=1, source_target_pairs={{0,4},{2,10},{4,0},{6,14},{8,12},{10,2},{12,8},{14,6},{16,20},{18,... | collective-permute-start | bytes 3538952 | tf_op jit(solution)/shard_map/ppermute | solution.py:599
  144.6 10.0 %collective-permute-start.31 = (bf16[2,96,768]{2,1,0:T(8,128)(2,1)S(1)}, bf16[2,96,768]{2,1,0:T(8,128)(2,1)S(1)}, u32[]{:S(2)}, u32[]{:S(2)}) collective-permute-start(bf16[2,96,768]{2,1,0:T(8,128)(2,1)S(1)} %add_convert_fusion.7), channel_id=1, source_target_pairs={{0,8},{2,6},{4,12},{6,2},{8,0},{10,14},{12,4},{14,10},{16,24},{18,... | collective-permute-start | bytes 884744 | tf_op jit(solution)/shard_map/ppermute | solution.py:599
  162.0 10.7 %collective-permute-start.33 = (bf16[4,96,768]{2,1,0:T(8,128)(2,1)S(1)}, bf16[4,96,768]{2,1,0:T(8,128)(2,1)S(1)}, u32[]{:S(2)}, u32[]{:S(2)}) collective-permute-start(bf16[4,96,768]{2,1,0:T(8,128)(2,1)S(1)} %constant_dynamic-update-slice_fusion.4), channel_id=1, source_target_pairs={{0,4},{2,10},{4,0},{6,14},{8,12},{10,2},{12,8},{14,6},{16,20},{18,... | collective-permute-start | bytes 1769480 | tf_op jit(solution)/shard_map/ppermute | solution.py:599
  (24 other events, 148.4 us)

commit v2 on v1

--- a/solution.py
+++ b/solution.py
@@ -223,7 +223,7 @@
     @pl.when(step == 0)
     def _():
         cs[...] = jnp.zeros_like(cs)
-        cs[0 : terms[0].shape[1], :] = sum(term[0] for term in terms)
+        cs[0 : terms[0].shape[1], :] = sum(term[0].astype(F32) for term in terms)
         high, low = split(cs[...])
         bias_sum = jnp.zeros((1, gs.shape[1]), F32)
         tail, half = padded - 8, parts // 2
@@ -485,25 +485,28 @@
     out[...] = (grad - unit * jnp.sum(unit * grad, axis=1, keepdims=True)) * inverse
 
 
-def unpack_kernel(layout, group, places, own, other, *outs):
-    odd = places[0] == 1
-    step = pl.program_id(0)
-    pairs, _, wide = own.shape
-    for out, first, last, at, n, parts in layout:
-        for flag, a, b, c, d in ((False, own, other, 1, 1 + pairs), (True, other, own, 1 + pairs, 1)):
-
-            @pl.when((odd == flag) & (step >= first) & (step < last))
-            def _():
-                for g in range(group):
-                    pair = step * group + g
-                    for part in range(parts):
-                        rows = slice(at + part * n, at + (part + 1) * n)
-                        columns = slice(part * wide, (part + 1) * wide)
-                        low = 2 * g * n
-                        outs[out][low : low + n, columns] = a[places[c + pair], rows, :].astype(F32)
-                        outs[out][low + n : low + 2 * n, columns] = b[
-                            places[d + pair], rows, :
-                        ].astype(F32)
+def unpack_kernel(layout, own, places, held, *refs):
+    count = len(layout)
+    outs, wides, sems = refs[-2 * count - 1 : -count - 1], refs[-count - 1 : -1], refs[-1]
+    pairs, _, wide = held.shape
+    core = places[0] if own else 1 - places[0]
+    copies = []
+    for pair in range(pairs):
+        at = places[(1 if own else 1 + pairs) + pair]
+        for k, (first, last, low, n, parts) in enumerate(layout):
+            if not first <= pair < last:
+                continue
+            buffer = wides[k].at[pair - first]
+            for part in range(parts):
+                rows = slice(low + part * n, low + (part + 1) * n)
+                buffer[:, part * wide : (part + 1) * wide] = held[at, rows, :].astype(F32)
+            start = pl.multiple_of((2 * (pair - first) + core) * n, n)
+            copies.append(
+                pltpu.make_async_copy(buffer, outs[k].at[pl.ds(start, n), :], sems.at[k, pair])
+            )
+            copies[-1].start()
+    for copy in copies:
+        copy.wait()
 
 
 def tie(v, *after):
@@ -604,19 +607,36 @@
     return add_low(kept[:half], other[:half]), add_low(kept[half:], other[half:])
 
 
-def unpack(places, own, other, layout, group, outs, name):
-    return call(
-        functools.partial(unpack_kernel, layout, group),
-        (own.shape[0] // group,),
-        [whole(own.shape), whole(own.shape)],
-        outs,
-        [],
-        1,
-        (places, own, other),
-        name,
-        0,
-        30,
-    )
+def unpack(places, held, before, layout, shapes, name):
+    own = not before
+    anywhere = pl.BlockSpec(memory_space=pl.ANY)
+    return pl.pallas_call(
+        functools.partial(unpack_kernel, layout, own),
+        grid_spec=pltpu.PrefetchScalarGridSpec(
+            num_scalar_prefetch=1,
+            grid=(1,),
+            in_specs=[whole(held.shape)] + [anywhere] * len(before),
+            out_specs=[anywhere] * len(shapes),
+            scratch_shapes=[
+                *[
+                    pltpu.VMEM((last - first, n, shape[1]), F32)
+                    for (first, last, _, n, _), shape in zip(layout, shapes)
+                ],
+                pltpu.SemaphoreType.DMA((len(layout), held.shape[0])),
+            ],
+        ),
+        out_shape=[sds(shape, F32) for shape in shapes],
+        input_output_aliases={2 + i: i for i in range(len(before))},
+        compiler_params=pltpu.CompilerParams(
+            dimension_semantics=("arbitrary",), vmem_limit_bytes=20 * 2**20
+        ),
+        name=name,
+    )(places, held, *before)
+
+
+def unpack_both(places, own, other, layout, shapes, name):
+    first = unpack(places, own, (), layout, shapes, name + "_own")
+    return unpack(places, other, tuple(first), layout, shapes, name + "_other")
 
 
 def largest(count, most):
@@ -671,6 +691,7 @@
     vector = whole((width,))
 
     x0, x1 = gather_halves(patches, "tensor")
+    g0, g1 = gather_halves(out_grad, "tensor")
 
     proto_step = min(512, protos)
     crop_bits = bits_of(groups)[1:]
@@ -679,28 +700,18 @@
     def crop_step(kept, other, bit, *after):
         kept, other = (lax.optimization_barrier((v, after))[0] for v in (kept, other))
         half = kept.shape[0] // 2
-        return kept[:half] + other[:half], swap(kept[half:] + other[half:], "dp", bit)
-
-    tables = call(
-        functools.partial(table_kernel, heads, head_size**0.5),
-        (1,),
-        [whole(rel_table.shape)],
-        [(sds((heads * 2 * SLOTS, LANES), BF), whole((heads * 2 * SLOTS, LANES)))],
-        [],
-        1,
-        (ids, rel_table),
-        "tables",
-        0,
-        24,
-    )[0]
+        total = kept + other.astype(F32)
+        return total[:half], swap(total[half:].astype(BF), "dp", bit)
+
     w_t = jnp.transpose(qkv_weight, (1, 2, 0)).reshape(3 * inner, width)
     wp = proj_weight.reshape(inner, width)
     unroll = largest(heads, 12)
+    unroll_first = largest(heads, 6)
     block3 = lambda a, b: pl.BlockSpec((1, a, b), lambda i, *_: (i, 0, 0))
     halves3 = lambda a, b, dtype: (sds((half, a, b), dtype), block3(a, b))
 
     def attend(first, x, ids):
-        dims = (first, rows, padded, heads, head_size, crops, unroll)
+        dims = (first, rows, padded, heads, head_size, crops, unroll_first)
         return call(
             functools.partial(attend_kernel, dims),
             (half,),
@@ -746,42 +757,53 @@
         [(sds(crop_shape, F32), whole(crop_shape)), (sds(crop_shape, F32), whole(crop_shape))],
         [pltpu.VMEM((score_grad.shape[0], width), F32)],
         1,
-        (tie(ids, tables), score_grad, prototypes),
+        (ids, score_grad, prototypes),
         "crop_grads",
         2 * score_grad.shape[0] * protos * width,
         16,
     )
     crop_other = swap(tie(crop_send, x1), "dp", 1)
-    g0, g1 = gather_halves(tie(out_grad, x1), "tensor")
-    xf0, h1_0, qkv0, pt0, ot0, a0 = attend(0, x0, tie(ids, crop_send))
+    tables = call(
+        functools.partial(table_kernel, heads, head_size**0.5),
+        (1,),
+        [whole(rel_table.shape)],
+        [(sds((heads * 2 * SLOTS, LANES), BF), whole((heads * 2 * SLOTS, LANES)))],
+        [],
+        1,
+        (tie(ids, crop_send), rel_table),
+        "tables",
+        0,
+        8,
+    )[0]
+    crop_held = crop_step(crop_keep, crop_other, crop_bits[0], tables)
+    xf0, h1_0, qkv0, pt0, ot0, a0 = attend(0, x0, tie(ids, crop_held[0]))
     a0, g1 = lax.optimization_barrier((a0, g1))
     b0 = swap(a0, "tensor", 1)
-    crop_held = crop_step(crop_keep, crop_other, crop_bits[0], a0)
+    crop_held = crop_step(*crop_held, crop_bits[1], a0)
     xf1, h1_1, qkv1, pt1, ot1, a1 = attend(half, x1, tie(ids, crop_held[0]))
     b1 = swap(tie(a1, b0, g1), "tensor", 1)
     if parts > 2:
         a_all, b_all = sum_halves(jnp.concatenate([a0, a1]), "tensor")
         a0, a1, b0, b1 = a_all[:half], a_all[half:], b_all[:half], b_all[half:]
-    for bit in crop_bits[1:-1]:
+    for bit in crop_bits[2:-1]:
         crop_held = crop_step(*crop_held, bit, a1)
     kept, other = (tie(v, a1) for v in crop_held)
-    kept, sent = kept[:1] + other[:1], kept[1:] + other[1:]
+    total = kept + other.astype(F32)
+    kept, sent = total[:1].astype(BF), total[1:].astype(BF)
     far = crop_bits[-1] * parts
-    crop_terms = [kept, swap(sent, ("dp", "tensor"), far)]
+    crop_terms = [total[:1], swap(sent, ("dp", "tensor"), far)]
     for move in range(1, parts):
         crop_terms += [
             swap(kept, ("dp", "tensor"), move),
             swap(sent, ("dp", "tensor"), far + move),
         ]
 
-    hidden_step = 768 if hidden % 768 == 0 else hidden
-    hidden_steps = hidden // hidden_step
     crops_slots = -(-group_crops // 16) * 16
     full = whole((parts, padded, width))
-    columns = lambda a: pl.BlockSpec((a, hidden_step), lambda i, *_: (0, i))
+    columns = lambda a: whole((a, hidden))
     y1, gy, h2, gz, m, gu, gh2_near, gh2_far, ob, hb = call(
         functools.partial(hidden_kernel, (parts, rows, padded, crops, group_crops)),
-        (hidden_steps,),
+        (1,),
         [
             *[whole((half, padded, width))] * 6,
             whole(g0.shape),
@@ -792,7 +814,7 @@
             vector,
             columns(width),
             columns(1),
-            pl.BlockSpec((hidden_step, width), lambda i, *_: (i, 0)),
+            whole((hidden, width)),
         ],
         [
             (sds((parts, padded, width), F32), full),
@@ -818,23 +840,23 @@
         ),
         "hidden",
         6 * all_rows * hidden * width,
-        34,
+        40,
     )
     near_other = swap(gh2_near, "tensor", half)
 
-    chunks_step = chunks // hidden_steps
+    chunks_step = chunks
     wide = min(hidden, width)
     n1, n2 = width // chunks, hidden // chunks
     rows_a = (n1 * hidden + n2 * width) // wide
     chunk_a = whole((pairs, rows_a, wide))
     keep_a, send_a = call(
         functools.partial(hidden_grad_kernel, (chunks, chunks_step, wide, orders_a)),
-        (hidden_steps,),
+        (1,),
         [
             whole((all_rows, width)),
             whole((all_rows, width)),
-            pl.BlockSpec((all_rows, hidden_step), lambda i, s: (0, i)),
-            pl.BlockSpec((all_rows, hidden_step), lambda i, s: (0, i)),
+            pl.BlockSpec((all_rows, hidden), lambda i, s: (0, i)),
+            pl.BlockSpec((all_rows, hidden), lambda i, s: (0, i)),
         ],
         [
             (sds((pairs, rows_a, wide), BF), chunk_a),
@@ -853,7 +875,10 @@
         near_other, far_other = f_all[:half], f_all[half:]
     else:
         far_other = swap(tie(gh2_far, near_other), "tensor", half)
-    core_a = swap(tie(send_a, near_other), "dp", 1)
+    send_a = tie(send_a, near_other)
+    cut = pairs // 2
+    core_high = swap(send_a[cut:], "dp", 1)
+    core_low = swap(send_a[:cut], "dp", 1)
 
     n_b = 4 * inner // chunks
     chunk_b = whole((pairs, n_b, width))
@@ -895,11 +920,8 @@
 
     z_part = call(
         functools.partial(share_kernel, parts, padded),
-        (hidden_steps,),
-        [
-            pl.BlockSpec((all_rows, hidden_step), lambda i: (0, i)),
-            pl.BlockSpec((hidden_step, width), lambda i: (i, 0)),
-        ],
+        (1,),
+        [whole((all_rows, hidden)), whole((hidden, width))],
         [(sds((parts, padded, width), BF), full)],
         [pltpu.VMEM((all_rows, width), F32)],
         0,
@@ -908,12 +930,13 @@
         2 * all_rows * hidden * width,
         16,
     )[0]
-    kept_a, sent_a = add_halves(tie(keep_a, z_part), tie(core_a, z_part))
+    sent_a = add_low(tie(keep_a[cut:], z_part), tie(core_high, z_part))
     other_a = mixed_swap(sent_a, list(zip(*orders_a))[0])
     _, gh1_far, ga1, gq1, sums1, qb1, tt1 = attend_back(
         half, gh2_far, near_other, xf1, qkv1, pt1, tie(ids, sent_a)
     )
-    gh1_far, far_other = lax.optimization_barrier((gh1_far, far_other))
+    gh1_far, far_other, core_low = lax.optimization_barrier((gh1_far, far_other, core_low))
+    kept_a = add_low(tie(keep_a[:cut], gh1_far), core_low)
     z0, z1 = scatter_halves(tie(z_part, gh1_far), "tensor")
     g_own, gh1_near, ga0, gq0, sums0, qb0, tt0 = attend_back(
         0, gh2_near, far_other, xf0, qkv0, pt0, tie(ids, gh1_far)
@@ -932,7 +955,7 @@
         ],
         [pltpu.VMEM((inner, width), F32), pltpu.VMEM((3 * inner, width), F32)],
         1,
-        (tie(ids, other_a, z1), *args),
+        (tie(ids, other_a), *args),
         "attend_grads",
         2 * all_rows * 4 * inner * width,
         30,
@@ -968,30 +991,21 @@
     def hidden_sum():
         kept, other = yield kept_a, other_a
         held, other = yield from all_sum(kept, other, orders_a, 1, 2)
-        group = 2 - pairs % 2
         layout = (
-            (0, 0, pairs, 0, n1, hidden // wide),
-            (1, 0, pairs, rows_a - n2 * width // wide, n2, width // wide),
+            (0, pairs, 0, n1, hidden // wide),
+            (0, pairs, rows_a - n2 * width // wide, n2, width // wide),
         )
-        outs = [
-            (sds((width, hidden), F32), pl.BlockSpec((2 * group * n1, hidden), lambda i, s: (i, 0))),
-            (sds((hidden, width), F32), pl.BlockSpec((2 * group * n2, width), lambda i, s: (i, 0))),
-        ]
-        return (yield unpack(places_of(orders_a), held, other, layout, group, outs, "unpack_hidden"))
+        shapes = ((width, hidden), (hidden, width))
+        return (yield unpack_both(places_of(orders_a), held, other, layout, shapes, "unpack_hidden"))
 
     def attend_sum():
         kept, sent = yield keep_b, send_b
         kept, other = yield kept, swap(sent, "dp", 1)
         held, other = yield from all_sum(kept, other, orders_b, 0, 1)
         edge = inner // (2 * n_b)
-        group = 2 - edge % 2
-        edge = edge // group
-        layout = ((0, 0, edge, 0, n_b, 1), (1, edge, pairs, 0, n_b, 1))
-        shape = (2 * group * n_b, width)
-        early = pl.BlockSpec(shape, lambda i, s: (jnp.minimum(i, edge - 1), 0))
-        late = pl.BlockSpec(shape, lambda i, s: (jnp.maximum(i - edge, 0), 0))
-        outs = [(sds((inner, width), F32), early), (sds((3 * inner, width), F32), late)]
-        return unpack(places_of(orders_b), held, other, layout, group, outs, "unpack_attend")
+        layout = ((0, edge, 0, n_b, 1), (edge, pairs, 0, n_b, 1))
+        shapes = ((inner, width), (3 * inner, width))
+        return unpack_both(places_of(orders_b), held, other, layout, shapes, "unpack_attend")
 
     def patch():
         yield ()

time: 179 us -> 167 us (0.933)
  waiting for transfers between devices: 71.8 us -> 63 us
  starting transfers between devices: 39.6 us -> 36.8 us
    pallas_call x16 -> x14, Pallas kernels: 58.2 us -> 46 us  [call(): pl.pallas_call(body, grid_spec=pltpu.PrefetchScalarGridSpec(num_scalar_pr...]
    pallas_call x0 -> x4, Pallas kernels: none -> 11.6 us  [unpack(): pl.pallas_call(functools.partial(unpack_kernel, layout, own), grid_spec=p...]
    ppermute x11, waiting for transfers between devices: 29.4 us -> 21.9 us  [mixed_swap(): return lax.ppermute(v, 'dp', [(i, i ^ bits[i & 1]) for i in range(size)])]
    ppermute x24 -> x25, starting transfers between devices: 25.8 us -> 22.1 us  [swap(): return lax.ppermute(v, axis, partner(axis, bit))]
    ppermute x24 -> x25, waiting for transfers between devices: 42.4 us -> 41.1 us  [swap(): return lax.ppermute(v, axis, partner(axis, bit))]
  transfers between devices with their start and end apart: 35 -> 36, of which waited for: 25 -> 21; matrix products, arithmetic and copies ran while one was open for 1% -> 2% of each run, Pallas kernels for 27% -> 31%
where the time goes in v2:
time: 167 us; the launch traced here: 166 us
  waiting for transfers between devices  63 us (38%)
  Pallas kernels  57.6 us (34%)
  starting transfers between devices  36.8 us (22%)
  local copies, waits for them, and re-layouts  5.03 us (3%)
  other arithmetic  2.46 us (1%)
    pallas_call x14, Pallas kernels, call(): pl.pallas_call(body, grid_spec=pltpu.PrefetchScalarGridSpec(num_scalar_pr...  46 us
    ppermute x25, waiting for transfers between devices, swap(): return lax.ppermute(v, axis, partner(axis, bit))  41.1 us
    ppermute x25, starting transfers between devices, swap(): return lax.ppermute(v, axis, partner(axis, bit))  22.1 us
    ppermute x11, waiting for transfers between devices, mixed_swap(): return lax.ppermute(v, 'dp', [(i, i ^ bits[i & 1]) for i in range(size)])  21.9 us
    ppermute x11, starting transfers between devices, mixed_swap(): return lax.ppermute(v, 'dp', [(i, i ^ bits[i & 1]) for i in range(size)])  14.7 us
    pallas_call x4, Pallas kernels, unpack(): pl.pallas_call(functools.partial(unpack_kernel, layout, own), grid_spec=p...  11.6 us
    unnamed x46, local copies, waits for them, and re-layouts  4.32 us
  transfers between devices with their start and end apart: 36, of which 21 were waited for; matrix products, arithmetic and copies ran while one was open for 2% of the time, Pallas kernels for 31%

profile of v2, /device:TPU:0, one launch (start us, length us, event | category | flops | bytes accessed | tf_op | source)
XLA Modules:
  0.0 166.4 jit_solution(5714824644075340605)
XLA Ops:
  0.6 3.0 %collective-permute-start = (bf16[1,170,768]{2,1,0:T(8,128)(2,1)}, bf16[1,170,768]{2,1,0:T(8,128)(2,1)S(1)}, u32[]{:S(2)}, u32[]{:S(2)}) collective-permute-start(bf16[1,170,768]{2,1,0:T(8,128)(2,1)} %bitcast.24), channel_id=1, source_target_pairs={{0,1},{1,0},{2,3},{3,2},{4,5},{5,4},{6,7},{7,6},{8,9},{9,8},{10,11... | collective-permute-start | bytes 783368 | tf_op jit(solution)/shard_map/ppermute | solution.py:558
  3.8 1.9 %copy-done.1 = bf16[2048,768]{1,0:T(8,128)(2,1)S(1)} copy-done((bf16[2048,768]{1,0:T(8,128)(2,1)S(1)}, bf16[2048,768]{1,0:T(8,128)(2,1)}, u32[]{:S(2)}) %copy-start.1) | copy-done | bytes 3145752
  7.0 3.4 %crop_grads.1 = (f32[8,24,768]{2,1,0:T(8,128)S(1)}, f32[8,24,768]{2,1,0:T(8,128)S(1)}) custom-call(s32[3]{0:T(128)S(1)} %pad_add_fusion.ids, bf16[320,2048]{1,0:T(8,128)(2,1)S(1)} %copy-done.5, bf16[2048,768]{1,0:T(8,128)(2,1)S(1)} %copy-done.1), custom_call_target="tpu_custom_call" | custom-call | flops 10066329 | bytes 56361 | tf_op jit(solution)/shard_map/crop_grads/pallas_call | solution.py:82
  15.5 4.9 %attend.2 = (bf16[1,176,768]{2,1,0:T(8,128)(2,1)S(1)}, bf16[1,176,768]{2,1,0:T(8,128)(2,1)S(1)}, bf16[1,1152,176]{2,1,0:T(8,128)(2,1)S(1)}, bf16[1,12,176,176]{3...) custom-call(s32[3]{0:T(128)S(1)} %pad_add_fusion.ids, s32[20]{0:T(128)S(1)} %copy-done.13, ...), custom_call_target="tpu_custom_call" | custom-call | flops 4152360 | bytes 53146 | tf_op jit(solution)/shard_map/attend/pallas_call | solution.py:82
  21.1 1.6 collective-permute-start.6
  22.8 5.0 %attend.3 = (bf16[1,176,768]{2,1,0:T(8,128)(2,1)S(1)}, bf16[1,176,768]{2,1,0:T(8,128)(2,1)S(1)}, bf16[1,1152,176]{2,1,0:T(8,128)(2,1)S(1)}, bf16[1,12,176,176]{3...) custom-call(s32[3]{0:T(128)S(1)} %pad_add_fusion.ids, s32[20]{0:T(128)S(1)} %copy-done.13, ...), custom_call_target="tpu_custom_call" | custom-call | flops 4152360 | bytes 53146 | tf_op jit(solution)/shard_map/attend/pallas_call | solution.py:82
  29.4 2.7 %collective-permute-start.7 = (bf16[1,24,768]{2,1,0:T(8,128)(2,1)S(1)}, bf16[1,24,768]{2,1,0:T(8,128)(2,1)S(1)}, u32[]{:S(2)}, u32[]{:S(2)}) collective-permute-start(bf16[1,24,768]{2,1,0:T(8,128)(2,1)S(1)} %get-tuple-element.329), channel_id=1, source_target_pairs={{0,16},{1,17},{2,18},{3,19},{4,20},{5,21},{6,22},{7,23},{8,24},{9,... | collective-permute-start | bytes 110600 | tf_op jit(solution)/shard_map/ppermute | solution.py:558
  34.4 3.3 %collective-permute-done.8.rest_2_ = bf16[1,24,768]{2,1,0:T(8,128)(2,1)S(1)} collective-permute-done((bf16[1,24,768]{2,1,0:T(8,128)(2,1)S(1)}, bf16[1,24,768]{2,1,0:T(8,128)(2,1)S(1)}, u32[]{:S(2)}, u32[]{:S(2)}) %collective-permute-start.8) | collective-permute-done | bytes 36896 | tf_op jit(solution)/shard_map/ppermute | solution.py:558
  37.7 1.7 %collective-permute-done.9.rest_3_ = bf16[1,24,768]{2,1,0:T(8,128)(2,1)S(1)} collective-permute-done((bf16[1,24,768]{2,1,0:T(8,128)(2,1)S(1)}, bf16[1,24,768]{2,1,0:T(8,128)(2,1)S(1)}, u32[]{:S(2)}, u32[]{:S(2)}) %collective-permute-start.9) | collective-permute-done | bytes 36896 | tf_op jit(solution)/shard_map/ppermute | solution.py:558
  39.5 4.3 %hidden.1 = (f32[2,176,768]{2,1,0:T(8,128)S(1)}, f32[2,176,768]{2,1,0:T(8,128)S(1)}, bf16[352,768]{1,0:T(8,128)(2,1)S(1)}, bf16[352,768]{1,0:T(8,128)(2,1)S(1)},...) custom-call(s32[3]{0:T(128)S(1)} %pad_add_fusion.ids, ...), custom_call_target="tpu_custom_call" | custom-call | flops 24914164 | bytes 130192 | tf_op jit(solution)/shard_map/hidden/pallas_call | solution.py:82
  44.4 3.2 %hidden_grads.1 = (bf16[8,192,768]{2,1,0:T(8,128)(2,1)S(1)}, bf16[8,192,768]{2,1,0:T(8,128)(2,1)S(1)}) custom-call(s32[3]{0:T(128)S(1)} %pad_add_fusion.ids, bf16[352,768]{1,0:T(8,128)(2,1)S(1)} %get-tuple-element.182.h2, bf16[352,768]{1,0:T(8,128)(2,1)S(1)} %get-tuple-element.183.gz, bf16[352,1536]{1,0:T(8,128)(2,1)S(1)} %get-tuple-element.187.m, ...), custom_call_target="tpu_custom_call" | custom-call | flops 16609443 | bytes 79626 | tf_op jit(solution)/shard_map/hidden_grads/pallas_call | solution.py:82
  47.6 2.8 %collective-permute-done.10.e1 = bf16[1,176,768]{2,1,0:T(8,128)(2,1)S(1)} collective-permute-done((bf16[1,176,768]{2,1,0:T(8,128)(2,1)S(1)}, bf16[1,176,768]{2,1,0:T(8,128)(2,1)S(1)}, u32[]{:S(2)}, u32[]{:S(2)}) %collective-permute-start.10) | collective-permute-done | bytes 270368 | tf_op jit(solution)/shard_map/ppermute | solution.py:558
  55.8 5.8 %attend_back.2 = (f32[1,176,768]{2,1,0:T(8,128)}, bf16[1,176,768]{2,1,0:T(8,128)(2,1)S(1)}, bf16[1,176,768]{2,1,0:T(8,128)(2,1)S(1)}, bf16[1,1152,176]{2,1,0:T(8...) custom-call(s32[3]{0:T(128)S(1)} %pad_add_fusion.ids, s32[20]{0:T(128)S(1)} %copy-done.13, ...), custom_call_target="tpu_custom_call" | custom-call | flops 8304721 | bytes 86231 | tf_op jit(solution)/shard_map/attend_back/pallas_call | solution.py:82
  61.6 2.0 %collective-permute-done.12.e1 = bf16[1,176,768]{2,1,0:T(8,128)(2,1)S(1)} collective-permute-done((bf16[1,176,768]{2,1,0:T(8,128)(2,1)S(1)}, bf16[1,176,768]{2,1,0:T(8,128)(2,1)S(1)}, u32[]{:S(2)}, u32[]{:S(2)}) %collective-permute-start.12) | collective-permute-done | bytes 270368 | tf_op jit(solution)/shard_map/ppermute | solution.py:558
  64.2 5.6 %attend_back.3 = (f32[1,176,768]{2,1,0:T(8,128)S(1)}, bf16[1,176,768]{2,1,0:T(8,128)(2,1)S(1)}, bf16[1,176,768]{2,1,0:T(8,128)(2,1)S(1)}, bf16[1,1152,176]{2,1,0...) custom-call(s32[3]{0:T(128)S(1)} %pad_add_fusion.ids, s32[20]{0:T(128)S(1)} %copy-done.13, ...), custom_call_target="tpu_custom_call" | custom-call | flops 8304721 | bytes 86231 | tf_op jit(solution)/shard_map/attend_back/pallas_call | solution.py:82
  70.2 2.1 %attend_grads.1 = (bf16[8,96,768]{2,1,0:T(8,128)(2,1)S(1)}, bf16[8,96,768]{2,1,0:T(8,128)(2,1)S(1)}, f32[16,768]{1,0:T(8,128)S(1)}) custom-call(s32[3]{0:T(128)S(1)} %pad_add_fusion.ids, bf16[1,384,176]{2,1,0:T(8,128)(2,1)S(1)} %get-tuple-element.204.o0, bf16[1,384,176]{2,1,0:T(8,128)(2,1)S(1)} %get-tuple-element.205.o1, ...), custom_call_target="tpu_custom_call" | custom-call | flops 8304721 | bytes 58828 | tf_op jit(solution)/shard_map/attend_grads/pallas_call | solution.py:82
  77.4 5.4 %collective-permute-done.19.e1 = bf16[1,176,768]{2,1,0:T(8,128)(2,1)S(1)} collective-permute-done((bf16[1,176,768]{2,1,0:T(8,128)(2,1)S(1)}, bf16[1,176,768]{2,1,0:T(8,128)(2,1)S(1)}, u32[]{:S(2)}, u32[]{:S(2)}) %collective-permute-start.19) | collective-permute-done | bytes 270368 | tf_op jit(solution)/shard_map/ppermute | solution.py:558
  84.4 2.4 %collective-permute-start.20 = (bf16[1,192,768]{2,1,0:T(8,128)(2,1)S(1)}, bf16[1,192,768]{2,1,0:T(8,128)(2,1)S(1)}, u32[]{:S(2)}, u32[]{:S(2)}) collective-permute-start(bf16[1,192,768]{2,1,0:T(8,128)(2,1)S(1)} %get-tuple-element.249), channel_id=1, source_target_pairs={{0,16},{2,18},{4,20},{6,22},{8,24},{10,26},{12,28},{14,30},{16,0},... | collective-permute-start | bytes 884744 | tf_op jit(solution)/shard_map/ppermute | solution.py:602
  90.5 9.2 %collective-permute-done.22 = bf16[64,768]{1,0:T(8,128)(2,1)S(1)} collective-permute-done((bf16[64,768]{1,0:T(8,128)(2,1)S(1)}, bf16[64,768]{1,0:T(8,128)(2,1)S(1)}, u32[]{:S(2)}, u32[]{:S(2)}) %collective-permute-start.22) | collective-permute-done | bytes 98336 | tf_op jit(solution)/shard_map/ppermute | solution.py:558
  99.9 1.9 %collective-permute-start.24 = (bf16[2,96,768]{2,1,0:T(8,128)(2,1)S(1)}, bf16[2,96,768]{2,1,0:T(8,128)(2,1)S(1)}, u32[]{:S(2)}, u32[]{:S(2)}) collective-permute-start(bf16[2,96,768]{2,1,0:T(8,128)(2,1)S(1)} %get-tuple-element.322), channel_id=1, source_target_pairs={{0,8},{2,6},{4,12},{6,2},{8,0},{10,14},{12,4},{14,10},{16,24},{18,... | collective-permute-start | bytes 884744 | tf_op jit(solution)/shard_map/ppermute | solution.py:602
  103.4 5.2 %collective-permute-done.25 = bf16[96,768]{1,0:T(8,128)(2,1)S(1)} collective-permute-done((bf16[96,768]{1,0:T(8,128)(2,1)S(1)}, bf16[96,768]{1,0:T(8,128)(2,1)S(1)}, u32[]{:S(2)}, u32[]{:S(2)}) %collective-permute-start.25) | collective-permute-done | bytes 147488 | tf_op jit(solution)/shard_map/ppermute | solution.py:558
  108.5 6.7 %collective-permute-done.23 = bf16[1,192,768]{2,1,0:T(8,128)(2,1)S(1)} collective-permute-done((bf16[1,192,768]{2,1,0:T(8,128)(2,1)S(1)}, bf16[1,192,768]{2,1,0:T(8,128)(2,1)S(1)}, u32[]{:S(2)}, u32[]{:S(2)}) %collective-permute-start.23) | collective-permute-done | bytes 294944 | tf_op jit(solution)/shard_map/ppermute | solution.py:602
  115.6 3.0 %collective-permute-start.27 = (bf16[2,96,768]{2,1,0:T(8,128)(2,1)S(1)}, bf16[2,96,768]{2,1,0:T(8,128)(2,1)S(1)}, u32[]{:S(2)}, u32[]{:S(2)}) collective-permute-start(bf16[2,96,768]{2,1,0:T(8,128)(2,1)S(1)} %add_convert_fusion.8), channel_id=1, source_target_pairs={{0,16},{2,18},{4,20},{6,22},{8,24},{10,26},{12,28},{14,30},{16,0},... | collective-permute-start | bytes 884744 | tf_op jit(solution)/shard_map/ppermute | solution.py:602
  120.8 6.7 %collective-permute-done.28 = bf16[160,768]{1,0:T(8,128)(2,1)S(1)} collective-permute-done((bf16[160,768]{1,0:T(8,128)(2,1)S(1)}, bf16[160,768]{1,0:T(8,128)(2,1)S(1)}, u32[]{:S(2)}, u32[]{:S(2)}) %collective-permute-start.28) | collective-permute-done | bytes 245792 | tf_op jit(solution)/shard_map/ppermute | solution.py:558
  128.3 3.8 %collective-permute-done.27 = bf16[2,96,768]{2,1,0:T(8,128)(2,1)S(1)} collective-permute-done((bf16[2,96,768]{2,1,0:T(8,128)(2,1)S(1)}, bf16[2,96,768]{2,1,0:T(8,128)(2,1)S(1)}, u32[]{:S(2)}, u32[]{:S(2)}) %collective-permute-start.27) | collective-permute-done | bytes 294944 | tf_op jit(solution)/shard_map/ppermute | solution.py:602
  135.6 5.9 %proto_grads.1 = f32[2048,768]{1,0:T(8,128)} custom-call(s32[3]{0:T(128)S(1)} %pad_add_fusion.ids, bf16[320,2048]{1,0:T(8,128)(2,1)S(1)} %copy-done.6, bf16[512,768]{1,0:T(8,128)(2,1)S(1)} %pad_maximum_fusion.pooled, bf16[2048,768]{1,0:T(8,128)(2,1)S(1)} %copy-done.2, s32[1,2048]{1,0:T(1,128)S(1)} %bitcast.31), custom_call_target="tpu_custom_call" | custom-call | flops 10066329 | bytes 115425 | tf_op jit(solution)/shard_map/proto_grads/pallas_call | solution.py:82
  141.5 2.3 %collective-permute-done.32 = bf16[2,96,768]{2,1,0:T(8,128)(2,1)S(1)} collective-permute-done((bf16[2,96,768]{2,1,0:T(8,128)(2,1)S(1)}, bf16[2,96,768]{2,1,0:T(8,128)(2,1)S(1)}, u32[]{:S(2)}, u32[]{:S(2)}) %collective-permute-start.32) | collective-permute-done | bytes 294944 | tf_op jit(solution)/shard_map/ppermute | solution.py:602
  143.8 7.1 %collective-permute-done.31 = bf16[4,192,768]{2,1,0:T(8,128)(2,1)S(1)} collective-permute-done((bf16[4,192,768]{2,1,0:T(8,128)(2,1)S(1)}, bf16[4,192,768]{2,1,0:T(8,128)(2,1)S(1)}, u32[]{:S(2)}, u32[]{:S(2)}) %collective-permute-start.31) | collective-permute-done | bytes 1179680 | tf_op jit(solution)/shard_map/ppermute | solution.py:602
  152.5 2.9 %unpack_hidden_own.1 = (f32[768,1536]{1,0:T(8,128)}, f32[1536,768]{1,0:T(8,128)}) custom-call(s32[17]{0:T(128)S(1)} %pad_add_fusion.1.places, bf16[8,192,768]{2,1,0:T(8,128)(2,1)S(1)} %constant_dynamic-update-slice_fusion.2.held), custom_call_target="tpu_custom_call" | custom-call | tf_op jit(solution)/shard_map/unpack_hidden_own/pallas_call | solution.py:613
  155.8 4.5 %unpack_hidden_other.1 = (f32[768,1536]{1,0:T(8,128)}, f32[1536,768]{1,0:T(8,128)}) custom-call(s32[17]{0:T(128)S(1)} %pad_add_fusion.1.places, bf16[8,192,768]{2,1,0:T(8,128)(2,1)} %collective-permute-done.33.held, f32[768,1536]{1,0:T(8,128)} %get-tuple-element.286.refs_0_, ...), custom_call_target="tpu_custom_call", output_to_operand_aliasing={{0}: (2, {}), {1}: (3, {})} | custom-call | tf_op jit(solution)/shard_map/unpack_hidden_other/pallas_call | solution.py:613
  161.3 2.1 %unpack_attend_own.1 = (f32[384,768]{1,0:T(8,128)}, f32[1152,768]{1,0:T(8,128)}) custom-call(s32[17]{0:T(128)S(1)} %pad_add_fusion.1.places, bf16[8,96,768]{2,1,0:T(8,128)(2,1)S(1)} %constant_dynamic-update-slice_fusion.6.held), custom_call_target="tpu_custom_call" | custom-call | tf_op jit(solution)/shard_map/unpack_attend_own/pallas_call | solution.py:613
  164.2 2.1 %unpack_attend_other.1 = (f32[384,768]{1,0:T(8,128)}, f32[1152,768]{1,0:T(8,128)}) custom-call(s32[17]{0:T(128)S(1)} %pad_add_fusion.1.places, bf16[8,96,768]{2,1,0:T(8,128)(2,1)S(1)} %collective-permute-done.35.held, f32[384,768]{1,0:T(8,128)} %get-tuple-element.294.refs_0_, ...), custom_call_target="tpu_custom_call", output_to_operand_aliasing={{0}: (2, {}), {1}: (3, {})} | custom-call | tf_op jit(solution)/shard_map/unpack_attend_other/pallas_call | solution.py:613
  (159 shorter events, 40.4 us)
Async XLA Ops:
  0.6 9.7 %collective-permute-start = (bf16[1,170,768]{2,1,0:T(8,128)(2,1)}, bf16[1,170,768]{2,1,0:T(8,128)(2,1)S(1)}, u32[]{:S(2)}, u32[]{:S(2)}) collective-permute-start(bf16[1,170,768]{2,1,0:T(8,128)(2,1)} %bitcast.24), channel_id=1, source_target_pairs={{0,1},{1,0},{2,3},{3,2},{4,5},{5,4},{6,7},{7,6},{8,9},{9,8},{10,11... | collective-permute-start | bytes 783368 | tf_op jit(solution)/shard_map/ppermute | solution.py:558
  10.5 10.0 %collective-permute-start.2 = (bf16[1,170,768]{2,1,0:T(8,128)(2,1)S(1)}, bf16[1,170,768]{2,1,0:T(8,128)(2,1)S(1)}, u32[]{:S(2)}, u32[]{:S(2)}) collective-permute-start(bf16[1,170,768]{2,1,0:T(8,128)(2,1)S(1)} %bitcast.26), channel_id=1, source_target_pairs={{0,1},{1,0},{2,3},{3,2},{4,5},{5,4},{6,7},{7,6},{8,9},{9,8},{10,11... | collective-permute-start | bytes 783368 | tf_op jit(solution)/shard_map/ppermute | solution.py:558
  13.8 7.2 %collective-permute-start.3 = (bf16[4,24,768]{2,1,0:T(8,128)(2,1)S(1)}, bf16[4,24,768]{2,1,0:T(8,128)(2,1)S(1)}, u32[]{:S(2)}, u32[]{:S(2)}) collective-permute-start(bf16[4,24,768]{2,1,0:T(8,128)(2,1)S(1)} %slice.216), channel_id=1, source_target_pairs={{0,4},{2,6},{4,0},{6,2},{8,12},{10,14},{12,8},{14,10},{16,20},{18,... | collective-permute-start | bytes 442376 | tf_op jit(solution)/shard_map/ppermute | solution.py:558
  20.4 8.5 %collective-permute-start.4 = (bf16[1,176,768]{2,1,0:T(8,128)(2,1)S(1)}, bf16[1,176,768]{2,1,0:T(8,128)(2,1)S(1)}, u32[]{:S(2)}, u32[]{:S(2)}) collective-permute-start(bf16[1,176,768]{2,1,0:T(8,128)(2,1)S(1)} %get-tuple-element.171.a0), channel_id=1, source_target_pairs={{0,1},{1,0},{2,3},{3,2},{4,5},{5,4},{6,7},{7,6},{8,9},{9,8},{10,11... | collective-permute-start | bytes 811016 | tf_op jit(solution)/shard_map/ppermute | solution.py:558
  21.1 6.7 %collective-permute-start.6 = (bf16[2,24,768]{2,1,0:T(8,128)(2,1)S(1)}, bf16[2,24,768]{2,1,0:T(8,128)(2,1)S(1)}, u32[]{:S(2)}, u32[]{:S(2)}) collective-permute-start(bf16[2,24,768]{2,1,0:T(8,128)(2,1)S(1)} %slice.217), channel_id=1, source_target_pairs={{0,8},{2,10},{4,12},{6,14},{8,0},{10,2},{12,4},{14,6},{16,24},{18,... | collective-permute-start | bytes 221192 | tf_op jit(solution)/shard_map/ppermute | solution.py:558
  28.9 10.5 %collective-permute-start.5 = (bf16[1,176,768]{2,1,0:T(8,128)(2,1)S(1)}, bf16[1,176,768]{2,1,0:T(8,128)(2,1)S(1)}, u32[]{:S(2)}, u32[]{:S(2)}) collective-permute-start(bf16[1,176,768]{2,1,0:T(8,128)(2,1)S(1)} %get-tuple-element.178.a1), channel_id=1, source_target_pairs={{0,1},{1,0},{2,3},{3,2},{4,5},{5,4},{6,7},{7,6},{8,9},{9,8},{10,11... | collective-permute-start | bytes 811016 | tf_op jit(solution)/shard_map/ppermute | solution.py:558
  29.4 4.9 %collective-permute-start.7 = (bf16[1,24,768]{2,1,0:T(8,128)(2,1)S(1)}, bf16[1,24,768]{2,1,0:T(8,128)(2,1)S(1)}, u32[]{:S(2)}, u32[]{:S(2)}) collective-permute-start(bf16[1,24,768]{2,1,0:T(8,128)(2,1)S(1)} %get-tuple-element.329), channel_id=1, source_target_pairs={{0,16},{1,17},{2,18},{3,19},{4,20},{5,21},{6,22},{7,23},{8,24},{9,... | collective-permute-start | bytes 110600 | tf_op jit(solution)/shard_map/ppermute | solution.py:558
  32.1 5.6 %collective-permute-start.8 = (bf16[1,24,768]{2,1,0:T(8,128)(2,1)S(1)}, bf16[1,24,768]{2,1,0:T(8,128)(2,1)S(1)}, u32[]{:S(2)}, u32[]{:S(2)}) collective-permute-start(bf16[1,24,768]{2,1,0:T(8,128)(2,1)S(1)} %get-tuple-element.328), channel_id=1, source_target_pairs={{0,1},{1,0},{2,3},{3,2},{4,5},{5,4},{6,7},{7,6},{8,9},{9,8},{10,11... | collective-permute-start | bytes 110600 | tf_op jit(solution)/shard_map/ppermute | solution.py:558
  33.7 5.8 %collective-permute-start.9 = (bf16[1,24,768]{2,1,0:T(8,128)(2,1)S(1)}, bf16[1,24,768]{2,1,0:T(8,128)(2,1)S(1)}, u32[]{:S(2)}, u32[]{:S(2)}) collective-permute-start(bf16[1,24,768]{2,1,0:T(8,128)(2,1)S(1)} %get-tuple-element.329), channel_id=1, source_target_pairs={{0,17},{1,16},{2,19},{3,18},{4,21},{5,20},{6,23},{7,22},{8,25},{9,... | collective-permute-start | bytes 110600 | tf_op jit(solution)/shard_map/ppermute | solution.py:558
  43.8 6.5 %collective-permute-start.10 = (bf16[1,176,768]{2,1,0:T(8,128)(2,1)S(1)}, bf16[1,176,768]{2,1,0:T(8,128)(2,1)S(1)}, u32[]{:S(2)}, u32[]{:S(2)}) collective-permute-start(bf16[1,176,768]{2,1,0:T(8,128)(2,1)S(1)} %get-tuple-element.190.e0), channel_id=1, source_target_pairs={{0,1},{1,0},{2,3},{3,2},{4,5},{5,4},{6,7},{7,6},{8,9},{9,8},{10,11... | collective-permute-start | bytes 811016 | tf_op jit(solution)/shard_map/ppermute | solution.py:558
  51.6 12.0 %collective-permute-start.13 = (bf16[4,192,768]{2,1,0:T(8,128)(2,1)S(1)}, bf16[4,192,768]{2,1,0:T(8,128)(2,1)S(1)}, u32[]{:S(2)}, u32[]{:S(2)}) collective-permute-start(bf16[4,192,768]{2,1,0:T(8,128)(2,1)S(1)} %get-tuple-element.320), channel_id=1, source_target_pairs={{0,2},{2,0},{4,6},{6,4},{8,10},{10,8},{12,14},{14,12},{16,18},{18,... | collective-permute-start | bytes 3538952 | tf_op jit(solution)/shard_map/ppermute | solution.py:558
  53.7 16.4 %collective-permute-start.14 = (bf16[4,192,768]{2,1,0:T(8,128)(2,1)S(1)}, bf16[4,192,768]{2,1,0:T(8,128)(2,1)S(1)}, u32[]{:S(2)}, u32[]{:S(2)}) collective-permute-start(bf16[4,192,768]{2,1,0:T(8,128)(2,1)S(1)} %add_convert_fusion.1), channel_id=1, source_target_pairs={{0,4},{2,10},{4,0},{6,14},{8,12},{10,2},{12,8},{14,6},{16,20},{18,... | collective-permute-start | bytes 3538952 | tf_op jit(solution)/shard_map/ppermute | solution.py:602
  55.3 8.3 %collective-permute-start.12 = (bf16[1,176,768]{2,1,0:T(8,128)(2,1)S(1)}, bf16[1,176,768]{2,1,0:T(8,128)(2,1)S(1)}, u32[]{:S(2)}, u32[]{:S(2)}) collective-permute-start(bf16[1,176,768]{2,1,0:T(8,128)(2,1)S(1)} %get-tuple-element.199.e0), channel_id=1, source_target_pairs={{0,1},{1,0},{2,3},{3,2},{4,5},{5,4},{6,7},{7,6},{8,9},{9,8},{10,11... | collective-permute-start | bytes 811016 | tf_op jit(solution)/shard_map/ppermute | solution.py:558
  63.7 8.6 %collective-permute-start.15 = (bf16[1,176,768]{2,1,0:T(8,128)(2,1)S(1)}, bf16[1,176,768]{2,1,0:T(8,128)(2,1)S(1)}, u32[]{:S(2)}, u32[]{:S(2)}) collective-permute-start(bf16[1,176,768]{2,1,0:T(8,128)(2,1)S(1)} %get-tuple-element.326), channel_id=1, source_target_pairs={{0,1},{1,0},{2,3},{3,2},{4,5},{5,4},{6,7},{7,6},{8,9},{9,8},{10,11... | collective-permute-start | bytes 811016 | tf_op jit(solution)/shard_map/ppermute | solution.py:558
  72.3 11.9 %collective-permute-start.17 = (bf16[8,96,768]{2,1,0:T(8,128)(2,1)S(1)}, bf16[8,96,768]{2,1,0:T(8,128)(2,1)S(1)}, u32[]{:S(2)}, u32[]{:S(2)}) collective-permute-start(bf16[8,96,768]{2,1,0:T(8,128)(2,1)S(1)} %get-tuple-element.234), channel_id=1, source_target_pairs={{0,2},{2,0},{4,6},{6,4},{8,10},{10,8},{12,14},{14,12},{16,18},{18,... | collective-permute-start | bytes 3538952 | tf_op jit(solution)/shard_map/ppermute | solution.py:558
  72.6 11.5 %collective-permute-start.16 = (bf16[2,192,768]{2,1,0:T(8,128)(2,1)S(1)}, bf16[2,192,768]{2,1,0:T(8,128)(2,1)S(1)}, u32[]{:S(2)}, u32[]{:S(2)}) collective-permute-start(bf16[2,192,768]{2,1,0:T(8,128)(2,1)S(1)} %get-tuple-element.316), channel_id=1, source_target_pairs={{0,8},{2,6},{4,12},{6,2},{8,0},{10,14},{12,4},{14,10},{16,24},{18,... | collective-permute-start | bytes 1769480 | tf_op jit(solution)/shard_map/ppermute | solution.py:602
  74.1 8.7 %collective-permute-start.19 = (bf16[1,176,768]{2,1,0:T(8,128)(2,1)S(1)}, bf16[1,176,768]{2,1,0:T(8,128)(2,1)S(1)}, u32[]{:S(2)}, u32[]{:S(2)}) collective-permute-start(bf16[1,176,768]{2,1,0:T(8,128)(2,1)S(1)} %get-tuple-element.200), channel_id=1, source_target_pairs={{0,1},{1,0},{2,3},{3,2},{4,5},{5,4},{6,7},{7,6},{8,9},{9,8},{10,11... | collective-permute-start | bytes 811016 | tf_op jit(solution)/shard_map/ppermute | solution.py:558
  76.1 7.0 %collective-permute-start.18 = (bf16[48,768]{1,0:T(8,128)(2,1)S(1)}, bf16[48,768]{1,0:T(8,128)(2,1)S(1)}, u32[]{:S(2)}, u32[]{:S(2)}) collective-permute-start(bf16[48,768]{1,0:T(8,128)(2,1)S(1)} %pad_maximum_fusion.7), channel_id=1, source_target_pairs={{0,16},{1,17},{2,18},{3,19},{4,20},{5,21},{6,22},{7,23},{8,24},{9,... | collective-permute-start | bytes 221192 | tf_op jit(solution)/shard_map/ppermute | solution.py:558
  84.4 15.4 %collective-permute-start.20 = (bf16[1,192,768]{2,1,0:T(8,128)(2,1)S(1)}, bf16[1,192,768]{2,1,0:T(8,128)(2,1)S(1)}, u32[]{:S(2)}, u32[]{:S(2)}) collective-permute-start(bf16[1,192,768]{2,1,0:T(8,128)(2,1)S(1)} %get-tuple-element.249), channel_id=1, source_target_pairs={{0,16},{2,18},{4,20},{6,22},{8,24},{10,26},{12,28},{14,30},{16,0},... | collective-permute-start | bytes 884744 | tf_op jit(solution)/shard_map/ppermute | solution.py:602
  87.0 12.7 %collective-permute-start.21 = (bf16[4,96,768]{2,1,0:T(8,128)(2,1)S(1)}, bf16[4,96,768]{2,1,0:T(8,128)(2,1)S(1)}, u32[]{:S(2)}, u32[]{:S(2)}) collective-permute-start(bf16[4,96,768]{2,1,0:T(8,128)(2,1)S(1)} %get-tuple-element.314), channel_id=1, source_target_pairs={{0,4},{2,10},{4,0},{6,14},{8,12},{10,2},{12,8},{14,6},{16,20},{18,... | collective-permute-start | bytes 1769480 | tf_op jit(solution)/shard_map/ppermute | solution.py:602
  88.6 11.1 %collective-permute-start.22 = (bf16[64,768]{1,0:T(8,128)(2,1)S(1)}, bf16[64,768]{1,0:T(8,128)(2,1)S(1)}, u32[]{:S(2)}, u32[]{:S(2)}) collective-permute-start(bf16[64,768]{1,0:T(8,128)(2,1)S(1)} %pad_maximum_fusion.5), channel_id=1, source_target_pairs={{0,8},{1,9},{2,10},{3,11},{4,12},{5,13},{6,14},{7,15},{8,0},{9,1},... | collective-permute-start | bytes 294920 | tf_op jit(solution)/shard_map/ppermute | solution.py:558
  99.7 15.5 %collective-permute-start.23 = (bf16[1,192,768]{2,1,0:T(8,128)(2,1)S(1)}, bf16[1,192,768]{2,1,0:T(8,128)(2,1)S(1)}, u32[]{:S(2)}, u32[]{:S(2)}) collective-permute-start(bf16[1,192,768]{2,1,0:T(8,128)(2,1)S(1)} %get-tuple-element.257), channel_id=1, source_target_pairs={{0,16},{2,18},{4,20},{6,22},{8,24},{10,26},{12,28},{14,30},{16,0},... | collective-permute-start | bytes 884744 | tf_op jit(solution)/shard_map/ppermute | solution.py:602
  99.9 15.4 %collective-permute-start.24 = (bf16[2,96,768]{2,1,0:T(8,128)(2,1)S(1)}, bf16[2,96,768]{2,1,0:T(8,128)(2,1)S(1)}, u32[]{:S(2)}, u32[]{:S(2)}) collective-permute-start(bf16[2,96,768]{2,1,0:T(8,128)(2,1)S(1)} %get-tuple-element.322), channel_id=1, source_target_pairs={{0,8},{2,6},{4,12},{6,2},{8,0},{10,14},{12,4},{14,10},{16,24},{18,... | collective-permute-start | bytes 884744 | tf_op jit(solution)/shard_map/ppermute | solution.py:602
  101.8 6.7 %collective-permute-start.25 = (bf16[96,768]{1,0:T(8,128)(2,1)S(1)}, bf16[96,768]{1,0:T(8,128)(2,1)S(1)}, u32[]{:S(2)}, u32[]{:S(2)}) collective-permute-start(bf16[96,768]{1,0:T(8,128)(2,1)S(1)} %pad_maximum_fusion.4), channel_id=1, source_target_pairs={{0,4},{1,5},{2,6},{3,7},{4,0},{5,1},{6,2},{7,3},{8,12},{9,13},{10,... | collective-permute-start | bytes 442376 | tf_op jit(solution)/shard_map/ppermute | solution.py:558
  115.4 16.6 %collective-permute-start.26 = (bf16[2,192,768]{2,1,0:T(8,128)(2,1)S(1)}, bf16[2,192,768]{2,1,0:T(8,128)(2,1)S(1)}, u32[]{:S(2)}, u32[]{:S(2)}) collective-permute-start(bf16[2,192,768]{2,1,0:T(8,128)(2,1)S(1)} %pad_maximum_fusion.1), channel_id=1, source_target_pairs={{0,8},{2,6},{4,12},{6,2},{8,0},{10,14},{12,4},{14,10},{16,24},{18,... | collective-permute-start | bytes 1769480 | tf_op jit(solution)/shard_map/ppermute | solution.py:602
  115.6 16.5 %collective-permute-start.27 = (bf16[2,96,768]{2,1,0:T(8,128)(2,1)S(1)}, bf16[2,96,768]{2,1,0:T(8,128)(2,1)S(1)}, u32[]{:S(2)}, u32[]{:S(2)}) collective-permute-start(bf16[2,96,768]{2,1,0:T(8,128)(2,1)S(1)} %add_convert_fusion.8), channel_id=1, source_target_pairs={{0,16},{2,18},{4,20},{6,22},{8,24},{10,26},{12,28},{14,30},{16,0},... | collective-permute-start | bytes 884744 | tf_op jit(solution)/shard_map/ppermute | solution.py:602
  118.6 8.9 %collective-permute-start.28 = (bf16[160,768]{1,0:T(8,128)(2,1)S(1)}, bf16[160,768]{1,0:T(8,128)(2,1)S(1)}, u32[]{:S(2)}, u32[]{:S(2)}) collective-permute-start(bf16[160,768]{1,0:T(8,128)(2,1)S(1)} %pad_maximum_fusion.2), channel_id=1, source_target_pairs={{0,1},{1,0},{2,3},{3,2},{4,5},{5,4},{6,7},{7,6},{8,9},{9,8},{10,11... | collective-permute-start | bytes 737288 | tf_op jit(solution)/shard_map/ppermute | solution.py:558
  119.2 8.4 %collective-permute-start.29 = (bf16[160,768]{1,0:T(8,128)(2,1)S(1)}, bf16[160,768]{1,0:T(8,128)(2,1)S(1)}, u32[]{:S(2)}, u32[]{:S(2)}) collective-permute-start(bf16[160,768]{1,0:T(8,128)(2,1)S(1)} %pad_maximum_fusion.2), channel_id=1, source_target_pairs={{0,2},{1,3},{2,0},{3,1},{4,6},{5,7},{6,4},{7,5},{8,10},{9,11},{10,... | collective-permute-start | bytes 737288 | tf_op jit(solution)/shard_map/ppermute | solution.py:558
  119.2 9.1 %collective-permute-start.30 = (bf16[160,768]{1,0:T(8,128)(2,1)S(1)}, bf16[160,768]{1,0:T(8,128)(2,1)S(1)}, u32[]{:S(2)}, u32[]{:S(2)}) collective-permute-start(bf16[160,768]{1,0:T(8,128)(2,1)S(1)} %pad_maximum_fusion.2), channel_id=1, source_target_pairs={{0,3},{1,2},{2,1},{3,0},{4,7},{5,6},{6,5},{7,4},{8,11},{9,10},{10,... | collective-permute-start | bytes 737288 | tf_op jit(solution)/shard_map/ppermute | solution.py:558
  132.2 18.8 %collective-permute-start.31 = (bf16[4,192,768]{2,1,0:T(8,128)(2,1)S(1)}, bf16[4,192,768]{2,1,0:T(8,128)(2,1)S(1)}, u32[]{:S(2)}, u32[]{:S(2)}) collective-permute-start(bf16[4,192,768]{2,1,0:T(8,128)(2,1)S(1)} %constant_dynamic-update-slice_fusion), channel_id=1, source_target_pairs={{0,4},{2,10},{4,0},{6,14},{8,12},{10,2},{12,8},{14,6},{16,20},{18,... | collective-permute-start | bytes 3538952 | tf_op jit(solution)/shard_map/ppermute | solution.py:602
  133.8 10.0 %collective-permute-start.32 = (bf16[2,96,768]{2,1,0:T(8,128)(2,1)S(1)}, bf16[2,96,768]{2,1,0:T(8,128)(2,1)S(1)}, u32[]{:S(2)}, u32[]{:S(2)}) collective-permute-start(bf16[2,96,768]{2,1,0:T(8,128)(2,1)S(1)} %add_convert_fusion.7), channel_id=1, source_target_pairs={{0,8},{2,6},{4,12},{6,2},{8,0},{10,14},{12,4},{14,10},{16,24},{18,... | collective-permute-start | bytes 884744 | tf_op jit(solution)/shard_map/ppermute | solution.py:602
  151.2 9.9 %collective-permute-start.34 = (bf16[4,96,768]{2,1,0:T(8,128)(2,1)S(1)}, bf16[4,96,768]{2,1,0:T(8,128)(2,1)S(1)}, u32[]{:S(2)}, u32[]{:S(2)}) collective-permute-start(bf16[4,96,768]{2,1,0:T(8,128)(2,1)S(1)} %constant_dynamic-update-slice_fusion.4), channel_id=1, source_target_pairs={{0,4},{2,10},{4,0},{6,14},{8,12},{10,2},{12,8},{14,6},{16,20},{18,... | collective-permute-start | bytes 1769480 | tf_op jit(solution)/shard_map/ppermute | solution.py:602
  (25 other events, 143.2 us)

commit v3 on v2

--- a/solution.py
+++ b/solution.py
@@ -693,7 +693,7 @@
     x0, x1 = gather_halves(patches, "tensor")
     g0, g1 = gather_halves(out_grad, "tensor")
 
-    proto_step = min(512, protos)
+    proto_step = min(1024, protos)
     crop_bits = bits_of(groups)[1:]
     crop_rows = -(-group_crops // 8) * 8
     crop_shape = (groups // 2, crop_rows, width)
@@ -760,7 +760,7 @@
         (ids, score_grad, prototypes),
         "crop_grads",
         2 * score_grad.shape[0] * protos * width,
-        16,
+        24,
     )
     crop_other = swap(tie(crop_send, x1), "dp", 1)
     tables = call(
@@ -781,7 +781,7 @@
     b0 = swap(a0, "tensor", 1)
     crop_held = crop_step(*crop_held, crop_bits[1], a0)
     xf1, h1_1, qkv1, pt1, ot1, a1 = attend(half, x1, tie(ids, crop_held[0]))
-    b1 = swap(tie(a1, b0, g1), "tensor", 1)
+    b1 = swap(a1, "tensor", 1)
     if parts > 2:
         a_all, b_all = sum_halves(jnp.concatenate([a0, a1]), "tensor")
         a0, a1, b0, b1 = a_all[:half], a_all[half:], b_all[:half], b_all[half:]
@@ -930,12 +930,12 @@
         2 * all_rows * hidden * width,
         16,
     )[0]
-    sent_a = add_low(tie(keep_a[cut:], z_part), tie(core_high, z_part))
+    sent_a = add_low(keep_a[cut:], core_high)
     other_a = mixed_swap(sent_a, list(zip(*orders_a))[0])
     _, gh1_far, ga1, gq1, sums1, qb1, tt1 = attend_back(
         half, gh2_far, near_other, xf1, qkv1, pt1, tie(ids, sent_a)
     )
-    gh1_far, far_other, core_low = lax.optimization_barrier((gh1_far, far_other, core_low))
+    gh1_far, core_low = lax.optimization_barrier((gh1_far, core_low))
     kept_a = add_low(tie(keep_a[:cut], gh1_far), core_low)
     z0, z1 = scatter_halves(tie(z_part, gh1_far), "tensor")
     g_own, gh1_near, ga0, gq0, sums0, qb0, tt0 = attend_back(
@@ -1046,7 +1046,7 @@
             0,
             24,
         )
-        steps = [[b * parts] for b in bits_of(groups)[:0:-1]]
+        steps = [[b * parts] for b in (bits_of(groups)[:2:-1] + bits_of(groups)[1:3])]
         steps += [[1, parts]] if parts == 2 else [[b] for b in [*bits_of(parts), parts]]
         weights = [weight for step in steps for weight in step]
         pooled = pooled[0]

time: 167 us -> 164 us (0.982)
    ppermute x11, waiting for transfers between devices: 21.9 us -> 16.3 us  [mixed_swap(): return lax.ppermute(v, 'dp', [(i, i ^ bits[i & 1]) for i in range(size)])]
    ppermute x25, waiting for transfers between devices: 41.1 us -> 45.1 us  [swap(): return lax.ppermute(v, axis, partner(axis, bit))]
    ppermute x25, starting transfers between devices: 22.1 us -> 25.5 us  [swap(): return lax.ppermute(v, axis, partner(axis, bit))]
    ppermute x11, starting transfers between devices: 14.7 us -> 11.4 us  [mixed_swap(): return lax.ppermute(v, 'dp', [(i, i ^ bits[i & 1]) for i in range(size)])]
  transfers between devices with their start and end apart: 36 -> 36, of which waited for: 21 -> 21; matrix products, arithmetic and copies ran while one was open for 2% -> 1% of each run, Pallas kernels for 31% -> 31%
where the time goes in v3:
time: 164 us
  waiting for transfers between devices  61.4 us (37%)
  Pallas kernels  57 us (35%)
  starting transfers between devices  36.9 us (22%)
  local copies, waits for them, and re-layouts  4.95 us (3%)
  other arithmetic  2.46 us (2%)
    pallas_call x14, Pallas kernels, call(): pl.pallas_call(body, grid_spec=pltpu.PrefetchScalarGridSpec(num_scalar_pr...  45.4 us
    ppermute x25, waiting for transfers between devices, swap(): return lax.ppermute(v, axis, partner(axis, bit))  45.1 us
    ppermute x25, starting transfers between devices, swap(): return lax.ppermute(v, axis, partner(axis, bit))  25.5 us
    ppermute x11, waiting for transfers between devices, mixed_swap(): return lax.ppermute(v, 'dp', [(i, i ^ bits[i & 1]) for i in range(size)])  16.3 us
    pallas_call x4, Pallas kernels, unpack(): pl.pallas_call(functools.partial(unpack_kernel, layout, own), grid_spec=p...  11.6 us
    ppermute x11, starting transfers between devices, mixed_swap(): return lax.ppermute(v, 'dp', [(i, i ^ bits[i & 1]) for i in range(size)])  11.4 us
    unnamed x46, local copies, waits for them, and re-layouts  4.33 us
  transfers between devices with their start and end apart: 36, of which 21 were waited for; matrix products, arithmetic and copies ran while one was open for 1% of the time, Pallas kernels for 31%

profile of v3, /device:TPU:0, one launch (start us, length us, event | category | flops | bytes accessed | tf_op | source)
XLA Modules:
  0.0 164.2 jit_solution(7648885500928086507)
XLA Ops:
  0.6 3.0 %collective-permute-start = (bf16[1,170,768]{2,1,0:T(8,128)(2,1)}, bf16[1,170,768]{2,1,0:T(8,128)(2,1)S(1)}, u32[]{:S(2)}, u32[]{:S(2)}) collective-permute-start(bf16[1,170,768]{2,1,0:T(8,128)(2,1)} %bitcast.24), channel_id=1, source_target_pairs={{0,1},{1,0},{2,3},{3,2},{4,5},{5,4},{6,7},{7,6},{8,9},{9,8},{10,11... | collective-permute-start | bytes 783368 | tf_op jit(solution)/shard_map/ppermute | solution.py:558
  3.8 1.9 %copy-done.1 = bf16[2048,768]{1,0:T(8,128)(2,1)S(1)} copy-done((bf16[2048,768]{1,0:T(8,128)(2,1)S(1)}, bf16[2048,768]{1,0:T(8,128)(2,1)}, u32[]{:S(2)}) %copy-start.1) | copy-done | bytes 3145752
  7.0 2.9 %crop_grads.1 = (f32[8,24,768]{2,1,0:T(8,128)S(1)}, f32[8,24,768]{2,1,0:T(8,128)S(1)}) custom-call(s32[3]{0:T(128)S(1)} %pad_add_fusion.ids, bf16[320,2048]{1,0:T(8,128)(2,1)S(1)} %copy-done.5, bf16[2048,768]{1,0:T(8,128)(2,1)S(1)} %copy-done.1), custom_call_target="tpu_custom_call" | custom-call | flops 10066329 | bytes 56361 | tf_op jit(solution)/shard_map/crop_grads/pallas_call | solution.py:82
  10.4 1.7 %collective-permute-start.2 = (bf16[1,170,768]{2,1,0:T(8,128)(2,1)S(1)}, bf16[1,170,768]{2,1,0:T(8,128)(2,1)S(1)}, u32[]{:S(2)}, u32[]{:S(2)}) collective-permute-start(bf16[1,170,768]{2,1,0:T(8,128)(2,1)S(1)} %bitcast.26), channel_id=1, source_target_pairs={{0,1},{1,0},{2,3},{3,2},{4,5},{5,4},{6,7},{7,6},{8,9},{9,8},{10,11... | collective-permute-start | bytes 783368 | tf_op jit(solution)/shard_map/ppermute | solution.py:558
  15.5 4.9 %attend.2 = (bf16[1,176,768]{2,1,0:T(8,128)(2,1)S(1)}, bf16[1,176,768]{2,1,0:T(8,128)(2,1)S(1)}, bf16[1,1152,176]{2,1,0:T(8,128)(2,1)S(1)}, bf16[1,12,176,176]{3...) custom-call(s32[3]{0:T(128)S(1)} %pad_add_fusion.ids, s32[20]{0:T(128)S(1)} %copy-done.13, ...), custom_call_target="tpu_custom_call" | custom-call | flops 4152360 | bytes 53146 | tf_op jit(solution)/shard_map/attend/pallas_call | solution.py:82
  22.8 5.0 %attend.3 = (bf16[1,176,768]{2,1,0:T(8,128)(2,1)S(1)}, bf16[1,176,768]{2,1,0:T(8,128)(2,1)S(1)}, bf16[1,1152,176]{2,1,0:T(8,128)(2,1)S(1)}, bf16[1,12,176,176]{3...) custom-call(s32[3]{0:T(128)S(1)} %pad_add_fusion.ids, s32[20]{0:T(128)S(1)} %copy-done.13, ...), custom_call_target="tpu_custom_call" | custom-call | flops 4152360 | bytes 53146 | tf_op jit(solution)/shard_map/attend/pallas_call | solution.py:82
  29.4 2.7 %collective-permute-start.7 = (bf16[1,24,768]{2,1,0:T(8,128)(2,1)S(1)}, bf16[1,24,768]{2,1,0:T(8,128)(2,1)S(1)}, u32[]{:S(2)}, u32[]{:S(2)}) collective-permute-start(bf16[1,24,768]{2,1,0:T(8,128)(2,1)S(1)} %get-tuple-element.319), channel_id=1, source_target_pairs={{0,16},{1,17},{2,18},{3,19},{4,20},{5,21},{6,22},{7,23},{8,24},{9,... | collective-permute-start | bytes 110600 | tf_op jit(solution)/shard_map/ppermute | solution.py:558
  34.6 2.7 %collective-permute-done.8.rest_2_ = bf16[1,24,768]{2,1,0:T(8,128)(2,1)S(1)} collective-permute-done((bf16[1,24,768]{2,1,0:T(8,128)(2,1)S(1)}, bf16[1,24,768]{2,1,0:T(8,128)(2,1)S(1)}, u32[]{:S(2)}, u32[]{:S(2)}) %collective-permute-start.8) | collective-permute-done | bytes 36896 | tf_op jit(solution)/shard_map/ppermute | solution.py:558
  38.7 4.3 %hidden.1 = (f32[2,176,768]{2,1,0:T(8,128)S(1)}, f32[2,176,768]{2,1,0:T(8,128)S(1)}, bf16[352,768]{1,0:T(8,128)(2,1)S(1)}, bf16[352,768]{1,0:T(8,128)(2,1)S(1)},...) custom-call(s32[3]{0:T(128)S(1)} %pad_add_fusion.ids, ...), custom_call_target="tpu_custom_call" | custom-call | flops 24914164 | bytes 130192 | tf_op jit(solution)/shard_map/hidden/pallas_call | solution.py:82
  44.6 3.2 %hidden_grads.1 = (bf16[8,192,768]{2,1,0:T(8,128)(2,1)S(1)}, bf16[8,192,768]{2,1,0:T(8,128)(2,1)S(1)}) custom-call(s32[3]{0:T(128)S(1)} %pad_add_fusion.ids, bf16[352,768]{1,0:T(8,128)(2,1)S(1)} %get-tuple-element.177.h2, bf16[352,768]{1,0:T(8,128)(2,1)S(1)} %get-tuple-element.178.gz, bf16[352,1536]{1,0:T(8,128)(2,1)S(1)} %get-tuple-element.217.m, ...), custom_call_target="tpu_custom_call" | custom-call | flops 16609443 | bytes 79626 | tf_op jit(solution)/shard_map/hidden_grads/pallas_call | solution.py:82
  47.7 1.8 %collective-permute-done.10.e1 = bf16[1,176,768]{2,1,0:T(8,128)(2,1)S(1)} collective-permute-done((bf16[1,176,768]{2,1,0:T(8,128)(2,1)S(1)}, bf16[1,176,768]{2,1,0:T(8,128)(2,1)S(1)}, u32[]{:S(2)}, u32[]{:S(2)}) %collective-permute-start.10) | collective-permute-done | bytes 270368 | tf_op jit(solution)/shard_map/ppermute | solution.py:558
  50.3 2.3 %collective-permute-done.11 = bf16[4,192,768]{2,1,0:T(8,128)(2,1)S(1)} collective-permute-done((bf16[4,192,768]{2,1,0:T(8,128)(2,1)S(1)}, bf16[4,192,768]{2,1,0:T(8,128)(2,1)S(1)}, u32[]{:S(2)}, u32[]{:S(2)}) %collective-permute-start.11) | collective-permute-done | bytes 1179680 | tf_op jit(solution)/shard_map/ppermute | solution.py:558
  56.9 5.8 %attend_back.2 = (f32[1,176,768]{2,1,0:T(8,128)}, bf16[1,176,768]{2,1,0:T(8,128)(2,1)S(1)}, bf16[1,176,768]{2,1,0:T(8,128)(2,1)S(1)}, bf16[1,1152,176]{2,1,0:T(8...) custom-call(s32[3]{0:T(128)S(1)} %pad_add_fusion.ids, s32[20]{0:T(128)S(1)} %copy-done.13, ...), custom_call_target="tpu_custom_call" | custom-call | flops 8304721 | bytes 86231 | tf_op jit(solution)/shard_map/attend_back/pallas_call | solution.py:82
  63.5 5.6 %attend_back.3 = (f32[1,176,768]{2,1,0:T(8,128)S(1)}, bf16[1,176,768]{2,1,0:T(8,128)(2,1)S(1)}, bf16[1,176,768]{2,1,0:T(8,128)(2,1)S(1)}, bf16[1,1152,176]{2,1,0...) custom-call(s32[3]{0:T(128)S(1)} %pad_add_fusion.ids, s32[20]{0:T(128)S(1)} %copy-done.13, ...), custom_call_target="tpu_custom_call" | custom-call | flops 8304721 | bytes 86231 | tf_op jit(solution)/shard_map/attend_back/pallas_call | solution.py:82
  69.5 2.1 %attend_grads.1 = (bf16[8,96,768]{2,1,0:T(8,128)(2,1)S(1)}, bf16[8,96,768]{2,1,0:T(8,128)(2,1)S(1)}, f32[16,768]{1,0:T(8,128)S(1)}) custom-call(s32[3]{0:T(128)S(1)} %pad_add_fusion.ids, bf16[1,384,176]{2,1,0:T(8,128)(2,1)S(1)} %get-tuple-element.195.o0, bf16[1,384,176]{2,1,0:T(8,128)(2,1)S(1)} %get-tuple-element.196.o1, ...), custom_call_target="tpu_custom_call" | custom-call | flops 8304721 | bytes 58828 | tf_op jit(solution)/shard_map/attend_grads/pallas_call | solution.py:82
  74.9 2.0 %collective-permute-start.18 = (bf16[48,768]{1,0:T(8,128)(2,1)S(1)}, bf16[48,768]{1,0:T(8,128)(2,1)S(1)}, u32[]{:S(2)}, u32[]{:S(2)}) collective-permute-start(bf16[48,768]{1,0:T(8,128)(2,1)S(1)} %pad_maximum_fusion.7), channel_id=1, source_target_pairs={{0,16},{1,17},{2,18},{3,19},{4,20},{5,21},{6,22},{7,23},{8,24},{9,... | collective-permute-start | bytes 221192 | tf_op jit(solution)/shard_map/ppermute | solution.py:558
  77.0 4.3 %collective-permute-done.19.e1 = bf16[1,176,768]{2,1,0:T(8,128)(2,1)S(1)} collective-permute-done((bf16[1,176,768]{2,1,0:T(8,128)(2,1)S(1)}, bf16[1,176,768]{2,1,0:T(8,128)(2,1)S(1)}, u32[]{:S(2)}, u32[]{:S(2)}) %collective-permute-start.19) | collective-permute-done | bytes 270368 | tf_op jit(solution)/shard_map/ppermute | solution.py:558
  81.7 1.8 %collective-permute-done.16 = bf16[2,192,768]{2,1,0:T(8,128)(2,1)S(1)} collective-permute-done((bf16[2,192,768]{2,1,0:T(8,128)(2,1)S(1)}, bf16[2,192,768]{2,1,0:T(8,128)(2,1)S(1)}, u32[]{:S(2)}, u32[]{:S(2)}) %collective-permute-start.16) | collective-permute-done | bytes 589856 | tf_op jit(solution)/shard_map/ppermute | solution.py:602
  83.7 1.8 %collective-permute-start.20 = (bf16[1,192,768]{2,1,0:T(8,128)(2,1)S(1)}, bf16[1,192,768]{2,1,0:T(8,128)(2,1)S(1)}, u32[]{:S(2)}, u32[]{:S(2)}) collective-permute-start(bf16[1,192,768]{2,1,0:T(8,128)(2,1)S(1)} %get-tuple-element.241), channel_id=1, source_target_pairs={{0,16},{2,18},{4,20},{6,22},{8,24},{10,26},{12,28},{14,30},{16,0},... | collective-permute-start | bytes 884744 | tf_op jit(solution)/shard_map/ppermute | solution.py:602
  89.2 7.6 %collective-permute-done.22 = bf16[64,768]{1,0:T(8,128)(2,1)S(1)} collective-permute-done((bf16[64,768]{1,0:T(8,128)(2,1)S(1)}, bf16[64,768]{1,0:T(8,128)(2,1)S(1)}, u32[]{:S(2)}, u32[]{:S(2)}) %collective-permute-start.22) | collective-permute-done | bytes 98336 | tf_op jit(solution)/shard_map/ppermute | solution.py:558
  98.3 2.8 %collective-permute-start.24 = (bf16[2,96,768]{2,1,0:T(8,128)(2,1)S(1)}, bf16[2,96,768]{2,1,0:T(8,128)(2,1)S(1)}, u32[]{:S(2)}, u32[]{:S(2)}) collective-permute-start(bf16[2,96,768]{2,1,0:T(8,128)(2,1)S(1)} %get-tuple-element.312), channel_id=1, source_target_pairs={{0,8},{2,6},{4,12},{6,2},{8,0},{10,14},{12,4},{14,10},{16,24},{18,... | collective-permute-start | bytes 884744 | tf_op jit(solution)/shard_map/ppermute | solution.py:602
  101.4 13.9 %collective-permute-done.25 = bf16[96,768]{1,0:T(8,128)(2,1)S(1)} collective-permute-done((bf16[96,768]{1,0:T(8,128)(2,1)S(1)}, bf16[96,768]{1,0:T(8,128)(2,1)S(1)}, u32[]{:S(2)}, u32[]{:S(2)}) %collective-permute-start.25) | collective-permute-done | bytes 147488 | tf_op jit(solution)/shard_map/ppermute | solution.py:558
  117.6 1.9 %collective-permute-start.30 = (bf16[160,768]{1,0:T(8,128)(2,1)S(1)}, bf16[160,768]{1,0:T(8,128)(2,1)S(1)}, u32[]{:S(2)}, u32[]{:S(2)}) collective-permute-start(bf16[160,768]{1,0:T(8,128)(2,1)S(1)} %pad_maximum_fusion.2), channel_id=1, source_target_pairs={{0,3},{1,2},{2,1},{3,0},{4,7},{5,6},{6,5},{7,4},{8,11},{9,10},{10,... | collective-permute-start | bytes 737288 | tf_op jit(solution)/shard_map/ppermute | solution.py:558
  119.6 6.7 %collective-permute-done.28 = bf16[160,768]{1,0:T(8,128)(2,1)S(1)} collective-permute-done((bf16[160,768]{1,0:T(8,128)(2,1)S(1)}, bf16[160,768]{1,0:T(8,128)(2,1)S(1)}, u32[]{:S(2)}, u32[]{:S(2)}) %collective-permute-start.28) | collective-permute-done | bytes 245792 | tf_op jit(solution)/shard_map/ppermute | solution.py:558
  127.4 2.9 %collective-permute-done.27 = bf16[2,96,768]{2,1,0:T(8,128)(2,1)S(1)} collective-permute-done((bf16[2,96,768]{2,1,0:T(8,128)(2,1)S(1)}, bf16[2,96,768]{2,1,0:T(8,128)(2,1)S(1)}, u32[]{:S(2)}, u32[]{:S(2)}) %collective-permute-start.27) | collective-permute-done | bytes 294944 | tf_op jit(solution)/shard_map/ppermute | solution.py:602
  135.1 5.8 %proto_grads.1 = f32[2048,768]{1,0:T(8,128)} custom-call(s32[3]{0:T(128)S(1)} %pad_add_fusion.ids, bf16[320,2048]{1,0:T(8,128)(2,1)S(1)} %copy-done.6, bf16[512,768]{1,0:T(8,128)(2,1)S(1)} %pad_maximum_fusion.pooled, bf16[2048,768]{1,0:T(8,128)(2,1)S(1)} %copy-done.2, s32[1,2048]{1,0:T(1,128)S(1)} %bitcast.31), custom_call_target="tpu_custom_call" | custom-call | flops 10066329 | bytes 115425 | tf_op jit(solution)/shard_map/proto_grads/pallas_call | solution.py:82
  140.8 2.4 %collective-permute-done.32 = bf16[2,96,768]{2,1,0:T(8,128)(2,1)S(1)} collective-permute-done((bf16[2,96,768]{2,1,0:T(8,128)(2,1)S(1)}, bf16[2,96,768]{2,1,0:T(8,128)(2,1)S(1)}, u32[]{:S(2)}, u32[]{:S(2)}) %collective-permute-start.32) | collective-permute-done | bytes 294944 | tf_op jit(solution)/shard_map/ppermute | solution.py:602
  143.2 5.5 %collective-permute-done.31 = bf16[4,192,768]{2,1,0:T(8,128)(2,1)S(1)} collective-permute-done((bf16[4,192,768]{2,1,0:T(8,128)(2,1)S(1)}, bf16[4,192,768]{2,1,0:T(8,128)(2,1)S(1)}, u32[]{:S(2)}, u32[]{:S(2)}) %collective-permute-start.31) | collective-permute-done | bytes 1179680 | tf_op jit(solution)/shard_map/ppermute | solution.py:602
  149.8 2.9 %unpack_hidden_own.1 = (f32[768,1536]{1,0:T(8,128)}, f32[1536,768]{1,0:T(8,128)}) custom-call(s32[17]{0:T(128)S(1)} %pad_add_fusion.1.places, bf16[8,192,768]{2,1,0:T(8,128)(2,1)S(1)} %constant_dynamic-update-slice_fusion.2.held), custom_call_target="tpu_custom_call" | custom-call | tf_op jit(solution)/shard_map/unpack_hidden_own/pallas_call | solution.py:613
  153.6 4.5 %unpack_hidden_other.1 = (f32[768,1536]{1,0:T(8,128)}, f32[1536,768]{1,0:T(8,128)}) custom-call(s32[17]{0:T(128)S(1)} %pad_add_fusion.1.places, bf16[8,192,768]{2,1,0:T(8,128)(2,1)} %collective-permute-done.33.held, f32[768,1536]{1,0:T(8,128)} %get-tuple-element.278.refs_0_, ...), custom_call_target="tpu_custom_call", output_to_operand_aliasing={{0}: (2, {}), {1}: (3, {})} | custom-call | tf_op jit(solution)/shard_map/unpack_hidden_other/pallas_call | solution.py:613
  159.1 2.1 %unpack_attend_own.1 = (f32[384,768]{1,0:T(8,128)}, f32[1152,768]{1,0:T(8,128)}) custom-call(s32[17]{0:T(128)S(1)} %pad_add_fusion.1.places, bf16[8,96,768]{2,1,0:T(8,128)(2,1)S(1)} %constant_dynamic-update-slice_fusion.6.held), custom_call_target="tpu_custom_call" | custom-call | tf_op jit(solution)/shard_map/unpack_attend_own/pallas_call | solution.py:613
  162.0 2.1 %unpack_attend_other.1 = (f32[384,768]{1,0:T(8,128)}, f32[1152,768]{1,0:T(8,128)}) custom-call(s32[17]{0:T(128)S(1)} %pad_add_fusion.1.places, bf16[8,96,768]{2,1,0:T(8,128)(2,1)S(1)} %collective-permute-done.35.held, f32[384,768]{1,0:T(8,128)} %get-tuple-element.286.refs_0_, ...), custom_call_target="tpu_custom_call", output_to_operand_aliasing={{0}: (2, {}), {1}: (3, {})} | custom-call | tf_op jit(solution)/shard_map/unpack_attend_other/pallas_call | solution.py:613
  (159 shorter events, 41.6 us)
Async XLA Ops:
  0.6 9.7 %collective-permute-start = (bf16[1,170,768]{2,1,0:T(8,128)(2,1)}, bf16[1,170,768]{2,1,0:T(8,128)(2,1)S(1)}, u32[]{:S(2)}, u32[]{:S(2)}) collective-permute-start(bf16[1,170,768]{2,1,0:T(8,128)(2,1)} %bitcast.24), channel_id=1, source_target_pairs={{0,1},{1,0},{2,3},{3,2},{4,5},{5,4},{6,7},{7,6},{8,9},{9,8},{10,11... | collective-permute-start | bytes 783368 | tf_op jit(solution)/shard_map/ppermute | solution.py:558
  10.4 10.1 %collective-permute-start.2 = (bf16[1,170,768]{2,1,0:T(8,128)(2,1)S(1)}, bf16[1,170,768]{2,1,0:T(8,128)(2,1)S(1)}, u32[]{:S(2)}, u32[]{:S(2)}) collective-permute-start(bf16[1,170,768]{2,1,0:T(8,128)(2,1)S(1)} %bitcast.26), channel_id=1, source_target_pairs={{0,1},{1,0},{2,3},{3,2},{4,5},{5,4},{6,7},{7,6},{8,9},{9,8},{10,11... | collective-permute-start | bytes 783368 | tf_op jit(solution)/shard_map/ppermute | solution.py:558
  13.8 6.6 %collective-permute-start.3 = (bf16[4,24,768]{2,1,0:T(8,128)(2,1)S(1)}, bf16[4,24,768]{2,1,0:T(8,128)(2,1)S(1)}, u32[]{:S(2)}, u32[]{:S(2)}) collective-permute-start(bf16[4,24,768]{2,1,0:T(8,128)(2,1)S(1)} %slice.217), channel_id=1, source_target_pairs={{0,4},{2,6},{4,0},{6,2},{8,12},{10,14},{12,8},{14,10},{16,20},{18,... | collective-permute-start | bytes 442376 | tf_op jit(solution)/shard_map/ppermute | solution.py:558
  20.5 8.8 %collective-permute-start.6 = (bf16[2,24,768]{2,1,0:T(8,128)(2,1)S(1)}, bf16[2,24,768]{2,1,0:T(8,128)(2,1)S(1)}, u32[]{:S(2)}, u32[]{:S(2)}) collective-permute-start(bf16[2,24,768]{2,1,0:T(8,128)(2,1)S(1)} %slice.218), channel_id=1, source_target_pairs={{0,8},{2,10},{4,12},{6,14},{8,0},{10,2},{12,4},{14,6},{16,24},{18,... | collective-permute-start | bytes 221192 | tf_op jit(solution)/shard_map/ppermute | solution.py:558
  22.2 16.5 %collective-permute-start.4 = (bf16[1,176,768]{2,1,0:T(8,128)(2,1)S(1)}, bf16[1,176,768]{2,1,0:T(8,128)(2,1)S(1)}, u32[]{:S(2)}, u32[]{:S(2)}) collective-permute-start(bf16[1,176,768]{2,1,0:T(8,128)(2,1)S(1)} %get-tuple-element.167.a0), channel_id=1, source_target_pairs={{0,1},{1,0},{2,3},{3,2},{4,5},{5,4},{6,7},{7,6},{8,9},{9,8},{10,11... | collective-permute-start | bytes 811016 | tf_op jit(solution)/shard_map/ppermute | solution.py:558
  27.8 10.8 %collective-permute-start.5 = (bf16[1,176,768]{2,1,0:T(8,128)(2,1)S(1)}, bf16[1,176,768]{2,1,0:T(8,128)(2,1)S(1)}, u32[]{:S(2)}, u32[]{:S(2)}) collective-permute-start(bf16[1,176,768]{2,1,0:T(8,128)(2,1)S(1)} %get-tuple-element.172.a1), channel_id=1, source_target_pairs={{0,1},{1,0},{2,3},{3,2},{4,5},{5,4},{6,7},{7,6},{8,9},{9,8},{10,11... | collective-permute-start | bytes 811016 | tf_op jit(solution)/shard_map/ppermute | solution.py:558
  29.4 5.2 %collective-permute-start.7 = (bf16[1,24,768]{2,1,0:T(8,128)(2,1)S(1)}, bf16[1,24,768]{2,1,0:T(8,128)(2,1)S(1)}, u32[]{:S(2)}, u32[]{:S(2)}) collective-permute-start(bf16[1,24,768]{2,1,0:T(8,128)(2,1)S(1)} %get-tuple-element.319), channel_id=1, source_target_pairs={{0,16},{1,17},{2,18},{3,19},{4,20},{5,21},{6,22},{7,23},{8,24},{9,... | collective-permute-start | bytes 110600 | tf_op jit(solution)/shard_map/ppermute | solution.py:558
  32.0 5.3 %collective-permute-start.8 = (bf16[1,24,768]{2,1,0:T(8,128)(2,1)S(1)}, bf16[1,24,768]{2,1,0:T(8,128)(2,1)S(1)}, u32[]{:S(2)}, u32[]{:S(2)}) collective-permute-start(bf16[1,24,768]{2,1,0:T(8,128)(2,1)S(1)} %get-tuple-element.318), channel_id=1, source_target_pairs={{0,1},{1,0},{2,3},{3,2},{4,5},{5,4},{6,7},{7,6},{8,9},{9,8},{10,11... | collective-permute-start | bytes 110600 | tf_op jit(solution)/shard_map/ppermute | solution.py:558
  32.6 6.0 %collective-permute-start.9 = (bf16[1,24,768]{2,1,0:T(8,128)(2,1)S(1)}, bf16[1,24,768]{2,1,0:T(8,128)(2,1)S(1)}, u32[]{:S(2)}, u32[]{:S(2)}) collective-permute-start(bf16[1,24,768]{2,1,0:T(8,128)(2,1)S(1)} %get-tuple-element.319), channel_id=1, source_target_pairs={{0,17},{1,16},{2,19},{3,18},{4,21},{5,20},{6,23},{7,22},{8,25},{9,... | collective-permute-start | bytes 110600 | tf_op jit(solution)/shard_map/ppermute | solution.py:558
  43.0 6.5 %collective-permute-start.10 = (bf16[1,176,768]{2,1,0:T(8,128)(2,1)S(1)}, bf16[1,176,768]{2,1,0:T(8,128)(2,1)S(1)}, u32[]{:S(2)}, u32[]{:S(2)}) collective-permute-start(bf16[1,176,768]{2,1,0:T(8,128)(2,1)S(1)} %get-tuple-element.183.e0), channel_id=1, source_target_pairs={{0,1},{1,0},{2,3},{3,2},{4,5},{5,4},{6,7},{7,6},{8,9},{9,8},{10,11... | collective-permute-start | bytes 811016 | tf_op jit(solution)/shard_map/ppermute | solution.py:558
  49.8 12.9 %collective-permute-start.12 = (bf16[4,192,768]{2,1,0:T(8,128)(2,1)S(1)}, bf16[4,192,768]{2,1,0:T(8,128)(2,1)S(1)}, u32[]{:S(2)}, u32[]{:S(2)}) collective-permute-start(bf16[4,192,768]{2,1,0:T(8,128)(2,1)S(1)} %get-tuple-element.310), channel_id=1, source_target_pairs={{0,2},{2,0},{4,6},{6,4},{8,10},{10,8},{12,14},{14,12},{16,18},{18,... | collective-permute-start | bytes 3538952 | tf_op jit(solution)/shard_map/ppermute | solution.py:558
  52.9 16.6 %collective-permute-start.13 = (bf16[4,192,768]{2,1,0:T(8,128)(2,1)S(1)}, bf16[4,192,768]{2,1,0:T(8,128)(2,1)S(1)}, u32[]{:S(2)}, u32[]{:S(2)}) collective-permute-start(bf16[4,192,768]{2,1,0:T(8,128)(2,1)S(1)} %add_convert_fusion.1), channel_id=1, source_target_pairs={{0,4},{2,10},{4,0},{6,14},{8,12},{10,2},{12,8},{14,6},{16,20},{18,... | collective-permute-start | bytes 3538952 | tf_op jit(solution)/shard_map/ppermute | solution.py:602
  54.5 9.0 %collective-permute-start.14 = (bf16[1,176,768]{2,1,0:T(8,128)(2,1)S(1)}, bf16[1,176,768]{2,1,0:T(8,128)(2,1)S(1)}, u32[]{:S(2)}, u32[]{:S(2)}) collective-permute-start(bf16[1,176,768]{2,1,0:T(8,128)(2,1)S(1)} %get-tuple-element.198.e0), channel_id=1, source_target_pairs={{0,1},{1,0},{2,3},{3,2},{4,5},{5,4},{6,7},{7,6},{8,9},{9,8},{10,11... | collective-permute-start | bytes 811016 | tf_op jit(solution)/shard_map/ppermute | solution.py:558
  62.7 8.8 %collective-permute-start.15 = (bf16[1,176,768]{2,1,0:T(8,128)(2,1)S(1)}, bf16[1,176,768]{2,1,0:T(8,128)(2,1)S(1)}, u32[]{:S(2)}, u32[]{:S(2)}) collective-permute-start(bf16[1,176,768]{2,1,0:T(8,128)(2,1)S(1)} %get-tuple-element.316), channel_id=1, source_target_pairs={{0,1},{1,0},{2,3},{3,2},{4,5},{5,4},{6,7},{7,6},{8,9},{9,8},{10,11... | collective-permute-start | bytes 811016 | tf_op jit(solution)/shard_map/ppermute | solution.py:558
  71.6 11.9 %collective-permute-start.17 = (bf16[8,96,768]{2,1,0:T(8,128)(2,1)S(1)}, bf16[8,96,768]{2,1,0:T(8,128)(2,1)S(1)}, u32[]{:S(2)}, u32[]{:S(2)}) collective-permute-start(bf16[8,96,768]{2,1,0:T(8,128)(2,1)S(1)} %get-tuple-element.226), channel_id=1, source_target_pairs={{0,2},{2,0},{4,6},{6,4},{8,10},{10,8},{12,14},{14,12},{16,18},{18,... | collective-permute-start | bytes 3538952 | tf_op jit(solution)/shard_map/ppermute | solution.py:558
  71.9 11.5 %collective-permute-start.16 = (bf16[2,192,768]{2,1,0:T(8,128)(2,1)S(1)}, bf16[2,192,768]{2,1,0:T(8,128)(2,1)S(1)}, u32[]{:S(2)}, u32[]{:S(2)}) collective-permute-start(bf16[2,192,768]{2,1,0:T(8,128)(2,1)S(1)} %get-tuple-element.308), channel_id=1, source_target_pairs={{0,8},{2,6},{4,12},{6,2},{8,0},{10,14},{12,4},{14,10},{16,24},{18,... | collective-permute-start | bytes 1769480 | tf_op jit(solution)/shard_map/ppermute | solution.py:602
  72.2 9.1 %collective-permute-start.19 = (bf16[1,176,768]{2,1,0:T(8,128)(2,1)S(1)}, bf16[1,176,768]{2,1,0:T(8,128)(2,1)S(1)}, u32[]{:S(2)}, u32[]{:S(2)}) collective-permute-start(bf16[1,176,768]{2,1,0:T(8,128)(2,1)S(1)} %get-tuple-element.191), channel_id=1, source_target_pairs={{0,1},{1,0},{2,3},{3,2},{4,5},{5,4},{6,7},{7,6},{8,9},{9,8},{10,11... | collective-permute-start | bytes 811016 | tf_op jit(solution)/shard_map/ppermute | solution.py:558
  74.9 6.7 %collective-permute-start.18 = (bf16[48,768]{1,0:T(8,128)(2,1)S(1)}, bf16[48,768]{1,0:T(8,128)(2,1)S(1)}, u32[]{:S(2)}, u32[]{:S(2)}) collective-permute-start(bf16[48,768]{1,0:T(8,128)(2,1)S(1)} %pad_maximum_fusion.7), channel_id=1, source_target_pairs={{0,16},{1,17},{2,18},{3,19},{4,20},{5,21},{6,22},{7,23},{8,24},{9,... | collective-permute-start | bytes 221192 | tf_op jit(solution)/shard_map/ppermute | solution.py:558
  83.7 14.5 %collective-permute-start.20 = (bf16[1,192,768]{2,1,0:T(8,128)(2,1)S(1)}, bf16[1,192,768]{2,1,0:T(8,128)(2,1)S(1)}, u32[]{:S(2)}, u32[]{:S(2)}) collective-permute-start(bf16[1,192,768]{2,1,0:T(8,128)(2,1)S(1)} %get-tuple-element.241), channel_id=1, source_target_pairs={{0,16},{2,18},{4,20},{6,22},{8,24},{10,26},{12,28},{14,30},{16,0},... | collective-permute-start | bytes 884744 | tf_op jit(solution)/shard_map/ppermute | solution.py:602
  85.8 12.4 %collective-permute-start.21 = (bf16[4,96,768]{2,1,0:T(8,128)(2,1)S(1)}, bf16[4,96,768]{2,1,0:T(8,128)(2,1)S(1)}, u32[]{:S(2)}, u32[]{:S(2)}) collective-permute-start(bf16[4,96,768]{2,1,0:T(8,128)(2,1)S(1)} %get-tuple-element.306), channel_id=1, source_target_pairs={{0,4},{2,10},{4,0},{6,14},{8,12},{10,2},{12,8},{14,6},{16,20},{18,... | collective-permute-start | bytes 1769480 | tf_op jit(solution)/shard_map/ppermute | solution.py:602
  87.1 9.7 %collective-permute-start.22 = (bf16[64,768]{1,0:T(8,128)(2,1)S(1)}, bf16[64,768]{1,0:T(8,128)(2,1)S(1)}, u32[]{:S(2)}, u32[]{:S(2)}) collective-permute-start(bf16[64,768]{1,0:T(8,128)(2,1)S(1)} %pad_maximum_fusion.5), channel_id=1, source_target_pairs={{0,4},{1,5},{2,6},{3,7},{4,0},{5,1},{6,2},{7,3},{8,12},{9,13},{10,... | collective-permute-start | bytes 294920 | tf_op jit(solution)/shard_map/ppermute | solution.py:558
  98.2 17.2 %collective-permute-start.23 = (bf16[1,192,768]{2,1,0:T(8,128)(2,1)S(1)}, bf16[1,192,768]{2,1,0:T(8,128)(2,1)S(1)}, u32[]{:S(2)}, u32[]{:S(2)}) collective-permute-start(bf16[1,192,768]{2,1,0:T(8,128)(2,1)S(1)} %get-tuple-element.249), channel_id=1, source_target_pairs={{0,16},{2,18},{4,20},{6,22},{8,24},{10,26},{12,28},{14,30},{16,0},... | collective-permute-start | bytes 884744 | tf_op jit(solution)/shard_map/ppermute | solution.py:602
  98.3 17.0 %collective-permute-start.24 = (bf16[2,96,768]{2,1,0:T(8,128)(2,1)S(1)}, bf16[2,96,768]{2,1,0:T(8,128)(2,1)S(1)}, u32[]{:S(2)}, u32[]{:S(2)}) collective-permute-start(bf16[2,96,768]{2,1,0:T(8,128)(2,1)S(1)} %get-tuple-element.312), channel_id=1, source_target_pairs={{0,8},{2,6},{4,12},{6,2},{8,0},{10,14},{12,4},{14,10},{16,24},{18,... | collective-permute-start | bytes 884744 | tf_op jit(solution)/shard_map/ppermute | solution.py:602
  101.2 14.1 %collective-permute-start.25 = (bf16[96,768]{1,0:T(8,128)(2,1)S(1)}, bf16[96,768]{1,0:T(8,128)(2,1)S(1)}, u32[]{:S(2)}, u32[]{:S(2)}) collective-permute-start(bf16[96,768]{1,0:T(8,128)(2,1)S(1)} %pad_maximum_fusion.4), channel_id=1, source_target_pairs={{0,8},{1,9},{2,10},{3,11},{4,12},{5,13},{6,14},{7,15},{8,0},{9,1},... | collective-permute-start | bytes 442376 | tf_op jit(solution)/shard_map/ppermute | solution.py:558
  115.5 16.3 %collective-permute-start.26 = (bf16[2,192,768]{2,1,0:T(8,128)(2,1)S(1)}, bf16[2,192,768]{2,1,0:T(8,128)(2,1)S(1)}, u32[]{:S(2)}, u32[]{:S(2)}) collective-permute-start(bf16[2,192,768]{2,1,0:T(8,128)(2,1)S(1)} %pad_maximum_fusion.1), channel_id=1, source_target_pairs={{0,8},{2,6},{4,12},{6,2},{8,0},{10,14},{12,4},{14,10},{16,24},{18,... | collective-permute-start | bytes 1769480 | tf_op jit(solution)/shard_map/ppermute | solution.py:602
  115.7 14.6 %collective-permute-start.27 = (bf16[2,96,768]{2,1,0:T(8,128)(2,1)S(1)}, bf16[2,96,768]{2,1,0:T(8,128)(2,1)S(1)}, u32[]{:S(2)}, u32[]{:S(2)}) collective-permute-start(bf16[2,96,768]{2,1,0:T(8,128)(2,1)S(1)} %add_convert_fusion.8), channel_id=1, source_target_pairs={{0,16},{2,18},{4,20},{6,22},{8,24},{10,26},{12,28},{14,30},{16,0},... | collective-permute-start | bytes 884744 | tf_op jit(solution)/shard_map/ppermute | solution.py:602
  117.3 9.0 %collective-permute-start.28 = (bf16[160,768]{1,0:T(8,128)(2,1)S(1)}, bf16[160,768]{1,0:T(8,128)(2,1)S(1)}, u32[]{:S(2)}, u32[]{:S(2)}) collective-permute-start(bf16[160,768]{1,0:T(8,128)(2,1)S(1)} %pad_maximum_fusion.2), channel_id=1, source_target_pairs={{0,1},{1,0},{2,3},{3,2},{4,5},{5,4},{6,7},{7,6},{8,9},{9,8},{10,11... | collective-permute-start | bytes 737288 | tf_op jit(solution)/shard_map/ppermute | solution.py:558
  117.6 8.7 %collective-permute-start.29 = (bf16[160,768]{1,0:T(8,128)(2,1)S(1)}, bf16[160,768]{1,0:T(8,128)(2,1)S(1)}, u32[]{:S(2)}, u32[]{:S(2)}) collective-permute-start(bf16[160,768]{1,0:T(8,128)(2,1)S(1)} %pad_maximum_fusion.2), channel_id=1, source_target_pairs={{0,2},{1,3},{2,0},{3,1},{4,6},{5,7},{6,4},{7,5},{8,10},{9,11},{10,... | collective-permute-start | bytes 737288 | tf_op jit(solution)/shard_map/ppermute | solution.py:558
  117.6 9.7 %collective-permute-start.30 = (bf16[160,768]{1,0:T(8,128)(2,1)S(1)}, bf16[160,768]{1,0:T(8,128)(2,1)S(1)}, u32[]{:S(2)}, u32[]{:S(2)}) collective-permute-start(bf16[160,768]{1,0:T(8,128)(2,1)S(1)} %pad_maximum_fusion.2), channel_id=1, source_target_pairs={{0,3},{1,2},{2,1},{3,0},{4,7},{5,6},{6,5},{7,4},{8,11},{9,10},{10,... | collective-permute-start | bytes 737288 | tf_op jit(solution)/shard_map/ppermute | solution.py:558
  131.9 16.8 %collective-permute-start.31 = (bf16[4,192,768]{2,1,0:T(8,128)(2,1)S(1)}, bf16[4,192,768]{2,1,0:T(8,128)(2,1)S(1)}, u32[]{:S(2)}, u32[]{:S(2)}) collective-permute-start(bf16[4,192,768]{2,1,0:T(8,128)(2,1)S(1)} %constant_dynamic-update-slice_fusion), channel_id=1, source_target_pairs={{0,4},{2,10},{4,0},{6,14},{8,12},{10,2},{12,8},{14,6},{16,20},{18,... | collective-permute-start | bytes 3538952 | tf_op jit(solution)/shard_map/ppermute | solution.py:602
  133.2 10.0 %collective-permute-start.32 = (bf16[2,96,768]{2,1,0:T(8,128)(2,1)S(1)}, bf16[2,96,768]{2,1,0:T(8,128)(2,1)S(1)}, u32[]{:S(2)}, u32[]{:S(2)}) collective-permute-start(bf16[2,96,768]{2,1,0:T(8,128)(2,1)S(1)} %add_convert_fusion.7), channel_id=1, source_target_pairs={{0,8},{2,6},{4,12},{6,2},{8,0},{10,14},{12,4},{14,10},{16,24},{18,... | collective-permute-start | bytes 884744 | tf_op jit(solution)/shard_map/ppermute | solution.py:602
  149.0 9.9 %collective-permute-start.34 = (bf16[4,96,768]{2,1,0:T(8,128)(2,1)S(1)}, bf16[4,96,768]{2,1,0:T(8,128)(2,1)S(1)}, u32[]{:S(2)}, u32[]{:S(2)}) collective-permute-start(bf16[4,96,768]{2,1,0:T(8,128)(2,1)S(1)} %constant_dynamic-update-slice_fusion.4), channel_id=1, source_target_pairs={{0,4},{2,10},{4,0},{6,14},{8,12},{10,2},{12,8},{14,6},{16,20},{18,... | collective-permute-start | bytes 1769480 | tf_op jit(solution)/shard_map/ppermute | solution.py:602
  (25 other events, 139.0 us)

commit v4 on v3

--- a/solution.py
+++ b/solution.py
@@ -776,7 +776,7 @@
         8,
     )[0]
     crop_held = crop_step(crop_keep, crop_other, crop_bits[0], tables)
-    xf0, h1_0, qkv0, pt0, ot0, a0 = attend(0, x0, tie(ids, crop_held[0]))
+    xf0, h1_0, qkv0, pt0, ot0, a0 = attend(0, x0, tie(ids, crop_send))
     a0, g1 = lax.optimization_barrier((a0, g1))
     b0 = swap(a0, "tensor", 1)
     crop_held = crop_step(*crop_held, crop_bits[1], a0)
@@ -955,7 +955,7 @@
         ],
         [pltpu.VMEM((inner, width), F32), pltpu.VMEM((3 * inner, width), F32)],
         1,
-        (tie(ids, other_a), *args),
+        (ids, *args),
         "attend_grads",
         2 * all_rows * 4 * inner * width,
         30,

time: 164 us -> 163 us (level)
  starting transfers between devices: 36.9 us -> 35.1 us
    ppermute x11, starting transfers between devices: 11.4 us -> 9.75 us  [mixed_swap(): return lax.ppermute(v, 'dp', [(i, i ^ bits[i & 1]) for i in range(size)])]
  transfers between devices with their start and end apart: 36 -> 36, of which waited for: 21 -> 21; matrix products, arithmetic and copies ran while one was open for 1% -> 2% of each run, Pallas kernels for 31% -> 31%
where the time goes in v4:
time: 163 us
  waiting for transfers between devices  61.9 us (38%)
  Pallas kernels  57 us (35%)
  starting transfers between devices  35.1 us (22%)
  local copies, waits for them, and re-layouts  5.05 us (3%)
  other arithmetic  2.51 us (2%)
    ppermute x25, waiting for transfers between devices, swap(): return lax.ppermute(v, axis, partner(axis, bit))  45.5 us
    pallas_call x14, Pallas kernels, call(): pl.pallas_call(body, grid_spec=pltpu.PrefetchScalarGridSpec(num_scalar_pr...  45.4 us
    ppermute x25, starting transfers between devices, swap(): return lax.ppermute(v, axis, partner(axis, bit))  25.3 us
    ppermute x11, waiting for transfers between devices, mixed_swap(): return lax.ppermute(v, 'dp', [(i, i ^ bits[i & 1]) for i in range(size)])  16.3 us
    pallas_call x4, Pallas kernels, unpack(): pl.pallas_call(functools.partial(unpack_kernel, layout, own), grid_spec=p...  11.6 us
    ppermute x11, starting transfers between devices, mixed_swap(): return lax.ppermute(v, 'dp', [(i, i ^ bits[i & 1]) for i in range(size)])  9.75 us
    unnamed x46, local copies, waits for them, and re-layouts  4.42 us
  transfers between devices with their start and end apart: 36, of which 21 were waited for; matrix products, arithmetic and copies ran while one was open for 2% of the time, Pallas kernels for 31%

profile of v4, /device:TPU:0, one launch (start us, length us, event | category | flops | bytes accessed | tf_op | source)
XLA Modules:
  0.0 163.0 jit_solution(5357575739028846006)
XLA Ops:
  0.6 3.0 %collective-permute-start = (bf16[1,170,768]{2,1,0:T(8,128)(2,1)}, bf16[1,170,768]{2,1,0:T(8,128)(2,1)S(1)}, u32[]{:S(2)}, u32[]{:S(2)}) collective-permute-start(bf16[1,170,768]{2,1,0:T(8,128)(2,1)} %bitcast.24), channel_id=1, source_target_pairs={{0,1},{1,0},{2,3},{3,2},{4,5},{5,4},{6,7},{7,6},{8,9},{9,8},{10,11... | collective-permute-start | bytes 783368 | tf_op jit(solution)/shard_map/ppermute | solution.py:558
  3.8 1.9 %copy-done.1 = bf16[2048,768]{1,0:T(8,128)(2,1)S(1)} copy-done((bf16[2048,768]{1,0:T(8,128)(2,1)S(1)}, bf16[2048,768]{1,0:T(8,128)(2,1)}, u32[]{:S(2)}) %copy-start.1) | copy-done | bytes 3145752
  7.0 2.9 %crop_grads.1 = (f32[8,24,768]{2,1,0:T(8,128)S(1)}, f32[8,24,768]{2,1,0:T(8,128)S(1)}) custom-call(s32[3]{0:T(128)S(1)} %pad_add_fusion.ids, bf16[320,2048]{1,0:T(8,128)(2,1)S(1)} %copy-done.5, bf16[2048,768]{1,0:T(8,128)(2,1)S(1)} %copy-done.1), custom_call_target="tpu_custom_call" | custom-call | flops 10066329 | bytes 56361 | tf_op jit(solution)/shard_map/crop_grads/pallas_call | solution.py:82
  10.4 1.7 %collective-permute-start.2 = (bf16[1,170,768]{2,1,0:T(8,128)(2,1)S(1)}, bf16[1,170,768]{2,1,0:T(8,128)(2,1)S(1)}, u32[]{:S(2)}, u32[]{:S(2)}) collective-permute-start(bf16[1,170,768]{2,1,0:T(8,128)(2,1)S(1)} %bitcast.26), channel_id=1, source_target_pairs={{0,1},{1,0},{2,3},{3,2},{4,5},{5,4},{6,7},{7,6},{8,9},{9,8},{10,11... | collective-permute-start | bytes 783368 | tf_op jit(solution)/shard_map/ppermute | solution.py:558
  15.4 4.9 %attend.2 = (bf16[1,176,768]{2,1,0:T(8,128)(2,1)S(1)}, bf16[1,176,768]{2,1,0:T(8,128)(2,1)S(1)}, bf16[1,1152,176]{2,1,0:T(8,128)(2,1)S(1)}, bf16[1,12,176,176]{3...) custom-call(s32[3]{0:T(128)S(1)} %pad_add_fusion.ids, s32[20]{0:T(128)S(1)} %copy-done.13, ...), custom_call_target="tpu_custom_call" | custom-call | flops 4152360 | bytes 53146 | tf_op jit(solution)/shard_map/attend/pallas_call | solution.py:82
  22.8 5.0 %attend.3 = (bf16[1,176,768]{2,1,0:T(8,128)(2,1)S(1)}, bf16[1,176,768]{2,1,0:T(8,128)(2,1)S(1)}, bf16[1,1152,176]{2,1,0:T(8,128)(2,1)S(1)}, bf16[1,12,176,176]{3...) custom-call(s32[3]{0:T(128)S(1)} %pad_add_fusion.ids, s32[20]{0:T(128)S(1)} %copy-done.13, ...), custom_call_target="tpu_custom_call" | custom-call | flops 4152360 | bytes 53146 | tf_op jit(solution)/shard_map/attend/pallas_call | solution.py:82
  29.3 2.6 %collective-permute-start.7 = (bf16[1,24,768]{2,1,0:T(8,128)(2,1)S(1)}, bf16[1,24,768]{2,1,0:T(8,128)(2,1)S(1)}, u32[]{:S(2)}, u32[]{:S(2)}) collective-permute-start(bf16[1,24,768]{2,1,0:T(8,128)(2,1)S(1)} %get-tuple-element.315), channel_id=1, source_target_pairs={{0,16},{1,17},{2,18},{3,19},{4,20},{5,21},{6,22},{7,23},{8,24},{9,... | collective-permute-start | bytes 110600 | tf_op jit(solution)/shard_map/ppermute | solution.py:558
  34.5 2.6 %collective-permute-done.8.rest_2_ = bf16[1,24,768]{2,1,0:T(8,128)(2,1)S(1)} collective-permute-done((bf16[1,24,768]{2,1,0:T(8,128)(2,1)S(1)}, bf16[1,24,768]{2,1,0:T(8,128)(2,1)S(1)}, u32[]{:S(2)}, u32[]{:S(2)}) %collective-permute-start.8) | collective-permute-done | bytes 36896 | tf_op jit(solution)/shard_map/ppermute | solution.py:558
  38.7 4.3 %hidden.1 = (f32[2,176,768]{2,1,0:T(8,128)S(1)}, f32[2,176,768]{2,1,0:T(8,128)S(1)}, bf16[352,768]{1,0:T(8,128)(2,1)S(1)}, bf16[352,768]{1,0:T(8,128)(2,1)S(1)},...) custom-call(s32[3]{0:T(128)S(1)} %pad_add_fusion.ids, ...), custom_call_target="tpu_custom_call" | custom-call | flops 24914164 | bytes 130192 | tf_op jit(solution)/shard_map/hidden/pallas_call | solution.py:82
  44.5 3.2 %hidden_grads.1 = (bf16[8,192,768]{2,1,0:T(8,128)(2,1)S(1)}, bf16[8,192,768]{2,1,0:T(8,128)(2,1)S(1)}) custom-call(s32[3]{0:T(128)S(1)} %pad_add_fusion.ids, bf16[352,768]{1,0:T(8,128)(2,1)S(1)} %get-tuple-element.174.h2, bf16[352,768]{1,0:T(8,128)(2,1)S(1)} %get-tuple-element.175.gz, bf16[352,1536]{1,0:T(8,128)(2,1)S(1)} %get-tuple-element.213.m, ...), custom_call_target="tpu_custom_call" | custom-call | flops 16609443 | bytes 79626 | tf_op jit(solution)/shard_map/hidden_grads/pallas_call | solution.py:82
  47.7 1.9 %collective-permute-done.10.e1 = bf16[1,176,768]{2,1,0:T(8,128)(2,1)S(1)} collective-permute-done((bf16[1,176,768]{2,1,0:T(8,128)(2,1)S(1)}, bf16[1,176,768]{2,1,0:T(8,128)(2,1)S(1)}, u32[]{:S(2)}, u32[]{:S(2)}) %collective-permute-start.10) | collective-permute-done | bytes 270368 | tf_op jit(solution)/shard_map/ppermute | solution.py:558
  50.3 2.3 %collective-permute-done.11 = bf16[4,192,768]{2,1,0:T(8,128)(2,1)S(1)} collective-permute-done((bf16[4,192,768]{2,1,0:T(8,128)(2,1)S(1)}, bf16[4,192,768]{2,1,0:T(8,128)(2,1)S(1)}, u32[]{:S(2)}, u32[]{:S(2)}) %collective-permute-start.11) | collective-permute-done | bytes 1179680 | tf_op jit(solution)/shard_map/ppermute | solution.py:558
  56.7 5.8 %attend_back.2 = (f32[1,176,768]{2,1,0:T(8,128)}, bf16[1,176,768]{2,1,0:T(8,128)(2,1)S(1)}, bf16[1,176,768]{2,1,0:T(8,128)(2,1)S(1)}, bf16[1,1152,176]{2,1,0:T(8...) custom-call(s32[3]{0:T(128)S(1)} %pad_add_fusion.ids, s32[20]{0:T(128)S(1)} %copy-done.13, ...), custom_call_target="tpu_custom_call" | custom-call | flops 8304721 | bytes 86231 | tf_op jit(solution)/shard_map/attend_back/pallas_call | solution.py:82
  63.6 5.6 %attend_back.3 = (f32[1,176,768]{2,1,0:T(8,128)S(1)}, bf16[1,176,768]{2,1,0:T(8,128)(2,1)S(1)}, bf16[1,176,768]{2,1,0:T(8,128)(2,1)S(1)}, bf16[1,1152,176]{2,1,0...) custom-call(s32[3]{0:T(128)S(1)} %pad_add_fusion.ids, s32[20]{0:T(128)S(1)} %copy-done.13, ...), custom_call_target="tpu_custom_call" | custom-call | flops 8304721 | bytes 86231 | tf_op jit(solution)/shard_map/attend_back/pallas_call | solution.py:82
  69.2 2.1 %attend_grads.1 = (bf16[8,96,768]{2,1,0:T(8,128)(2,1)S(1)}, bf16[8,96,768]{2,1,0:T(8,128)(2,1)S(1)}, f32[16,768]{1,0:T(8,128)S(1)}) custom-call(s32[3]{0:T(128)S(1)} %pad_add_fusion.ids, bf16[1,384,176]{2,1,0:T(8,128)(2,1)S(1)} %get-tuple-element.191.o0, bf16[1,384,176]{2,1,0:T(8,128)(2,1)S(1)} %get-tuple-element.192.o1, ...), custom_call_target="tpu_custom_call" | custom-call | flops 8304721 | bytes 58828 | tf_op jit(solution)/shard_map/attend_grads/pallas_call | solution.py:82
  74.8 2.0 %collective-permute-start.18 = (bf16[48,768]{1,0:T(8,128)(2,1)S(1)}, bf16[48,768]{1,0:T(8,128)(2,1)S(1)}, u32[]{:S(2)}, u32[]{:S(2)}) collective-permute-start(bf16[48,768]{1,0:T(8,128)(2,1)S(1)} %pad_maximum_fusion.7), channel_id=1, source_target_pairs={{0,16},{1,17},{2,18},{3,19},{4,20},{5,21},{6,22},{7,23},{8,24},{9,... | collective-permute-start | bytes 221192 | tf_op jit(solution)/shard_map/ppermute | solution.py:558
  76.9 4.3 %collective-permute-done.19.e1 = bf16[1,176,768]{2,1,0:T(8,128)(2,1)S(1)} collective-permute-done((bf16[1,176,768]{2,1,0:T(8,128)(2,1)S(1)}, bf16[1,176,768]{2,1,0:T(8,128)(2,1)S(1)}, u32[]{:S(2)}, u32[]{:S(2)}) %collective-permute-start.19) | collective-permute-done | bytes 270368 | tf_op jit(solution)/shard_map/ppermute | solution.py:558
  81.3 2.2 %collective-permute-done.16 = bf16[2,192,768]{2,1,0:T(8,128)(2,1)S(1)} collective-permute-done((bf16[2,192,768]{2,1,0:T(8,128)(2,1)S(1)}, bf16[2,192,768]{2,1,0:T(8,128)(2,1)S(1)}, u32[]{:S(2)}, u32[]{:S(2)}) %collective-permute-start.16) | collective-permute-done | bytes 589856 | tf_op jit(solution)/shard_map/ppermute | solution.py:602
  88.7 7.6 %collective-permute-done.22 = bf16[64,768]{1,0:T(8,128)(2,1)S(1)} collective-permute-done((bf16[64,768]{1,0:T(8,128)(2,1)S(1)}, bf16[64,768]{1,0:T(8,128)(2,1)S(1)}, u32[]{:S(2)}, u32[]{:S(2)}) %collective-permute-start.22) | collective-permute-done | bytes 98336 | tf_op jit(solution)/shard_map/ppermute | solution.py:558
  98.2 2.2 %collective-permute-start.24 = (bf16[2,96,768]{2,1,0:T(8,128)(2,1)S(1)}, bf16[2,96,768]{2,1,0:T(8,128)(2,1)S(1)}, u32[]{:S(2)}, u32[]{:S(2)}) collective-permute-start(bf16[2,96,768]{2,1,0:T(8,128)(2,1)S(1)} %get-tuple-element.308), channel_id=1, source_target_pairs={{0,8},{2,6},{4,12},{6,2},{8,0},{10,14},{12,4},{14,10},{16,24},{18,... | collective-permute-start | bytes 884744 | tf_op jit(solution)/shard_map/ppermute | solution.py:602
  100.7 13.9 %collective-permute-done.25 = bf16[96,768]{1,0:T(8,128)(2,1)S(1)} collective-permute-done((bf16[96,768]{1,0:T(8,128)(2,1)S(1)}, bf16[96,768]{1,0:T(8,128)(2,1)S(1)}, u32[]{:S(2)}, u32[]{:S(2)}) %collective-permute-start.25) | collective-permute-done | bytes 147488 | tf_op jit(solution)/shard_map/ppermute | solution.py:558
  118.3 6.7 %collective-permute-done.28 = bf16[160,768]{1,0:T(8,128)(2,1)S(1)} collective-permute-done((bf16[160,768]{1,0:T(8,128)(2,1)S(1)}, bf16[160,768]{1,0:T(8,128)(2,1)S(1)}, u32[]{:S(2)}, u32[]{:S(2)}) %collective-permute-start.28) | collective-permute-done | bytes 245792 | tf_op jit(solution)/shard_map/ppermute | solution.py:558
  125.1 1.9 %collective-permute-done.30 = bf16[160,768]{1,0:T(8,128)(2,1)S(1)} collective-permute-done((bf16[160,768]{1,0:T(8,128)(2,1)S(1)}, bf16[160,768]{1,0:T(8,128)(2,1)S(1)}, u32[]{:S(2)}, u32[]{:S(2)}) %collective-permute-start.30) | collective-permute-done | bytes 245792 | tf_op jit(solution)/shard_map/ppermute | solution.py:558
  126.9 2.2 %collective-permute-done.27 = bf16[2,96,768]{2,1,0:T(8,128)(2,1)S(1)} collective-permute-done((bf16[2,96,768]{2,1,0:T(8,128)(2,1)S(1)}, bf16[2,96,768]{2,1,0:T(8,128)(2,1)S(1)}, u32[]{:S(2)}, u32[]{:S(2)}) %collective-permute-start.27) | collective-permute-done | bytes 294944 | tf_op jit(solution)/shard_map/ppermute | solution.py:602
  129.1 2.0 %collective-permute-done.26 = bf16[2,192,768]{2,1,0:T(8,128)(2,1)S(1)} collective-permute-done((bf16[2,192,768]{2,1,0:T(8,128)(2,1)S(1)}, bf16[2,192,768]{2,1,0:T(8,128)(2,1)S(1)}, u32[]{:S(2)}, u32[]{:S(2)}) %collective-permute-start.26) | collective-permute-done | bytes 589856 | tf_op jit(solution)/shard_map/ppermute | solution.py:602
  134.1 5.8 %proto_grads.1 = f32[2048,768]{1,0:T(8,128)} custom-call(s32[3]{0:T(128)S(1)} %pad_add_fusion.ids, bf16[320,2048]{1,0:T(8,128)(2,1)S(1)} %copy-done.6, bf16[512,768]{1,0:T(8,128)(2,1)S(1)} %pad_maximum_fusion.pooled, bf16[2048,768]{1,0:T(8,128)(2,1)S(1)} %copy-done.2, s32[1,2048]{1,0:T(1,128)S(1)} %bitcast.31), custom_call_target="tpu_custom_call" | custom-call | flops 10066329 | bytes 115425 | tf_op jit(solution)/shard_map/proto_grads/pallas_call | solution.py:82
  139.8 2.3 %collective-permute-done.32 = bf16[2,96,768]{2,1,0:T(8,128)(2,1)S(1)} collective-permute-done((bf16[2,96,768]{2,1,0:T(8,128)(2,1)S(1)}, bf16[2,96,768]{2,1,0:T(8,128)(2,1)S(1)}, u32[]{:S(2)}, u32[]{:S(2)}) %collective-permute-start.32) | collective-permute-done | bytes 294944 | tf_op jit(solution)/shard_map/ppermute | solution.py:602
  142.1 5.3 %collective-permute-done.31 = bf16[4,192,768]{2,1,0:T(8,128)(2,1)S(1)} collective-permute-done((bf16[4,192,768]{2,1,0:T(8,128)(2,1)S(1)}, bf16[4,192,768]{2,1,0:T(8,128)(2,1)S(1)}, u32[]{:S(2)}, u32[]{:S(2)}) %collective-permute-start.31) | collective-permute-done | bytes 1179680 | tf_op jit(solution)/shard_map/ppermute | solution.py:602
  148.8 2.9 %unpack_hidden_own.1 = (f32[768,1536]{1,0:T(8,128)}, f32[1536,768]{1,0:T(8,128)}) custom-call(s32[17]{0:T(128)S(1)} %pad_add_fusion.1.places, bf16[8,192,768]{2,1,0:T(8,128)(2,1)S(1)} %constant_dynamic-update-slice_fusion.2.held), custom_call_target="tpu_custom_call" | custom-call | tf_op jit(solution)/shard_map/unpack_hidden_own/pallas_call | solution.py:613
  152.4 4.5 %unpack_hidden_other.1 = (f32[768,1536]{1,0:T(8,128)}, f32[1536,768]{1,0:T(8,128)}) custom-call(s32[17]{0:T(128)S(1)} %pad_add_fusion.1.places, bf16[8,192,768]{2,1,0:T(8,128)(2,1)} %collective-permute-done.33.held, f32[768,1536]{1,0:T(8,128)} %get-tuple-element.274.refs_0_, ...), custom_call_target="tpu_custom_call", output_to_operand_aliasing={{0}: (2, {}), {1}: (3, {})} | custom-call | tf_op jit(solution)/shard_map/unpack_hidden_other/pallas_call | solution.py:613
  157.9 2.1 %unpack_attend_own.1 = (f32[384,768]{1,0:T(8,128)}, f32[1152,768]{1,0:T(8,128)}) custom-call(s32[17]{0:T(128)S(1)} %pad_add_fusion.1.places, bf16[8,96,768]{2,1,0:T(8,128)(2,1)S(1)} %constant_dynamic-update-slice_fusion.6.held), custom_call_target="tpu_custom_call" | custom-call | tf_op jit(solution)/shard_map/unpack_attend_own/pallas_call | solution.py:613
  160.7 2.1 %unpack_attend_other.1 = (f32[384,768]{1,0:T(8,128)}, f32[1152,768]{1,0:T(8,128)}) custom-call(s32[17]{0:T(128)S(1)} %pad_add_fusion.1.places, bf16[8,96,768]{2,1,0:T(8,128)(2,1)S(1)} %collective-permute-done.35.held, f32[384,768]{1,0:T(8,128)} %get-tuple-element.282.refs_0_, ...), custom_call_target="tpu_custom_call", output_to_operand_aliasing={{0}: (2, {}), {1}: (3, {})} | custom-call | tf_op jit(solution)/shard_map/unpack_attend_other/pallas_call | solution.py:613
  (159 shorter events, 41.4 us)
Async XLA Ops:
  0.6 9.7 %collective-permute-start = (bf16[1,170,768]{2,1,0:T(8,128)(2,1)}, bf16[1,170,768]{2,1,0:T(8,128)(2,1)S(1)}, u32[]{:S(2)}, u32[]{:S(2)}) collective-permute-start(bf16[1,170,768]{2,1,0:T(8,128)(2,1)} %bitcast.24), channel_id=1, source_target_pairs={{0,1},{1,0},{2,3},{3,2},{4,5},{5,4},{6,7},{7,6},{8,9},{9,8},{10,11... | collective-permute-start | bytes 783368 | tf_op jit(solution)/shard_map/ppermute | solution.py:558
  10.4 10.0 %collective-permute-start.2 = (bf16[1,170,768]{2,1,0:T(8,128)(2,1)S(1)}, bf16[1,170,768]{2,1,0:T(8,128)(2,1)S(1)}, u32[]{:S(2)}, u32[]{:S(2)}) collective-permute-start(bf16[1,170,768]{2,1,0:T(8,128)(2,1)S(1)} %bitcast.26), channel_id=1, source_target_pairs={{0,1},{1,0},{2,3},{3,2},{4,5},{5,4},{6,7},{7,6},{8,9},{9,8},{10,11... | collective-permute-start | bytes 783368 | tf_op jit(solution)/shard_map/ppermute | solution.py:558
  13.8 6.6 %collective-permute-start.3 = (bf16[4,24,768]{2,1,0:T(8,128)(2,1)S(1)}, bf16[4,24,768]{2,1,0:T(8,128)(2,1)S(1)}, u32[]{:S(2)}, u32[]{:S(2)}) collective-permute-start(bf16[4,24,768]{2,1,0:T(8,128)(2,1)S(1)} %slice.217), channel_id=1, source_target_pairs={{0,4},{2,6},{4,0},{6,2},{8,12},{10,14},{12,8},{14,10},{16,20},{18,... | collective-permute-start | bytes 442376 | tf_op jit(solution)/shard_map/ppermute | solution.py:558
  20.5 8.8 %collective-permute-start.6 = (bf16[2,24,768]{2,1,0:T(8,128)(2,1)S(1)}, bf16[2,24,768]{2,1,0:T(8,128)(2,1)S(1)}, u32[]{:S(2)}, u32[]{:S(2)}) collective-permute-start(bf16[2,24,768]{2,1,0:T(8,128)(2,1)S(1)} %slice.218), channel_id=1, source_target_pairs={{0,8},{2,10},{4,12},{6,14},{8,0},{10,2},{12,4},{14,6},{16,24},{18,... | collective-permute-start | bytes 221192 | tf_op jit(solution)/shard_map/ppermute | solution.py:558
  22.1 11.7 %collective-permute-start.4 = (bf16[1,176,768]{2,1,0:T(8,128)(2,1)S(1)}, bf16[1,176,768]{2,1,0:T(8,128)(2,1)S(1)}, u32[]{:S(2)}, u32[]{:S(2)}) collective-permute-start(bf16[1,176,768]{2,1,0:T(8,128)(2,1)S(1)} %get-tuple-element.164.a0), channel_id=1, source_target_pairs={{0,1},{1,0},{2,3},{3,2},{4,5},{5,4},{6,7},{7,6},{8,9},{9,8},{10,11... | collective-permute-start | bytes 811016 | tf_op jit(solution)/shard_map/ppermute | solution.py:558
  27.8 10.8 %collective-permute-start.5 = (bf16[1,176,768]{2,1,0:T(8,128)(2,1)S(1)}, bf16[1,176,768]{2,1,0:T(8,128)(2,1)S(1)}, u32[]{:S(2)}, u32[]{:S(2)}) collective-permute-start(bf16[1,176,768]{2,1,0:T(8,128)(2,1)S(1)} %get-tuple-element.169.a1), channel_id=1, source_target_pairs={{0,1},{1,0},{2,3},{3,2},{4,5},{5,4},{6,7},{7,6},{8,9},{9,8},{10,11... | collective-permute-start | bytes 811016 | tf_op jit(solution)/shard_map/ppermute | solution.py:558
  29.3 5.2 %collective-permute-start.7 = (bf16[1,24,768]{2,1,0:T(8,128)(2,1)S(1)}, bf16[1,24,768]{2,1,0:T(8,128)(2,1)S(1)}, u32[]{:S(2)}, u32[]{:S(2)}) collective-permute-start(bf16[1,24,768]{2,1,0:T(8,128)(2,1)S(1)} %get-tuple-element.315), channel_id=1, source_target_pairs={{0,16},{1,17},{2,18},{3,19},{4,20},{5,21},{6,22},{7,23},{8,24},{9,... | collective-permute-start | bytes 110600 | tf_op jit(solution)/shard_map/ppermute | solution.py:558
  32.0 5.2 %collective-permute-start.8 = (bf16[1,24,768]{2,1,0:T(8,128)(2,1)S(1)}, bf16[1,24,768]{2,1,0:T(8,128)(2,1)S(1)}, u32[]{:S(2)}, u32[]{:S(2)}) collective-permute-start(bf16[1,24,768]{2,1,0:T(8,128)(2,1)S(1)} %get-tuple-element.314), channel_id=1, source_target_pairs={{0,1},{1,0},{2,3},{3,2},{4,5},{5,4},{6,7},{7,6},{8,9},{9,8},{10,11... | collective-permute-start | bytes 110600 | tf_op jit(solution)/shard_map/ppermute | solution.py:558
  32.6 6.0 %collective-permute-start.9 = (bf16[1,24,768]{2,1,0:T(8,128)(2,1)S(1)}, bf16[1,24,768]{2,1,0:T(8,128)(2,1)S(1)}, u32[]{:S(2)}, u32[]{:S(2)}) collective-permute-start(bf16[1,24,768]{2,1,0:T(8,128)(2,1)S(1)} %get-tuple-element.315), channel_id=1, source_target_pairs={{0,17},{1,16},{2,19},{3,18},{4,21},{5,20},{6,23},{7,22},{8,25},{9,... | collective-permute-start | bytes 110600 | tf_op jit(solution)/shard_map/ppermute | solution.py:558
  43.0 6.5 %collective-permute-start.10 = (bf16[1,176,768]{2,1,0:T(8,128)(2,1)S(1)}, bf16[1,176,768]{2,1,0:T(8,128)(2,1)S(1)}, u32[]{:S(2)}, u32[]{:S(2)}) collective-permute-start(bf16[1,176,768]{2,1,0:T(8,128)(2,1)S(1)} %get-tuple-element.180.e0), channel_id=1, source_target_pairs={{0,1},{1,0},{2,3},{3,2},{4,5},{5,4},{6,7},{7,6},{8,9},{9,8},{10,11... | collective-permute-start | bytes 811016 | tf_op jit(solution)/shard_map/ppermute | solution.py:558
  49.8 12.7 %collective-permute-start.12 = (bf16[4,192,768]{2,1,0:T(8,128)(2,1)S(1)}, bf16[4,192,768]{2,1,0:T(8,128)(2,1)S(1)}, u32[]{:S(2)}, u32[]{:S(2)}) collective-permute-start(bf16[4,192,768]{2,1,0:T(8,128)(2,1)S(1)} %get-tuple-element.306), channel_id=1, source_target_pairs={{0,2},{2,0},{4,6},{6,4},{8,10},{10,8},{12,14},{14,12},{16,18},{18,... | collective-permute-start | bytes 3538952 | tf_op jit(solution)/shard_map/ppermute | solution.py:558
  52.9 18.6 %collective-permute-start.13 = (bf16[4,192,768]{2,1,0:T(8,128)(2,1)S(1)}, bf16[4,192,768]{2,1,0:T(8,128)(2,1)S(1)}, u32[]{:S(2)}, u32[]{:S(2)}) collective-permute-start(bf16[4,192,768]{2,1,0:T(8,128)(2,1)S(1)} %add_convert_fusion.1), channel_id=1, source_target_pairs={{0,4},{2,10},{4,0},{6,14},{8,12},{10,2},{12,8},{14,6},{16,20},{18,... | collective-permute-start | bytes 3538952 | tf_op jit(solution)/shard_map/ppermute | solution.py:602
  54.5 9.0 %collective-permute-start.14 = (bf16[1,176,768]{2,1,0:T(8,128)(2,1)S(1)}, bf16[1,176,768]{2,1,0:T(8,128)(2,1)S(1)}, u32[]{:S(2)}, u32[]{:S(2)}) collective-permute-start(bf16[1,176,768]{2,1,0:T(8,128)(2,1)S(1)} %get-tuple-element.194.e0), channel_id=1, source_target_pairs={{0,1},{1,0},{2,3},{3,2},{4,5},{5,4},{6,7},{7,6},{8,9},{9,8},{10,11... | collective-permute-start | bytes 811016 | tf_op jit(solution)/shard_map/ppermute | solution.py:558
  62.6 9.0 %collective-permute-start.15 = (bf16[1,176,768]{2,1,0:T(8,128)(2,1)S(1)}, bf16[1,176,768]{2,1,0:T(8,128)(2,1)S(1)}, u32[]{:S(2)}, u32[]{:S(2)}) collective-permute-start(bf16[1,176,768]{2,1,0:T(8,128)(2,1)S(1)} %get-tuple-element.312), channel_id=1, source_target_pairs={{0,1},{1,0},{2,3},{3,2},{4,5},{5,4},{6,7},{7,6},{8,9},{9,8},{10,11... | collective-permute-start | bytes 811016 | tf_op jit(solution)/shard_map/ppermute | solution.py:558
  71.6 11.9 %collective-permute-start.17 = (bf16[8,96,768]{2,1,0:T(8,128)(2,1)S(1)}, bf16[8,96,768]{2,1,0:T(8,128)(2,1)S(1)}, u32[]{:S(2)}, u32[]{:S(2)}) collective-permute-start(bf16[8,96,768]{2,1,0:T(8,128)(2,1)S(1)} %get-tuple-element.222), channel_id=1, source_target_pairs={{0,2},{2,0},{4,6},{6,4},{8,10},{10,8},{12,14},{14,12},{16,18},{18,... | collective-permute-start | bytes 3538952 | tf_op jit(solution)/shard_map/ppermute | solution.py:558
  72.0 11.5 %collective-permute-start.16 = (bf16[2,192,768]{2,1,0:T(8,128)(2,1)S(1)}, bf16[2,192,768]{2,1,0:T(8,128)(2,1)S(1)}, u32[]{:S(2)}, u32[]{:S(2)}) collective-permute-start(bf16[2,192,768]{2,1,0:T(8,128)(2,1)S(1)} %get-tuple-element.304), channel_id=1, source_target_pairs={{0,8},{2,6},{4,12},{6,2},{8,0},{10,14},{12,4},{14,10},{16,24},{18,... | collective-permute-start | bytes 1769480 | tf_op jit(solution)/shard_map/ppermute | solution.py:602
  72.3 8.9 %collective-permute-start.19 = (bf16[1,176,768]{2,1,0:T(8,128)(2,1)S(1)}, bf16[1,176,768]{2,1,0:T(8,128)(2,1)S(1)}, u32[]{:S(2)}, u32[]{:S(2)}) collective-permute-start(bf16[1,176,768]{2,1,0:T(8,128)(2,1)S(1)} %get-tuple-element.188), channel_id=1, source_target_pairs={{0,1},{1,0},{2,3},{3,2},{4,5},{5,4},{6,7},{7,6},{8,9},{9,8},{10,11... | collective-permute-start | bytes 811016 | tf_op jit(solution)/shard_map/ppermute | solution.py:558
  74.8 6.5 %collective-permute-start.18 = (bf16[48,768]{1,0:T(8,128)(2,1)S(1)}, bf16[48,768]{1,0:T(8,128)(2,1)S(1)}, u32[]{:S(2)}, u32[]{:S(2)}) collective-permute-start(bf16[48,768]{1,0:T(8,128)(2,1)S(1)} %pad_maximum_fusion.7), channel_id=1, source_target_pairs={{0,16},{1,17},{2,18},{3,19},{4,20},{5,21},{6,22},{7,23},{8,24},{9,... | collective-permute-start | bytes 221192 | tf_op jit(solution)/shard_map/ppermute | solution.py:558
  83.7 14.0 %collective-permute-start.20 = (bf16[1,192,768]{2,1,0:T(8,128)(2,1)S(1)}, bf16[1,192,768]{2,1,0:T(8,128)(2,1)S(1)}, u32[]{:S(2)}, u32[]{:S(2)}) collective-permute-start(bf16[1,192,768]{2,1,0:T(8,128)(2,1)S(1)} %get-tuple-element.237), channel_id=1, source_target_pairs={{0,16},{2,18},{4,20},{6,22},{8,24},{10,26},{12,28},{14,30},{16,0},... | collective-permute-start | bytes 884744 | tf_op jit(solution)/shard_map/ppermute | solution.py:602
  85.2 12.5 %collective-permute-start.21 = (bf16[4,96,768]{2,1,0:T(8,128)(2,1)S(1)}, bf16[4,96,768]{2,1,0:T(8,128)(2,1)S(1)}, u32[]{:S(2)}, u32[]{:S(2)}) collective-permute-start(bf16[4,96,768]{2,1,0:T(8,128)(2,1)S(1)} %get-tuple-element.302), channel_id=1, source_target_pairs={{0,4},{2,10},{4,0},{6,14},{8,12},{10,2},{12,8},{14,6},{16,20},{18,... | collective-permute-start | bytes 1769480 | tf_op jit(solution)/shard_map/ppermute | solution.py:602
  86.5 9.8 %collective-permute-start.22 = (bf16[64,768]{1,0:T(8,128)(2,1)S(1)}, bf16[64,768]{1,0:T(8,128)(2,1)S(1)}, u32[]{:S(2)}, u32[]{:S(2)}) collective-permute-start(bf16[64,768]{1,0:T(8,128)(2,1)S(1)} %pad_maximum_fusion.5), channel_id=1, source_target_pairs={{0,4},{1,5},{2,6},{3,7},{4,0},{5,1},{6,2},{7,3},{8,12},{9,13},{10,... | collective-permute-start | bytes 294920 | tf_op jit(solution)/shard_map/ppermute | solution.py:558
  97.7 16.9 %collective-permute-start.23 = (bf16[1,192,768]{2,1,0:T(8,128)(2,1)S(1)}, bf16[1,192,768]{2,1,0:T(8,128)(2,1)S(1)}, u32[]{:S(2)}, u32[]{:S(2)}) collective-permute-start(bf16[1,192,768]{2,1,0:T(8,128)(2,1)S(1)} %get-tuple-element.245), channel_id=1, source_target_pairs={{0,16},{2,18},{4,20},{6,22},{8,24},{10,26},{12,28},{14,30},{16,0},... | collective-permute-start | bytes 884744 | tf_op jit(solution)/shard_map/ppermute | solution.py:602
  98.2 16.4 %collective-permute-start.24 = (bf16[2,96,768]{2,1,0:T(8,128)(2,1)S(1)}, bf16[2,96,768]{2,1,0:T(8,128)(2,1)S(1)}, u32[]{:S(2)}, u32[]{:S(2)}) collective-permute-start(bf16[2,96,768]{2,1,0:T(8,128)(2,1)S(1)} %get-tuple-element.308), channel_id=1, source_target_pairs={{0,8},{2,6},{4,12},{6,2},{8,0},{10,14},{12,4},{14,10},{16,24},{18,... | collective-permute-start | bytes 884744 | tf_op jit(solution)/shard_map/ppermute | solution.py:602
  100.5 14.1 %collective-permute-start.25 = (bf16[96,768]{1,0:T(8,128)(2,1)S(1)}, bf16[96,768]{1,0:T(8,128)(2,1)S(1)}, u32[]{:S(2)}, u32[]{:S(2)}) collective-permute-start(bf16[96,768]{1,0:T(8,128)(2,1)S(1)} %pad_maximum_fusion.4), channel_id=1, source_target_pairs={{0,8},{1,9},{2,10},{3,11},{4,12},{5,13},{6,14},{7,15},{8,0},{9,1},... | collective-permute-start | bytes 442376 | tf_op jit(solution)/shard_map/ppermute | solution.py:558
  114.8 16.3 %collective-permute-start.26 = (bf16[2,192,768]{2,1,0:T(8,128)(2,1)S(1)}, bf16[2,192,768]{2,1,0:T(8,128)(2,1)S(1)}, u32[]{:S(2)}, u32[]{:S(2)}) collective-permute-start(bf16[2,192,768]{2,1,0:T(8,128)(2,1)S(1)} %pad_maximum_fusion.1), channel_id=1, source_target_pairs={{0,8},{2,6},{4,12},{6,2},{8,0},{10,14},{12,4},{14,10},{16,24},{18,... | collective-permute-start | bytes 1769480 | tf_op jit(solution)/shard_map/ppermute | solution.py:602
  115.0 14.1 %collective-permute-start.27 = (bf16[2,96,768]{2,1,0:T(8,128)(2,1)S(1)}, bf16[2,96,768]{2,1,0:T(8,128)(2,1)S(1)}, u32[]{:S(2)}, u32[]{:S(2)}) collective-permute-start(bf16[2,96,768]{2,1,0:T(8,128)(2,1)S(1)} %add_convert_fusion.8), channel_id=1, source_target_pairs={{0,16},{2,18},{4,20},{6,22},{8,24},{10,26},{12,28},{14,30},{16,0},... | collective-permute-start | bytes 884744 | tf_op jit(solution)/shard_map/ppermute | solution.py:602
  116.1 9.0 %collective-permute-start.28 = (bf16[160,768]{1,0:T(8,128)(2,1)S(1)}, bf16[160,768]{1,0:T(8,128)(2,1)S(1)}, u32[]{:S(2)}, u32[]{:S(2)}) collective-permute-start(bf16[160,768]{1,0:T(8,128)(2,1)S(1)} %pad_maximum_fusion.2), channel_id=1, source_target_pairs={{0,1},{1,0},{2,3},{3,2},{4,5},{5,4},{6,7},{7,6},{8,9},{9,8},{10,11... | collective-permute-start | bytes 737288 | tf_op jit(solution)/shard_map/ppermute | solution.py:558
  117.3 7.7 %collective-permute-start.29 = (bf16[160,768]{1,0:T(8,128)(2,1)S(1)}, bf16[160,768]{1,0:T(8,128)(2,1)S(1)}, u32[]{:S(2)}, u32[]{:S(2)}) collective-permute-start(bf16[160,768]{1,0:T(8,128)(2,1)S(1)} %pad_maximum_fusion.2), channel_id=1, source_target_pairs={{0,2},{1,3},{2,0},{3,1},{4,6},{5,7},{6,4},{7,5},{8,10},{9,11},{10,... | collective-permute-start | bytes 737288 | tf_op jit(solution)/shard_map/ppermute | solution.py:558
  117.3 9.6 %collective-permute-start.30 = (bf16[160,768]{1,0:T(8,128)(2,1)S(1)}, bf16[160,768]{1,0:T(8,128)(2,1)S(1)}, u32[]{:S(2)}, u32[]{:S(2)}) collective-permute-start(bf16[160,768]{1,0:T(8,128)(2,1)S(1)} %pad_maximum_fusion.2), channel_id=1, source_target_pairs={{0,3},{1,2},{2,1},{3,0},{4,7},{5,6},{6,5},{7,4},{8,11},{9,10},{10,... | collective-permute-start | bytes 737288 | tf_op jit(solution)/shard_map/ppermute | solution.py:558
  131.2 16.3 %collective-permute-start.31 = (bf16[4,192,768]{2,1,0:T(8,128)(2,1)S(1)}, bf16[4,192,768]{2,1,0:T(8,128)(2,1)S(1)}, u32[]{:S(2)}, u32[]{:S(2)}) collective-permute-start(bf16[4,192,768]{2,1,0:T(8,128)(2,1)S(1)} %constant_dynamic-update-slice_fusion), channel_id=1, source_target_pairs={{0,4},{2,10},{4,0},{6,14},{8,12},{10,2},{12,8},{14,6},{16,20},{18,... | collective-permute-start | bytes 3538952 | tf_op jit(solution)/shard_map/ppermute | solution.py:602
  132.1 10.0 %collective-permute-start.32 = (bf16[2,96,768]{2,1,0:T(8,128)(2,1)S(1)}, bf16[2,96,768]{2,1,0:T(8,128)(2,1)S(1)}, u32[]{:S(2)}, u32[]{:S(2)}) collective-permute-start(bf16[2,96,768]{2,1,0:T(8,128)(2,1)S(1)} %add_convert_fusion.7), channel_id=1, source_target_pairs={{0,8},{2,6},{4,12},{6,2},{8,0},{10,14},{12,4},{14,10},{16,24},{18,... | collective-permute-start | bytes 884744 | tf_op jit(solution)/shard_map/ppermute | solution.py:602
  147.8 9.9 %collective-permute-start.34 = (bf16[4,96,768]{2,1,0:T(8,128)(2,1)S(1)}, bf16[4,96,768]{2,1,0:T(8,128)(2,1)S(1)}, u32[]{:S(2)}, u32[]{:S(2)}) collective-permute-start(bf16[4,96,768]{2,1,0:T(8,128)(2,1)S(1)} %constant_dynamic-update-slice_fusion.4), channel_id=1, source_target_pairs={{0,4},{2,10},{4,0},{6,14},{8,12},{10,2},{12,8},{14,6},{16,20},{18,... | collective-permute-start | bytes 1769480 | tf_op jit(solution)/shard_map/ppermute | solution.py:602
  (25 other events, 139.7 us)

commit v5 on v4

--- a/solution.py
+++ b/solution.py
@@ -1008,6 +1008,7 @@
         return unpack_both(places_of(orders_b), held, other, layout, shapes, "unpack_attend")
 
     def patch():
+        yield ()
         yield ()
         near, far = gh1_near, gh1_far
         if half > 1:

time: 163 us -> 163 us (level)
  transfers between devices with their start and end apart: 36 -> 36, of which waited for: 21 -> 20; matrix products, arithmetic and copies ran while one was open for 2% -> 2% of each run, Pallas kernels for 31% -> 31%
where the time goes in v5:
time: 163 us
  waiting for transfers between devices  61.5 us (38%)
  Pallas kernels  57 us (35%)
  starting transfers between devices  35.3 us (22%)
  local copies, waits for them, and re-layouts  5.04 us (3%)
  other arithmetic  2.52 us (2%)
    pallas_call x14, Pallas kernels, call(): pl.pallas_call(body, grid_spec=pltpu.PrefetchScalarGridSpec(num_scalar_pr...  45.4 us
    ppermute x25, waiting for transfers between devices, swap(): return lax.ppermute(v, axis, partner(axis, bit))  45 us
    ppermute x25, starting transfers between devices, swap(): return lax.ppermute(v, axis, partner(axis, bit))  25.3 us
    ppermute x11, waiting for transfers between devices, mixed_swap(): return lax.ppermute(v, 'dp', [(i, i ^ bits[i & 1]) for i in range(size)])  16.5 us
    pallas_call x4, Pallas kernels, unpack(): pl.pallas_call(functools.partial(unpack_kernel, layout, own), grid_spec=p...  11.6 us
    ppermute x11, starting transfers between devices, mixed_swap(): return lax.ppermute(v, 'dp', [(i, i ^ bits[i & 1]) for i in range(size)])  9.98 us
    unnamed x46, local copies, waits for them, and re-layouts  4.41 us
  transfers between devices with their start and end apart: 36, of which 20 were waited for; matrix products, arithmetic and copies ran while one was open for 2% of the time, Pallas kernels for 31%

profile of v5, /device:TPU:0, one launch (start us, length us, event | category | flops | bytes accessed | tf_op | source)
XLA Modules:
  0.0 162.9 jit_solution(7535412578081270199)
XLA Ops:
  0.6 3.0 %collective-permute-start = (bf16[1,170,768]{2,1,0:T(8,128)(2,1)}, bf16[1,170,768]{2,1,0:T(8,128)(2,1)S(1)}, u32[]{:S(2)}, u32[]{:S(2)}) collective-permute-start(bf16[1,170,768]{2,1,0:T(8,128)(2,1)} %bitcast.24), channel_id=1, source_target_pairs={{0,1},{1,0},{2,3},{3,2},{4,5},{5,4},{6,7},{7,6},{8,9},{9,8},{10,11... | collective-permute-start | bytes 783368 | tf_op jit(solution)/shard_map/ppermute | solution.py:558
  3.8 1.9 %copy-done.1 = bf16[2048,768]{1,0:T(8,128)(2,1)S(1)} copy-done((bf16[2048,768]{1,0:T(8,128)(2,1)S(1)}, bf16[2048,768]{1,0:T(8,128)(2,1)}, u32[]{:S(2)}) %copy-start.1) | copy-done | bytes 3145752
  7.0 2.9 %crop_grads.1 = (f32[8,24,768]{2,1,0:T(8,128)S(1)}, f32[8,24,768]{2,1,0:T(8,128)S(1)}) custom-call(s32[3]{0:T(128)S(1)} %pad_add_fusion.ids, bf16[320,2048]{1,0:T(8,128)(2,1)S(1)} %copy-done.5, bf16[2048,768]{1,0:T(8,128)(2,1)S(1)} %copy-done.1), custom_call_target="tpu_custom_call" | custom-call | flops 10066329 | bytes 56361 | tf_op jit(solution)/shard_map/crop_grads/pallas_call | solution.py:82
  10.4 1.7 %collective-permute-start.2 = (bf16[1,170,768]{2,1,0:T(8,128)(2,1)S(1)}, bf16[1,170,768]{2,1,0:T(8,128)(2,1)S(1)}, u32[]{:S(2)}, u32[]{:S(2)}) collective-permute-start(bf16[1,170,768]{2,1,0:T(8,128)(2,1)S(1)} %bitcast.26), channel_id=1, source_target_pairs={{0,1},{1,0},{2,3},{3,2},{4,5},{5,4},{6,7},{7,6},{8,9},{9,8},{10,11... | collective-permute-start | bytes 783368 | tf_op jit(solution)/shard_map/ppermute | solution.py:558
  15.4 4.9 %attend.2 = (bf16[1,176,768]{2,1,0:T(8,128)(2,1)S(1)}, bf16[1,176,768]{2,1,0:T(8,128)(2,1)S(1)}, bf16[1,1152,176]{2,1,0:T(8,128)(2,1)S(1)}, bf16[1,12,176,176]{3...) custom-call(s32[3]{0:T(128)S(1)} %pad_add_fusion.ids, s32[20]{0:T(128)S(1)} %copy-done.13, ...), custom_call_target="tpu_custom_call" | custom-call | flops 4152360 | bytes 53146 | tf_op jit(solution)/shard_map/attend/pallas_call | solution.py:82
  22.8 5.0 %attend.3 = (bf16[1,176,768]{2,1,0:T(8,128)(2,1)S(1)}, bf16[1,176,768]{2,1,0:T(8,128)(2,1)S(1)}, bf16[1,1152,176]{2,1,0:T(8,128)(2,1)S(1)}, bf16[1,12,176,176]{3...) custom-call(s32[3]{0:T(128)S(1)} %pad_add_fusion.ids, s32[20]{0:T(128)S(1)} %copy-done.13, ...), custom_call_target="tpu_custom_call" | custom-call | flops 4152360 | bytes 53146 | tf_op jit(solution)/shard_map/attend/pallas_call | solution.py:82
  29.3 2.6 %collective-permute-start.7 = (bf16[1,24,768]{2,1,0:T(8,128)(2,1)S(1)}, bf16[1,24,768]{2,1,0:T(8,128)(2,1)S(1)}, u32[]{:S(2)}, u32[]{:S(2)}) collective-permute-start(bf16[1,24,768]{2,1,0:T(8,128)(2,1)S(1)} %get-tuple-element.315), channel_id=1, source_target_pairs={{0,16},{1,17},{2,18},{3,19},{4,20},{5,21},{6,22},{7,23},{8,24},{9,... | collective-permute-start | bytes 110600 | tf_op jit(solution)/shard_map/ppermute | solution.py:558
  34.5 2.6 %collective-permute-done.8.rest_2_ = bf16[1,24,768]{2,1,0:T(8,128)(2,1)S(1)} collective-permute-done((bf16[1,24,768]{2,1,0:T(8,128)(2,1)S(1)}, bf16[1,24,768]{2,1,0:T(8,128)(2,1)S(1)}, u32[]{:S(2)}, u32[]{:S(2)}) %collective-permute-start.8) | collective-permute-done | bytes 36896 | tf_op jit(solution)/shard_map/ppermute | solution.py:558
  38.7 4.3 %hidden.1 = (f32[2,176,768]{2,1,0:T(8,128)S(1)}, f32[2,176,768]{2,1,0:T(8,128)S(1)}, bf16[352,768]{1,0:T(8,128)(2,1)S(1)}, bf16[352,768]{1,0:T(8,128)(2,1)S(1)},...) custom-call(s32[3]{0:T(128)S(1)} %pad_add_fusion.ids, ...), custom_call_target="tpu_custom_call" | custom-call | flops 24914164 | bytes 130192 | tf_op jit(solution)/shard_map/hidden/pallas_call | solution.py:82
  44.5 3.2 %hidden_grads.1 = (bf16[8,192,768]{2,1,0:T(8,128)(2,1)S(1)}, bf16[8,192,768]{2,1,0:T(8,128)(2,1)S(1)}) custom-call(s32[3]{0:T(128)S(1)} %pad_add_fusion.ids, bf16[352,768]{1,0:T(8,128)(2,1)S(1)} %get-tuple-element.174.h2, bf16[352,768]{1,0:T(8,128)(2,1)S(1)} %get-tuple-element.175.gz, bf16[352,1536]{1,0:T(8,128)(2,1)S(1)} %get-tuple-element.213.m, ...), custom_call_target="tpu_custom_call" | custom-call | flops 16609443 | bytes 79626 | tf_op jit(solution)/shard_map/hidden_grads/pallas_call | solution.py:82
  47.7 1.9 %collective-permute-done.10.e1 = bf16[1,176,768]{2,1,0:T(8,128)(2,1)S(1)} collective-permute-done((bf16[1,176,768]{2,1,0:T(8,128)(2,1)S(1)}, bf16[1,176,768]{2,1,0:T(8,128)(2,1)S(1)}, u32[]{:S(2)}, u32[]{:S(2)}) %collective-permute-start.10) | collective-permute-done | bytes 270368 | tf_op jit(solution)/shard_map/ppermute | solution.py:558
  50.3 2.3 %collective-permute-done.11 = bf16[4,192,768]{2,1,0:T(8,128)(2,1)S(1)} collective-permute-done((bf16[4,192,768]{2,1,0:T(8,128)(2,1)S(1)}, bf16[4,192,768]{2,1,0:T(8,128)(2,1)S(1)}, u32[]{:S(2)}, u32[]{:S(2)}) %collective-permute-start.11) | collective-permute-done | bytes 1179680 | tf_op jit(solution)/shard_map/ppermute | solution.py:558
  56.7 5.8 %attend_back.2 = (f32[1,176,768]{2,1,0:T(8,128)}, bf16[1,176,768]{2,1,0:T(8,128)(2,1)S(1)}, bf16[1,176,768]{2,1,0:T(8,128)(2,1)S(1)}, bf16[1,1152,176]{2,1,0:T(8...) custom-call(s32[3]{0:T(128)S(1)} %pad_add_fusion.ids, s32[20]{0:T(128)S(1)} %copy-done.13, ...), custom_call_target="tpu_custom_call" | custom-call | flops 8304721 | bytes 86231 | tf_op jit(solution)/shard_map/attend_back/pallas_call | solution.py:82
  63.6 5.6 %attend_back.3 = (f32[1,176,768]{2,1,0:T(8,128)S(1)}, bf16[1,176,768]{2,1,0:T(8,128)(2,1)S(1)}, bf16[1,176,768]{2,1,0:T(8,128)(2,1)S(1)}, bf16[1,1152,176]{2,1,0...) custom-call(s32[3]{0:T(128)S(1)} %pad_add_fusion.ids, s32[20]{0:T(128)S(1)} %copy-done.13, ...), custom_call_target="tpu_custom_call" | custom-call | flops 8304721 | bytes 86231 | tf_op jit(solution)/shard_map/attend_back/pallas_call | solution.py:82
  69.2 2.1 %attend_grads.1 = (bf16[8,96,768]{2,1,0:T(8,128)(2,1)S(1)}, bf16[8,96,768]{2,1,0:T(8,128)(2,1)S(1)}, f32[16,768]{1,0:T(8,128)S(1)}) custom-call(s32[3]{0:T(128)S(1)} %pad_add_fusion.ids, bf16[1,384,176]{2,1,0:T(8,128)(2,1)S(1)} %get-tuple-element.191.o0, bf16[1,384,176]{2,1,0:T(8,128)(2,1)S(1)} %get-tuple-element.192.o1, ...), custom_call_target="tpu_custom_call" | custom-call | flops 8304721 | bytes 58828 | tf_op jit(solution)/shard_map/attend_grads/pallas_call | solution.py:82
  73.7 2.1 %collective-permute-start.18 = (bf16[48,768]{1,0:T(8,128)(2,1)S(1)}, bf16[48,768]{1,0:T(8,128)(2,1)S(1)}, u32[]{:S(2)}, u32[]{:S(2)}) collective-permute-start(bf16[48,768]{1,0:T(8,128)(2,1)S(1)} %pad_maximum_fusion.7), channel_id=1, source_target_pairs={{0,16},{1,17},{2,18},{3,19},{4,20},{5,21},{6,22},{7,23},{8,24},{9,... | collective-permute-start | bytes 221192 | tf_op jit(solution)/shard_map/ppermute | solution.py:558
  76.9 4.3 %collective-permute-done.18 = bf16[48,768]{1,0:T(8,128)(2,1)S(1)} collective-permute-done((bf16[48,768]{1,0:T(8,128)(2,1)S(1)}, bf16[48,768]{1,0:T(8,128)(2,1)S(1)}, u32[]{:S(2)}, u32[]{:S(2)}) %collective-permute-start.18) | collective-permute-done | bytes 73760 | tf_op jit(solution)/shard_map/ppermute | solution.py:558
  81.3 2.3 %collective-permute-done.16 = bf16[2,192,768]{2,1,0:T(8,128)(2,1)S(1)} collective-permute-done((bf16[2,192,768]{2,1,0:T(8,128)(2,1)S(1)}, bf16[2,192,768]{2,1,0:T(8,128)(2,1)S(1)}, u32[]{:S(2)}, u32[]{:S(2)}) %collective-permute-start.16) | collective-permute-done | bytes 589856 | tf_op jit(solution)/shard_map/ppermute | solution.py:602
  87.5 8.8 %collective-permute-done.21 = bf16[64,768]{1,0:T(8,128)(2,1)S(1)} collective-permute-done((bf16[64,768]{1,0:T(8,128)(2,1)S(1)}, bf16[64,768]{1,0:T(8,128)(2,1)S(1)}, u32[]{:S(2)}, u32[]{:S(2)}) %collective-permute-start.21) | collective-permute-done | bytes 98336 | tf_op jit(solution)/shard_map/ppermute | solution.py:558
  98.2 2.2 %collective-permute-start.24 = (bf16[2,96,768]{2,1,0:T(8,128)(2,1)S(1)}, bf16[2,96,768]{2,1,0:T(8,128)(2,1)S(1)}, u32[]{:S(2)}, u32[]{:S(2)}) collective-permute-start(bf16[2,96,768]{2,1,0:T(8,128)(2,1)S(1)} %get-tuple-element.308), channel_id=1, source_target_pairs={{0,8},{2,6},{4,12},{6,2},{8,0},{10,14},{12,4},{14,10},{16,24},{18,... | collective-permute-start | bytes 884744 | tf_op jit(solution)/shard_map/ppermute | solution.py:602
  101.9 12.7 %collective-permute-done.25 = bf16[96,768]{1,0:T(8,128)(2,1)S(1)} collective-permute-done((bf16[96,768]{1,0:T(8,128)(2,1)S(1)}, bf16[96,768]{1,0:T(8,128)(2,1)S(1)}, u32[]{:S(2)}, u32[]{:S(2)}) %collective-permute-start.25) | collective-permute-done | bytes 147488 | tf_op jit(solution)/shard_map/ppermute | solution.py:558
  118.3 6.7 %collective-permute-done.28 = bf16[160,768]{1,0:T(8,128)(2,1)S(1)} collective-permute-done((bf16[160,768]{1,0:T(8,128)(2,1)S(1)}, bf16[160,768]{1,0:T(8,128)(2,1)S(1)}, u32[]{:S(2)}, u32[]{:S(2)}) %collective-permute-start.28) | collective-permute-done | bytes 245792 | tf_op jit(solution)/shard_map/ppermute | solution.py:558
  125.1 1.7 %collective-permute-done.30 = bf16[160,768]{1,0:T(8,128)(2,1)S(1)} collective-permute-done((bf16[160,768]{1,0:T(8,128)(2,1)S(1)}, bf16[160,768]{1,0:T(8,128)(2,1)S(1)}, u32[]{:S(2)}, u32[]{:S(2)}) %collective-permute-start.30) | collective-permute-done | bytes 245792 | tf_op jit(solution)/shard_map/ppermute | solution.py:558
  126.7 2.3 %collective-permute-done.27 = bf16[2,96,768]{2,1,0:T(8,128)(2,1)S(1)} collective-permute-done((bf16[2,96,768]{2,1,0:T(8,128)(2,1)S(1)}, bf16[2,96,768]{2,1,0:T(8,128)(2,1)S(1)}, u32[]{:S(2)}, u32[]{:S(2)}) %collective-permute-start.27) | collective-permute-done | bytes 294944 | tf_op jit(solution)/shard_map/ppermute | solution.py:602
  129.0 2.0 %collective-permute-done.26 = bf16[2,192,768]{2,1,0:T(8,128)(2,1)S(1)} collective-permute-done((bf16[2,192,768]{2,1,0:T(8,128)(2,1)S(1)}, bf16[2,192,768]{2,1,0:T(8,128)(2,1)S(1)}, u32[]{:S(2)}, u32[]{:S(2)}) %collective-permute-start.26) | collective-permute-done | bytes 589856 | tf_op jit(solution)/shard_map/ppermute | solution.py:602
  134.0 5.8 %proto_grads.1 = f32[2048,768]{1,0:T(8,128)} custom-call(s32[3]{0:T(128)S(1)} %pad_add_fusion.ids, bf16[320,2048]{1,0:T(8,128)(2,1)S(1)} %copy-done.6, bf16[512,768]{1,0:T(8,128)(2,1)S(1)} %pad_maximum_fusion.pooled, bf16[2048,768]{1,0:T(8,128)(2,1)S(1)} %copy-done.2, s32[1,2048]{1,0:T(1,128)S(1)} %bitcast.31), custom_call_target="tpu_custom_call" | custom-call | flops 10066329 | bytes 115425 | tf_op jit(solution)/shard_map/proto_grads/pallas_call | solution.py:82
  139.8 2.3 %collective-permute-done.32 = bf16[2,96,768]{2,1,0:T(8,128)(2,1)S(1)} collective-permute-done((bf16[2,96,768]{2,1,0:T(8,128)(2,1)S(1)}, bf16[2,96,768]{2,1,0:T(8,128)(2,1)S(1)}, u32[]{:S(2)}, u32[]{:S(2)}) %collective-permute-start.32) | collective-permute-done | bytes 294944 | tf_op jit(solution)/shard_map/ppermute | solution.py:602
  142.1 5.2 %collective-permute-done.31 = bf16[4,192,768]{2,1,0:T(8,128)(2,1)S(1)} collective-permute-done((bf16[4,192,768]{2,1,0:T(8,128)(2,1)S(1)}, bf16[4,192,768]{2,1,0:T(8,128)(2,1)S(1)}, u32[]{:S(2)}, u32[]{:S(2)}) %collective-permute-start.31) | collective-permute-done | bytes 1179680 | tf_op jit(solution)/shard_map/ppermute | solution.py:602
  148.8 2.9 %unpack_hidden_own.1 = (f32[768,1536]{1,0:T(8,128)}, f32[1536,768]{1,0:T(8,128)}) custom-call(s32[17]{0:T(128)S(1)} %pad_add_fusion.1.places, bf16[8,192,768]{2,1,0:T(8,128)(2,1)S(1)} %constant_dynamic-update-slice_fusion.2.held), custom_call_target="tpu_custom_call" | custom-call | tf_op jit(solution)/shard_map/unpack_hidden_own/pallas_call | solution.py:613
  152.3 4.5 %unpack_hidden_other.1 = (f32[768,1536]{1,0:T(8,128)}, f32[1536,768]{1,0:T(8,128)}) custom-call(s32[17]{0:T(128)S(1)} %pad_add_fusion.1.places, bf16[8,192,768]{2,1,0:T(8,128)(2,1)} %collective-permute-done.33.held, f32[768,1536]{1,0:T(8,128)} %get-tuple-element.274.refs_0_, ...), custom_call_target="tpu_custom_call", output_to_operand_aliasing={{0}: (2, {}), {1}: (3, {})} | custom-call | tf_op jit(solution)/shard_map/unpack_hidden_other/pallas_call | solution.py:613
  157.8 2.1 %unpack_attend_own.1 = (f32[384,768]{1,0:T(8,128)}, f32[1152,768]{1,0:T(8,128)}) custom-call(s32[17]{0:T(128)S(1)} %pad_add_fusion.1.places, bf16[8,96,768]{2,1,0:T(8,128)(2,1)S(1)} %constant_dynamic-update-slice_fusion.6.held), custom_call_target="tpu_custom_call" | custom-call | tf_op jit(solution)/shard_map/unpack_attend_own/pallas_call | solution.py:613
  160.6 2.1 %unpack_attend_other.1 = (f32[384,768]{1,0:T(8,128)}, f32[1152,768]{1,0:T(8,128)}) custom-call(s32[17]{0:T(128)S(1)} %pad_add_fusion.1.places, bf16[8,96,768]{2,1,0:T(8,128)(2,1)S(1)} %collective-permute-done.35.held, f32[384,768]{1,0:T(8,128)} %get-tuple-element.282.refs_0_, ...), custom_call_target="tpu_custom_call", output_to_operand_aliasing={{0}: (2, {}), {1}: (3, {})} | custom-call | tf_op jit(solution)/shard_map/unpack_attend_other/pallas_call | solution.py:613
  (159 shorter events, 41.5 us)
Async XLA Ops:
  0.6 9.7 %collective-permute-start = (bf16[1,170,768]{2,1,0:T(8,128)(2,1)}, bf16[1,170,768]{2,1,0:T(8,128)(2,1)S(1)}, u32[]{:S(2)}, u32[]{:S(2)}) collective-permute-start(bf16[1,170,768]{2,1,0:T(8,128)(2,1)} %bitcast.24), channel_id=1, source_target_pairs={{0,1},{1,0},{2,3},{3,2},{4,5},{5,4},{6,7},{7,6},{8,9},{9,8},{10,11... | collective-permute-start | bytes 783368 | tf_op jit(solution)/shard_map/ppermute | solution.py:558
  10.4 10.0 %collective-permute-start.2 = (bf16[1,170,768]{2,1,0:T(8,128)(2,1)S(1)}, bf16[1,170,768]{2,1,0:T(8,128)(2,1)S(1)}, u32[]{:S(2)}, u32[]{:S(2)}) collective-permute-start(bf16[1,170,768]{2,1,0:T(8,128)(2,1)S(1)} %bitcast.26), channel_id=1, source_target_pairs={{0,1},{1,0},{2,3},{3,2},{4,5},{5,4},{6,7},{7,6},{8,9},{9,8},{10,11... | collective-permute-start | bytes 783368 | tf_op jit(solution)/shard_map/ppermute | solution.py:558
  13.8 6.6 %collective-permute-start.3 = (bf16[4,24,768]{2,1,0:T(8,128)(2,1)S(1)}, bf16[4,24,768]{2,1,0:T(8,128)(2,1)S(1)}, u32[]{:S(2)}, u32[]{:S(2)}) collective-permute-start(bf16[4,24,768]{2,1,0:T(8,128)(2,1)S(1)} %slice.217), channel_id=1, source_target_pairs={{0,4},{2,6},{4,0},{6,2},{8,12},{10,14},{12,8},{14,10},{16,20},{18,... | collective-permute-start | bytes 442376 | tf_op jit(solution)/shard_map/ppermute | solution.py:558
  20.5 8.8 %collective-permute-start.6 = (bf16[2,24,768]{2,1,0:T(8,128)(2,1)S(1)}, bf16[2,24,768]{2,1,0:T(8,128)(2,1)S(1)}, u32[]{:S(2)}, u32[]{:S(2)}) collective-permute-start(bf16[2,24,768]{2,1,0:T(8,128)(2,1)S(1)} %slice.218), channel_id=1, source_target_pairs={{0,8},{2,10},{4,12},{6,14},{8,0},{10,2},{12,4},{14,6},{16,24},{18,... | collective-permute-start | bytes 221192 | tf_op jit(solution)/shard_map/ppermute | solution.py:558
  22.1 11.7 %collective-permute-start.4 = (bf16[1,176,768]{2,1,0:T(8,128)(2,1)S(1)}, bf16[1,176,768]{2,1,0:T(8,128)(2,1)S(1)}, u32[]{:S(2)}, u32[]{:S(2)}) collective-permute-start(bf16[1,176,768]{2,1,0:T(8,128)(2,1)S(1)} %get-tuple-element.164.a0), channel_id=1, source_target_pairs={{0,1},{1,0},{2,3},{3,2},{4,5},{5,4},{6,7},{7,6},{8,9},{9,8},{10,11... | collective-permute-start | bytes 811016 | tf_op jit(solution)/shard_map/ppermute | solution.py:558
  27.8 10.8 %collective-permute-start.5 = (bf16[1,176,768]{2,1,0:T(8,128)(2,1)S(1)}, bf16[1,176,768]{2,1,0:T(8,128)(2,1)S(1)}, u32[]{:S(2)}, u32[]{:S(2)}) collective-permute-start(bf16[1,176,768]{2,1,0:T(8,128)(2,1)S(1)} %get-tuple-element.169.a1), channel_id=1, source_target_pairs={{0,1},{1,0},{2,3},{3,2},{4,5},{5,4},{6,7},{7,6},{8,9},{9,8},{10,11... | collective-permute-start | bytes 811016 | tf_op jit(solution)/shard_map/ppermute | solution.py:558
  29.3 5.2 %collective-permute-start.7 = (bf16[1,24,768]{2,1,0:T(8,128)(2,1)S(1)}, bf16[1,24,768]{2,1,0:T(8,128)(2,1)S(1)}, u32[]{:S(2)}, u32[]{:S(2)}) collective-permute-start(bf16[1,24,768]{2,1,0:T(8,128)(2,1)S(1)} %get-tuple-element.315), channel_id=1, source_target_pairs={{0,16},{1,17},{2,18},{3,19},{4,20},{5,21},{6,22},{7,23},{8,24},{9,... | collective-permute-start | bytes 110600 | tf_op jit(solution)/shard_map/ppermute | solution.py:558
  32.0 5.2 %collective-permute-start.8 = (bf16[1,24,768]{2,1,0:T(8,128)(2,1)S(1)}, bf16[1,24,768]{2,1,0:T(8,128)(2,1)S(1)}, u32[]{:S(2)}, u32[]{:S(2)}) collective-permute-start(bf16[1,24,768]{2,1,0:T(8,128)(2,1)S(1)} %get-tuple-element.314), channel_id=1, source_target_pairs={{0,1},{1,0},{2,3},{3,2},{4,5},{5,4},{6,7},{7,6},{8,9},{9,8},{10,11... | collective-permute-start | bytes 110600 | tf_op jit(solution)/shard_map/ppermute | solution.py:558
  32.6 6.0 %collective-permute-start.9 = (bf16[1,24,768]{2,1,0:T(8,128)(2,1)S(1)}, bf16[1,24,768]{2,1,0:T(8,128)(2,1)S(1)}, u32[]{:S(2)}, u32[]{:S(2)}) collective-permute-start(bf16[1,24,768]{2,1,0:T(8,128)(2,1)S(1)} %get-tuple-element.315), channel_id=1, source_target_pairs={{0,17},{1,16},{2,19},{3,18},{4,21},{5,20},{6,23},{7,22},{8,25},{9,... | collective-permute-start | bytes 110600 | tf_op jit(solution)/shard_map/ppermute | solution.py:558
  43.0 6.5 %collective-permute-start.10 = (bf16[1,176,768]{2,1,0:T(8,128)(2,1)S(1)}, bf16[1,176,768]{2,1,0:T(8,128)(2,1)S(1)}, u32[]{:S(2)}, u32[]{:S(2)}) collective-permute-start(bf16[1,176,768]{2,1,0:T(8,128)(2,1)S(1)} %get-tuple-element.180.e0), channel_id=1, source_target_pairs={{0,1},{1,0},{2,3},{3,2},{4,5},{5,4},{6,7},{7,6},{8,9},{9,8},{10,11... | collective-permute-start | bytes 811016 | tf_op jit(solution)/shard_map/ppermute | solution.py:558
  49.8 12.7 %collective-permute-start.12 = (bf16[4,192,768]{2,1,0:T(8,128)(2,1)S(1)}, bf16[4,192,768]{2,1,0:T(8,128)(2,1)S(1)}, u32[]{:S(2)}, u32[]{:S(2)}) collective-permute-start(bf16[4,192,768]{2,1,0:T(8,128)(2,1)S(1)} %get-tuple-element.306), channel_id=1, source_target_pairs={{0,2},{2,0},{4,6},{6,4},{8,10},{10,8},{12,14},{14,12},{16,18},{18,... | collective-permute-start | bytes 3538952 | tf_op jit(solution)/shard_map/ppermute | solution.py:558
  52.9 18.6 %collective-permute-start.13 = (bf16[4,192,768]{2,1,0:T(8,128)(2,1)S(1)}, bf16[4,192,768]{2,1,0:T(8,128)(2,1)S(1)}, u32[]{:S(2)}, u32[]{:S(2)}) collective-permute-start(bf16[4,192,768]{2,1,0:T(8,128)(2,1)S(1)} %add_convert_fusion.1), channel_id=1, source_target_pairs={{0,4},{2,10},{4,0},{6,14},{8,12},{10,2},{12,8},{14,6},{16,20},{18,... | collective-permute-start | bytes 3538952 | tf_op jit(solution)/shard_map/ppermute | solution.py:602
  54.5 9.0 %collective-permute-start.14 = (bf16[1,176,768]{2,1,0:T(8,128)(2,1)S(1)}, bf16[1,176,768]{2,1,0:T(8,128)(2,1)S(1)}, u32[]{:S(2)}, u32[]{:S(2)}) collective-permute-start(bf16[1,176,768]{2,1,0:T(8,128)(2,1)S(1)} %get-tuple-element.194.e0), channel_id=1, source_target_pairs={{0,1},{1,0},{2,3},{3,2},{4,5},{5,4},{6,7},{7,6},{8,9},{9,8},{10,11... | collective-permute-start | bytes 811016 | tf_op jit(solution)/shard_map/ppermute | solution.py:558
  62.6 9.0 %collective-permute-start.15 = (bf16[1,176,768]{2,1,0:T(8,128)(2,1)S(1)}, bf16[1,176,768]{2,1,0:T(8,128)(2,1)S(1)}, u32[]{:S(2)}, u32[]{:S(2)}) collective-permute-start(bf16[1,176,768]{2,1,0:T(8,128)(2,1)S(1)} %get-tuple-element.312), channel_id=1, source_target_pairs={{0,1},{1,0},{2,3},{3,2},{4,5},{5,4},{6,7},{7,6},{8,9},{9,8},{10,11... | collective-permute-start | bytes 811016 | tf_op jit(solution)/shard_map/ppermute | solution.py:558
  71.6 11.9 %collective-permute-start.17 = (bf16[8,96,768]{2,1,0:T(8,128)(2,1)S(1)}, bf16[8,96,768]{2,1,0:T(8,128)(2,1)S(1)}, u32[]{:S(2)}, u32[]{:S(2)}) collective-permute-start(bf16[8,96,768]{2,1,0:T(8,128)(2,1)S(1)} %get-tuple-element.222), channel_id=1, source_target_pairs={{0,2},{2,0},{4,6},{6,4},{8,10},{10,8},{12,14},{14,12},{16,18},{18,... | collective-permute-start | bytes 3538952 | tf_op jit(solution)/shard_map/ppermute | solution.py:558
  72.0 11.5 %collective-permute-start.16 = (bf16[2,192,768]{2,1,0:T(8,128)(2,1)S(1)}, bf16[2,192,768]{2,1,0:T(8,128)(2,1)S(1)}, u32[]{:S(2)}, u32[]{:S(2)}) collective-permute-start(bf16[2,192,768]{2,1,0:T(8,128)(2,1)S(1)} %get-tuple-element.304), channel_id=1, source_target_pairs={{0,8},{2,6},{4,12},{6,2},{8,0},{10,14},{12,4},{14,10},{16,24},{18,... | collective-permute-start | bytes 1769480 | tf_op jit(solution)/shard_map/ppermute | solution.py:602
  73.7 7.5 %collective-permute-start.18 = (bf16[48,768]{1,0:T(8,128)(2,1)S(1)}, bf16[48,768]{1,0:T(8,128)(2,1)S(1)}, u32[]{:S(2)}, u32[]{:S(2)}) collective-permute-start(bf16[48,768]{1,0:T(8,128)(2,1)S(1)} %pad_maximum_fusion.7), channel_id=1, source_target_pairs={{0,16},{1,17},{2,18},{3,19},{4,20},{5,21},{6,22},{7,23},{8,24},{9,... | collective-permute-start | bytes 221192 | tf_op jit(solution)/shard_map/ppermute | solution.py:558
  75.8 11.7 %collective-permute-start.22 = (bf16[1,176,768]{2,1,0:T(8,128)(2,1)S(1)}, bf16[1,176,768]{2,1,0:T(8,128)(2,1)S(1)}, u32[]{:S(2)}, u32[]{:S(2)}) collective-permute-start(bf16[1,176,768]{2,1,0:T(8,128)(2,1)S(1)} %get-tuple-element.188), channel_id=1, source_target_pairs={{0,1},{1,0},{2,3},{3,2},{4,5},{5,4},{6,7},{7,6},{8,9},{9,8},{10,11... | collective-permute-start | bytes 811016 | tf_op jit(solution)/shard_map/ppermute | solution.py:558
  83.7 14.0 %collective-permute-start.19 = (bf16[1,192,768]{2,1,0:T(8,128)(2,1)S(1)}, bf16[1,192,768]{2,1,0:T(8,128)(2,1)S(1)}, u32[]{:S(2)}, u32[]{:S(2)}) collective-permute-start(bf16[1,192,768]{2,1,0:T(8,128)(2,1)S(1)} %get-tuple-element.243), channel_id=1, source_target_pairs={{0,16},{2,18},{4,20},{6,22},{8,24},{10,26},{12,28},{14,30},{16,0},... | collective-permute-start | bytes 884744 | tf_op jit(solution)/shard_map/ppermute | solution.py:602
  85.2 12.5 %collective-permute-start.20 = (bf16[4,96,768]{2,1,0:T(8,128)(2,1)S(1)}, bf16[4,96,768]{2,1,0:T(8,128)(2,1)S(1)}, u32[]{:S(2)}, u32[]{:S(2)}) collective-permute-start(bf16[4,96,768]{2,1,0:T(8,128)(2,1)S(1)} %get-tuple-element.302), channel_id=1, source_target_pairs={{0,4},{2,10},{4,0},{6,14},{8,12},{10,2},{12,8},{14,6},{16,20},{18,... | collective-permute-start | bytes 1769480 | tf_op jit(solution)/shard_map/ppermute | solution.py:602
  86.5 9.8 %collective-permute-start.21 = (bf16[64,768]{1,0:T(8,128)(2,1)S(1)}, bf16[64,768]{1,0:T(8,128)(2,1)S(1)}, u32[]{:S(2)}, u32[]{:S(2)}) collective-permute-start(bf16[64,768]{1,0:T(8,128)(2,1)S(1)} %pad_maximum_fusion.5), channel_id=1, source_target_pairs={{0,4},{1,5},{2,6},{3,7},{4,0},{5,1},{6,2},{7,3},{8,12},{9,13},{10,... | collective-permute-start | bytes 294920 | tf_op jit(solution)/shard_map/ppermute | solution.py:558
  97.7 16.8 %collective-permute-start.23 = (bf16[1,192,768]{2,1,0:T(8,128)(2,1)S(1)}, bf16[1,192,768]{2,1,0:T(8,128)(2,1)S(1)}, u32[]{:S(2)}, u32[]{:S(2)}) collective-permute-start(bf16[1,192,768]{2,1,0:T(8,128)(2,1)S(1)} %get-tuple-element.245), channel_id=1, source_target_pairs={{0,16},{2,18},{4,20},{6,22},{8,24},{10,26},{12,28},{14,30},{16,0},... | collective-permute-start | bytes 884744 | tf_op jit(solution)/shard_map/ppermute | solution.py:602
  98.2 16.4 %collective-permute-start.24 = (bf16[2,96,768]{2,1,0:T(8,128)(2,1)S(1)}, bf16[2,96,768]{2,1,0:T(8,128)(2,1)S(1)}, u32[]{:S(2)}, u32[]{:S(2)}) collective-permute-start(bf16[2,96,768]{2,1,0:T(8,128)(2,1)S(1)} %get-tuple-element.308), channel_id=1, source_target_pairs={{0,8},{2,6},{4,12},{6,2},{8,0},{10,14},{12,4},{14,10},{16,24},{18,... | collective-permute-start | bytes 884744 | tf_op jit(solution)/shard_map/ppermute | solution.py:602
  100.5 14.1 %collective-permute-start.25 = (bf16[96,768]{1,0:T(8,128)(2,1)S(1)}, bf16[96,768]{1,0:T(8,128)(2,1)S(1)}, u32[]{:S(2)}, u32[]{:S(2)}) collective-permute-start(bf16[96,768]{1,0:T(8,128)(2,1)S(1)} %pad_maximum_fusion.4), channel_id=1, source_target_pairs={{0,8},{1,9},{2,10},{3,11},{4,12},{5,13},{6,14},{7,15},{8,0},{9,1},... | collective-permute-start | bytes 442376 | tf_op jit(solution)/shard_map/ppermute | solution.py:558
  114.7 16.3 %collective-permute-start.26 = (bf16[2,192,768]{2,1,0:T(8,128)(2,1)S(1)}, bf16[2,192,768]{2,1,0:T(8,128)(2,1)S(1)}, u32[]{:S(2)}, u32[]{:S(2)}) collective-permute-start(bf16[2,192,768]{2,1,0:T(8,128)(2,1)S(1)} %pad_maximum_fusion.1), channel_id=1, source_target_pairs={{0,8},{2,6},{4,12},{6,2},{8,0},{10,14},{12,4},{14,10},{16,24},{18,... | collective-permute-start | bytes 1769480 | tf_op jit(solution)/shard_map/ppermute | solution.py:602
  114.9 14.1 %collective-permute-start.27 = (bf16[2,96,768]{2,1,0:T(8,128)(2,1)S(1)}, bf16[2,96,768]{2,1,0:T(8,128)(2,1)S(1)}, u32[]{:S(2)}, u32[]{:S(2)}) collective-permute-start(bf16[2,96,768]{2,1,0:T(8,128)(2,1)S(1)} %add_convert_fusion.8), channel_id=1, source_target_pairs={{0,16},{2,18},{4,20},{6,22},{8,24},{10,26},{12,28},{14,30},{16,0},... | collective-permute-start | bytes 884744 | tf_op jit(solution)/shard_map/ppermute | solution.py:602
  116.1 9.0 %collective-permute-start.28 = (bf16[160,768]{1,0:T(8,128)(2,1)S(1)}, bf16[160,768]{1,0:T(8,128)(2,1)S(1)}, u32[]{:S(2)}, u32[]{:S(2)}) collective-permute-start(bf16[160,768]{1,0:T(8,128)(2,1)S(1)} %pad_maximum_fusion.2), channel_id=1, source_target_pairs={{0,1},{1,0},{2,3},{3,2},{4,5},{5,4},{6,7},{7,6},{8,9},{9,8},{10,11... | collective-permute-start | bytes 737288 | tf_op jit(solution)/shard_map/ppermute | solution.py:558
  117.3 7.7 %collective-permute-start.29 = (bf16[160,768]{1,0:T(8,128)(2,1)S(1)}, bf16[160,768]{1,0:T(8,128)(2,1)S(1)}, u32[]{:S(2)}, u32[]{:S(2)}) collective-permute-start(bf16[160,768]{1,0:T(8,128)(2,1)S(1)} %pad_maximum_fusion.2), channel_id=1, source_target_pairs={{0,2},{1,3},{2,0},{3,1},{4,6},{5,7},{6,4},{7,5},{8,10},{9,11},{10,... | collective-permute-start | bytes 737288 | tf_op jit(solution)/shard_map/ppermute | solution.py:558
  117.3 9.4 %collective-permute-start.30 = (bf16[160,768]{1,0:T(8,128)(2,1)S(1)}, bf16[160,768]{1,0:T(8,128)(2,1)S(1)}, u32[]{:S(2)}, u32[]{:S(2)}) collective-permute-start(bf16[160,768]{1,0:T(8,128)(2,1)S(1)} %pad_maximum_fusion.2), channel_id=1, source_target_pairs={{0,3},{1,2},{2,1},{3,0},{4,7},{5,6},{6,5},{7,4},{8,11},{9,10},{10,... | collective-permute-start | bytes 737288 | tf_op jit(solution)/shard_map/ppermute | solution.py:558
  131.1 16.3 %collective-permute-start.31 = (bf16[4,192,768]{2,1,0:T(8,128)(2,1)S(1)}, bf16[4,192,768]{2,1,0:T(8,128)(2,1)S(1)}, u32[]{:S(2)}, u32[]{:S(2)}) collective-permute-start(bf16[4,192,768]{2,1,0:T(8,128)(2,1)S(1)} %constant_dynamic-update-slice_fusion), channel_id=1, source_target_pairs={{0,4},{2,10},{4,0},{6,14},{8,12},{10,2},{12,8},{14,6},{16,20},{18,... | collective-permute-start | bytes 3538952 | tf_op jit(solution)/shard_map/ppermute | solution.py:602
  132.1 10.0 %collective-permute-start.32 = (bf16[2,96,768]{2,1,0:T(8,128)(2,1)S(1)}, bf16[2,96,768]{2,1,0:T(8,128)(2,1)S(1)}, u32[]{:S(2)}, u32[]{:S(2)}) collective-permute-start(bf16[2,96,768]{2,1,0:T(8,128)(2,1)S(1)} %add_convert_fusion.7), channel_id=1, source_target_pairs={{0,8},{2,6},{4,12},{6,2},{8,0},{10,14},{12,4},{14,10},{16,24},{18,... | collective-permute-start | bytes 884744 | tf_op jit(solution)/shard_map/ppermute | solution.py:602
  147.7 9.9 %collective-permute-start.34 = (bf16[4,96,768]{2,1,0:T(8,128)(2,1)S(1)}, bf16[4,96,768]{2,1,0:T(8,128)(2,1)S(1)}, u32[]{:S(2)}, u32[]{:S(2)}) collective-permute-start(bf16[4,96,768]{2,1,0:T(8,128)(2,1)S(1)} %constant_dynamic-update-slice_fusion.4), channel_id=1, source_target_pairs={{0,4},{2,10},{4,0},{6,14},{8,12},{10,2},{12,8},{14,6},{16,20},{18,... | collective-permute-start | bytes 1769480 | tf_op jit(solution)/shard_map/ppermute | solution.py:602
  (25 other events, 138.6 us)
